TPU v7x, 32 devices: a whole 2x2x4 slice. The times are simulated.
32 devices in a mesh: groups: 2 (over x), cols: 8 (over z, y), comp: 2 (over core).
Axes of the slice: x: 2, y: 2, z: 4, core: 2. Of those that a mesh axis runs over, the one named last changes fastest.
Arguments:
- zonal_current: float32 [64, 256, 128], P(None, ('groups', 'cols', 'comp')), parts along dimension 1, may hold values from -3 to 3
- meridional_current: float32 [64, 256, 128], P(None, ('groups', 'cols', 'comp')), parts along dimension 1, may hold values from -3 to 3
- thermal_anomaly: float32 [64, 256, 128], P(None, ('groups', 'cols', 'comp')), parts along dimension 1, may hold values from -5 to 5
- saltiness_anomaly: float32 [64, 256, 128], P(None, ('groups', 'cols', 'comp')), parts along dimension 1, may hold values from -5 to 5
- species_amounts: float32 [16, 64, 32768], P(None, None, ('groups', 'cols', 'comp')), parts along dimension 2, may hold values from -5 to 5
- wet_layer_number: int32 [256, 128], P(('groups', 'cols', 'comp')), parts along dimension 0, may hold values from 0 to 64
- profile_block_order: int32 [256, 128], P(('groups', 'cols', 'comp')), parts along dimension 0, may hold values from 0 to 16383, as said below
- species_coupling: float32 [16, 16], replicated, may hold values from -1.5 to 1.5
- settling_fraction: float32 [16], replicated, may hold values from 0.05 to 0.5
Outputs:
- out_u: float32 [64, 256, 128], P(None, ('groups', 'cols', 'comp')), parts along dimension 1
- out_v: float32 [64, 256, 128], P(None, ('groups', 'cols', 'comp')), parts along dimension 1
- out_temperature: float32 [64, 256, 128], P(None, ('groups', 'cols', 'comp')), parts along dimension 1
- out_salinity: float32 [64, 256, 128], P(None, ('groups', 'cols', 'comp')), parts along dimension 1
- out_tracers: float32 [16, 64, 32768], P(None, None, ('groups', 'cols', 'comp')), parts along dimension 2
There are 2 independent parts, one for each index of `groups`. A program takes and returns all parts, laid end to end along the dimension named above; an argument that names none is the same for every part. Nothing has to cross between parts.
Inputs may be any that keep to these rules, and one draw needn't show every extreme that they name: profile_block_order holds each of 0 to 16383 once; the 1024 columns of tile t (longitudes t * 8 on) give exactly 64 columns to each patch d (positions d * 1024 to (d + 1) * 1024 - 1), placed at d * 1024 + t * 64 + r for r below 64.
All inputs are finite; a program needn't handle non-finite values.
Results may differ from a plain program's by a relative error of at most 0.0001.
Values sent between devices are 32-bit elements; how exact they have to be, the bound alone decides.
No kernel may reach another device: no remote copies, remote signals or barrier semaphores. Data moves between devices by JAX's collectives and lax.ppermute only.
A program may use at most 64 MiB of HBM per device.

v0:
```python
import jax
import jax.numpy as jnp
from jax import lax
from jax.experimental import pallas as pl
from jax.experimental.pallas import tpu as pltpu
from jax.sharding import PartitionSpec as P

SUBS = 2
AXES = ("cols", "comp")
F32 = jnp.float32
BF16 = jnp.bfloat16
MIB = 1024 * 1024
BLOCK = 256


def split(x):
    hi = x.astype(BF16)
    return hi, (x - hi.astype(F32)).astype(BF16)


def split3(x):
    hi = x.astype(BF16)
    rest = x - hi.astype(F32)
    mid = rest.astype(BF16)
    return hi, mid, (rest - mid.astype(F32)).astype(BF16)


def mxu(a, b):
    return jnp.dot(a, b, preferred_element_type=F32)


def iota(shape, dim):
    return lax.broadcasted_iota(jnp.int32, shape, dim)


def pack(out_ref, row, x, cpair):
    groups = 128 // cpair
    rows = x.shape[0] // groups
    lane_group = iota((rows, 128), 1) // cpair
    for e in range(x.shape[1] // 128):
        part = x[:, e * 128 : (e + 1) * 128]
        for o in range(groups):
            out = None
            for g in range(groups):
                piece = part[g * rows : (g + 1) * rows]
                shift = (g - o) * cpair % 128
                if shift:
                    piece = pltpu.roll(piece, shift, 1)
                out = piece if out is None else jnp.where(lane_group == g, piece, out)
            out_ref[e * groups + o, row : row + rows, :] = out


def unpack(in_ref, row, rows, cpair, first, blocks):
    groups = 128 // cpair
    lane_group = iota((rows, 128), 1) // cpair
    columns = []
    for e in range(blocks):
        levels = []
        for g in range(groups):
            out = None
            for o in range(groups):
                piece = in_ref[first + e * groups + o, row : row + rows, :]
                shift = (o - g) * cpair % 128
                if shift:
                    piece = pltpu.roll(piece, shift, 1)
                out = piece if out is None else jnp.where(lane_group == o, piece, out)
            levels.append(out)
        columns.append(jnp.concatenate(levels, axis=0))
    return jnp.concatenate(columns, axis=1)


def light(chloro):
    levels = chloro.shape[0]
    absorbed = (0.5 + 0.1 * chloro * chloro) * (1.0 / levels)
    lower = (iota((levels, levels), 1) <= iota((levels, levels), 0)).astype(F32).astype(BF16)
    total = mxu(jnp.concatenate([lower] * 3, axis=1), jnp.concatenate(split3(absorbed), axis=0))
    trans = jnp.exp(-total)
    above = jnp.where(iota(trans.shape, 0) == 0, 1.0, pltpu.roll(trans, 1, 0))
    return trans, levels * (above - trans)


def sink(amounts, fraction):
    for _ in range(SUBS):
        flux = fraction * amounts
        amounts = amounts - flux + pltpu.roll(flux, 1, 0)
    return amounts


def split_kron(coupling):
    return jnp.concatenate(split(coupling), axis=0)


def mix(kron2, kron_hi, tracers):
    rows = tracers.shape[0]
    hi, lo = split(tracers)
    both = mxu(kron2, hi)
    return both[:rows] + both[rows:] + mxu(kron_hi, lo)


def start_kernel(cpair, order_ref, depth_ref, temp_ref, species_ref, pay_ref, place_ref, heat_ref, trans_ref, lhs, temp, chloro, sems):
    levels, lons, lats = temp_ref.shape
    ctile = lons * lats
    copies = [
        pltpu.make_async_copy(species_ref.at[0], chloro, sems.at[0]),
        pltpu.make_async_copy(temp_ref, temp, sems.at[1]),
    ]
    for copy in copies:
        copy.start()
    order = order_ref[...]
    bucket = (order >> (ctile.bit_length() - 1)) * cpair + (order & (cpair - 1))
    across = bucket.astype(F32).T.astype(jnp.int32)
    target = iota((lats, ctile), 1)
    for r in range(lons):
        place_ref[r * lats : (r + 1) * lats, :] = jnp.where(target == across[:, r : r + 1], 1.0, 0.0).astype(BF16)
    depth = depth_ref[...].astype(F32)
    copies[0].wait()
    trans, heat = light(chloro[...])
    heat_ref[...] = heat
    trans_ref[...] = trans
    rows = levels * cpair // 128
    pack(pay_ref, rows, heat, cpair)
    copies[1].wait()
    for r in range(lons):
        hi, lo = split(temp[:, r, :])
        at = slice(r * lats, (r + 1) * lats)
        lhs[0:levels, at] = hi
        lhs[levels : 2 * levels, at] = lo
        lhs[2 * levels : 2 * levels + 16, at] = jnp.broadcast_to(depth[r : r + 1], (16, lats)).astype(BF16)
    sent = mxu(lhs[...], place_ref[...])
    pack(pay_ref, 0, sent[0:levels] + sent[levels : 2 * levels], cpair)
    deep = sent[2 * levels : 2 * levels + 8]
    for d in range(pay_ref.shape[0]):
        e, o = divmod(d * cpair, 128)
        part = deep[:, e * 128 : (e + 1) * 128]
        pay_ref[d, 2 * rows : 2 * rows + 8, :] = pltpu.roll(part, 128 - o, 1) if o else part


def react_kernel(species_ref, trans_ref, kron_ref, out_ref):
    tracers, levels, columns = species_ref.shape
    span = kron_ref.shape[0] // tracers
    kron2 = split_kron(kron_ref[...])
    for k in range(0, levels, span):
        mixed = mix(kron2, kron2[: span * tracers], species_ref[:, k : k + span, :].reshape(span * tracers, columns))
        out_ref[:, k : k + span, :] = mixed.reshape(tracers, span, columns) * (0.2 * trans_ref[k : k + span, :])[None]


def tile_levels(fields, left_ref, right_ref, depth_ref, fcor_ref, outs):
    levels, lons, lats = fields[0].shape
    shape = (lons, lats)
    lon, lat = iota(shape, 0), iota(shape, 1)
    first_lon, last_lon, first_lat, last_lat = lon == 0, lon == lons - 1, lat == 0, lat == lats - 1
    depth = depth_ref[...]
    turn = jnp.broadcast_to(0.2 * fcor_ref[...], shape)

    def neighbours(f, lower, upper):
        return (
            jnp.where(first_lon, lower, pltpu.roll(f, 1, 0)),
            jnp.where(last_lon, upper, pltpu.roll(f, lons - 1, 0)),
            jnp.where(first_lat, 0.0, pltpu.roll(f, 1, 1)),
            jnp.where(last_lat, 0.0, pltpu.roll(f, lats - 1, 1)),
        )

    def eight(i, carry):
        at = pl.ds(pl.multiple_of(i * 8, 8), 8)
        lefts = [left_ref[n, at, :] for n in range(4)]
        rights = [right_ref[n, at, :] for n in range(4)]
        for j in range(8):
            k = i * 8 + j
            u, v, t, s = (f[k] for f in fields)
            lu, lv, lt, ls = (jnp.broadcast_to(x[j : j + 1], shape) for x in lefts)
            ru, rv, rt, rs = (jnp.broadcast_to(x[j : j + 1], shape) for x in rights)
            load, load_left, load_right = carry
            load = load + (0.8 * s - 0.2 * t)
            load_left = load_left + (0.8 * ls - 0.2 * lt)
            load_right = load_right + (0.8 * rs - 0.2 * rt)
            carry = (load, load_left, load_right)
            wet = k < depth
            p0, p1, p2, p3 = neighbours(load, load_left, load_right)
            u0, u1, u2, u3 = neighbours(u, lu, ru)
            v0, v1, v2, v3 = neighbours(v, lv, rv)
            t0, t1, t2, t3 = neighbours(t, lt, rt)
            s0, s1, s2, s3 = neighbours(s, ls, rs)
            half_u, half_v = 0.1 * u, 0.1 * v
            new_u = 0.92 * u + turn * v - 0.01 * (p1 - p0) + 0.02 * ((u0 + u1) + (u2 + u3))
            new_v = 0.92 * v - turn * u - 0.01 * (p3 - p2) + 0.02 * ((v0 + v1) + (v2 + v3))
            new_t = 0.92 * t - half_u * (t1 - t0) - half_v * (t3 - t2) + 0.02 * ((t0 + t1) + (t2 + t3))
            new_s = 0.92 * s - half_u * (s1 - s0) - half_v * (s3 - s2) + 0.02 * ((s0 + s1) + (s2 + s3))
            for out, new in zip(outs, (new_u, new_v, new_t, new_s)):
                out[k] = jnp.where(wet, new, 0.0)
        return carry

    zero = jnp.zeros(shape, F32)
    lax.fori_loop(0, levels // 8, eight, (zero, zero, zero))


def first_tile_kernel(cpair, u_ref, v_ref, t_ref, s_ref, left_ref, right_ref, depth_ref, fcor_ref, order_ref, place_ref,
                      out_u, out_v, out_t, out_s, pay_ref, back_ref, lhs):
    levels, lons, lats = t_ref.shape
    ctile = lons * lats
    tile_levels((u_ref, v_ref, t_ref, s_ref), left_ref, right_ref, depth_ref, fcor_ref, (out_u, out_v, out_t, out_s))
    for r in range(lons):
        at = slice(r * lats, (r + 1) * lats)
        lhs[0:levels, at], lhs[levels : 2 * levels, at] = split(out_t[:, r, :])
    sent = mxu(lhs[...], place_ref[...])
    pack(pay_ref, 0, sent[0:levels] + sent[levels : 2 * levels], cpair)
    order = order_ref[...]
    bucket = (order >> (ctile.bit_length() - 1)) * cpair + (order & (cpair - 1))
    source = iota((ctile, lats), 0)
    for r in range(lons):
        back_ref[:, r * lats : (r + 1) * lats] = jnp.where(source == bucket[r : r + 1], 1.0, 0.0).astype(BF16)


def chloro_kernel(cpair, recv_ref, react_ref, species_ref, settling_ref, xpay_ref, pay_ref, warm_ref, depth_ref, trans_ref, react, chloro, sems):
    levels, columns = warm_ref.shape
    rows = levels * cpair // 128
    copies = [
        pltpu.make_async_copy(species_ref.at[0], chloro, sems.at[0]),
        pltpu.make_async_copy(react_ref.at[0], react, sems.at[1]),
    ]
    for copy in copies:
        copy.start()
    groups = 128 // cpair
    lane_group = iota((8, 128), 1) // cpair
    for e in range(columns // 128):
        out = None
        for o in range(groups):
            piece = recv_ref[e * groups + o, 2 * rows : 2 * rows + 8, :]
            if o:
                piece = pltpu.roll(piece, o * cpair, 1)
            out = piece if out is None else jnp.where(lane_group == o, piece, out)
        depth_ref[:, e * 128 : (e + 1) * 128] = out
    pay_ref[:, 0:rows, :] = xpay_ref[...]
    warm = jnp.exp(0.15 * unpack(recv_ref, 0, rows, cpair, 0, columns // 128))
    warm_ref[...] = warm
    level = iota((levels, columns), 0).astype(F32)
    depth = depth_ref[0:1, :]
    for copy in copies:
        copy.wait()
    amounts = chloro[...] + warm * react[...]
    amounts = sink(amounts, jnp.where(level + 1.0 < depth, settling_ref[0], 0.0))
    trans, heat = light(jnp.where(level < depth, amounts, 0.0))
    trans_ref[...] = trans
    pack(pay_ref, rows, heat, cpair)


def tracer_kernel(species_ref, react_ref, warm_ref, trans_ref, heat_ref, depth_ref, kron_ref, settling_ref, out_ref, next_ref):
    tracers, levels, columns = species_ref.shape
    level = iota((levels, columns), 0).astype(F32)
    depth = depth_ref[0:1, :]
    wet, below = level < depth, level + 1.0 < depth
    warm = warm_ref[...]
    for n in range(tracers):
        amounts = sink(species_ref[n] + warm * react_ref[n], jnp.where(below, settling_ref[n], 0.0))
        out_ref[n] = jnp.where(wet, amounts, 0.0)
    growth = 0.2 * trans_ref[...] * jnp.exp(0.03 * jnp.where(wet, heat_ref[...], 0.0))
    span = kron_ref.shape[0] // tracers
    kron2 = split_kron(kron_ref[...])
    for k in range(0, levels, span):
        mixed = mix(kron2, kron2[: span * tracers], out_ref[:, k : k + span, :].reshape(span * tracers, columns))
        next_ref[:, k : k + span, :] = mixed.reshape(tracers, span, columns) * growth[k : k + span][None]


def heat_kernel(cpair, recv_ref, back_ref, x_ref, depth_ref, u_ref, v_ref, s_ref, out_t, left_ref, right_ref):
    levels, lons, lats = x_ref.shape
    rows = levels * cpair // 128
    ctile = lons * lats
    heat = unpack(recv_ref, rows, rows, cpair, 0, ctile // 128)
    placed = mxu(jnp.concatenate(split(heat), axis=0), back_ref[...])
    placed = 0.2 * (placed[:levels] + placed[levels:])
    level = iota((levels, lats), 0)
    for r in range(lons):
        part = placed[:, r * lats : (r + 1) * lats]
        out_t[:, r, :] = x_ref[:, r, :] + jnp.where(level < depth_ref[r : r + 1, :], part, 0.0)
    for n, field in enumerate((u_ref, v_ref, out_t, s_ref)):
        left_ref[n] = field[:, 0, :]
        right_ref[n] = field[:, lons - 1, :]


def second_tile_kernel(u_ref, v_ref, t_ref, s_ref, left_ref, right_ref, depth_ref, fcor_ref, out_u, out_v, out_t, out_s):
    tile_levels((u_ref, v_ref, t_ref, s_ref), left_ref, right_ref, depth_ref, fcor_ref, (out_u, out_v, out_t, out_s))


def final_kernel(cpair, species_ref, react_ref, depth_ref, settling_ref, xrecv_ref, recv_ref, back_ref, wet_ref, part_ref, out_ref, out_t, heat):
    step = pl.program_id(0)
    tracers, levels, columns = species_ref.shape
    _, lons, lats = part_ref.shape
    rows = levels * cpair // 128

    @pl.when(step == 0)
    def _():
        heat[0:levels, :], heat[levels : 2 * levels, :] = split(unpack(recv_ref, rows, rows, cpair, 0, lons * lats // 128))
        out_t[...] = part_ref[...]

    warm = jnp.exp(0.15 * unpack(xrecv_ref, 0, rows, cpair, 0, columns // 128))
    level = iota((levels, columns), 0).astype(F32)
    depth = depth_ref[0:1, :]
    wet, below = level < depth, level + 1.0 < depth
    for n in range(tracers):
        amounts = sink(species_ref[n] + warm * react_ref[n], jnp.where(below, settling_ref[n], 0.0))
        out_ref[n] = jnp.where(wet, amounts, 0.0)
    placed = mxu(heat[...], back_ref[...])
    placed = 0.2 * (placed[:levels] + placed[levels:])
    tile_level = iota((levels, lats), 0)
    share = columns // lats
    for i in range(lons // share):

        @pl.when(step == i)
        def _():
            for r in range(share):
                lon = i * share + r
                part = placed[:, r * lats : (r + 1) * lats]
                out_t[:, lon, :] = part_ref[:, lon, :] + jnp.where(tile_level < wet_ref[lon : lon + 1, :], part, 0.0)


def whole(count):
    return [pl.BlockSpec(memory_space=pltpu.VMEM)] * count


ANY = pl.BlockSpec(memory_space=pl.ANY)
SMEM = pl.BlockSpec(memory_space=pltpu.SMEM)


def params(mib=48):
    return pltpu.CompilerParams(vmem_limit_bytes=mib * MIB)


def cost(flops, moved):
    return pl.CostEstimate(flops=flops, bytes_accessed=moved, transcendentals=0)


def shape(*dims, dtype=F32):
    return jax.ShapeDtypeStruct(dims, dtype)


def halo(left_edge, right_edge):
    count = lax.axis_size(AXES)
    ahead = [(i, (i + 1) % count) for i in range(count)]
    return lax.ppermute(right_edge, AXES, ahead), lax.ppermute(left_edge, AXES, [(b, a) for a, b in ahead])


def exchange(pay):
    return lax.all_to_all(pay, AXES, split_axis=0, concat_axis=0, tiled=True)


def body(u, v, temp, salt, species, wet_layers, order, coupling, settling):
    levels, lons, lats = temp.shape
    tracers, _, ctile = species.shape
    tiles = lax.axis_size(AXES)
    cpair = ctile // tiles
    rows = levels * cpair // 128
    field = shape(levels, lons, lats)
    column = shape(levels, ctile)
    edge = shape(4, levels, lats)
    onehot = shape(ctile, ctile, dtype=BF16)
    fcor = (0.8 * jnp.sin(jnp.pi * (jnp.arange(lats, dtype=F32) + 0.5) / lats - jnp.pi / 2))[None]
    kron = jnp.kron(coupling, jnp.eye(256 // tracers, dtype=F32))

    pay, place, heat1, trans1 = pl.pallas_call(
        lambda *refs: start_kernel(cpair, *refs),
        out_shape=[shape(tiles, 2 * rows + 8, 128), onehot, column, column],
        in_specs=whole(2) + [ANY, ANY],
        out_specs=whole(4),
        scratch_shapes=[
            pltpu.VMEM((2 * levels + 16, ctile), BF16),
            pltpu.VMEM((levels, lons, lats), F32),
            pltpu.VMEM((levels, ctile), F32),
            pltpu.SemaphoreType.DMA((2,)),
        ],
        compiler_params=params(),
        name="start",
    )(order, wet_layers, temp, species)
    recv_a = exchange(pay)

    stacked = jnp.stack([u, v, temp, salt])
    left, right = halo(stacked[:, :, 0], stacked[:, :, lons - 1])
    grid = (ctile // BLOCK,)
    tracer_block = pl.BlockSpec((tracers, levels, BLOCK), lambda i: (0, 0, i))
    column_block = pl.BlockSpec((levels, BLOCK), lambda i: (0, i))
    kron_block = pl.BlockSpec((256, 256), lambda i: (0, 0))
    mix_flops = 6 * 256 * levels * tracers * ctile
    react1 = pl.pallas_call(
        react_kernel,
        grid=grid,
        out_shape=shape(tracers, levels, ctile),
        in_specs=[tracer_block, column_block, kron_block],
        out_specs=tracer_block,
        compiler_params=params(),
        cost_estimate=cost(mix_flops, 8 * MIB),
        name="react",
    )(species, trans1, kron)
    u1, v1, x0, s1, xpay, back = pl.pallas_call(
        lambda *refs: first_tile_kernel(cpair, *refs),
        out_shape=[field] * 4 + [shape(tiles, rows, 128), onehot],
        in_specs=whole(10),
        out_specs=whole(6),
        scratch_shapes=[pltpu.VMEM((2 * levels, ctile), BF16)],
        compiler_params=params(),
        cost_estimate=cost(4 * levels * ctile * ctile, 8 * MIB),
        name="tile_one",
    )(u, v, temp, salt, left, right, wet_layers, fcor, order, place)

    pay, warm, depth, trans2 = pl.pallas_call(
        lambda *refs: chloro_kernel(cpair, *refs),
        out_shape=[shape(tiles, 2 * rows, 128), column, shape(8, ctile), column],
        in_specs=whole(1) + [ANY, ANY, SMEM] + whole(1),
        out_specs=whole(4),
        scratch_shapes=[
            pltpu.VMEM((levels, ctile), F32),
            pltpu.VMEM((levels, ctile), F32),
            pltpu.SemaphoreType.DMA((2,)),
        ],
        compiler_params=params(),
        name="chloro",
    )(recv_a, react1, species, settling, xpay)
    recv_b = exchange(pay)

    recv_a, _ = lax.optimization_barrier((recv_a, pay))
    t1, left_edge, right_edge = pl.pallas_call(
        lambda *refs: heat_kernel(cpair, *refs),
        out_shape=[field, edge, edge],
        in_specs=whole(7),
        out_specs=whole(3),
        compiler_params=params(),
        cost_estimate=cost(4 * levels * ctile * ctile, 4 * MIB),
        name="heat",
    )(recv_a, back, x0, wet_layers, u1, v1, s1)
    left, right = halo(left_edge, right_edge)
    species1, react2 = pl.pallas_call(
        tracer_kernel,
        grid=grid,
        out_shape=[shape(tracers, levels, ctile)] * 2,
        in_specs=[tracer_block, tracer_block] + [column_block] * 3 + [pl.BlockSpec((8, BLOCK), lambda i: (0, i)), kron_block, SMEM],
        out_specs=[tracer_block] * 2,
        compiler_params=params(),
        cost_estimate=cost(mix_flops, 16 * MIB),
        name="tracer",
    )(species, react1, warm, trans2, heat1, depth, kron, settling)
    u2, v2, t2, s2 = pl.pallas_call(
        second_tile_kernel,
        out_shape=[field] * 4,
        in_specs=whole(8),
        out_specs=whole(4),
        compiler_params=params(),
        cost_estimate=cost(60 * levels * ctile, 2 * MIB),
        name="tile_two",
    )(u1, v1, t1, s1, left, right, wet_layers, fcor)

    field_block = pl.BlockSpec((levels, lons, lats), lambda i: (0, 0, 0))
    species2, t2 = pl.pallas_call(
        lambda *refs: final_kernel(cpair, *refs),
        grid=grid,
        out_shape=[shape(tracers, levels, ctile), field],
        in_specs=[
            tracer_block,
            tracer_block,
            pl.BlockSpec((8, BLOCK), lambda i: (0, i)),
            SMEM,
            pl.BlockSpec((BLOCK // cpair, 2 * rows, 128), lambda i: (i, 0, 0)),
            pl.BlockSpec((tiles, 2 * rows, 128), lambda i: (0, 0, 0)),
            pl.BlockSpec((ctile, BLOCK), lambda i: (0, i)),
            pl.BlockSpec((lons, lats), lambda i: (0, 0)),
            field_block,
        ],
        out_specs=[tracer_block, field_block],
        scratch_shapes=[pltpu.VMEM((2 * levels, ctile), BF16)],
        compiler_params=params(),
        name="final",
    )(species1, react2, depth, settling, recv_b, recv_b, back, wet_layers, t2)
    return u2, v2, t2, s2, species2


def solution(mesh):
    tile = P(None, ("groups", "cols", "comp"), None)
    patch = P(None, None, ("groups", "cols", "comp"))
    index = P(("groups", "cols", "comp"), None)
    return jax.shard_map(
        body,
        mesh=mesh,
        in_specs=(tile, tile, tile, tile, patch, index, index, P(), P()),
        out_specs=(tile, tile, tile, tile, patch),
        check_vma=False,
    )
```

profile of v0, /device:TPU:0, one launch (start us, length us, event | category | flops | bytes accessed | tf_op | source)
XLA Modules:
  0.0 85.0 jit_solution(15847516087267378715)
XLA Ops:
  0.6 0.9 %copy-done.3 = f32[64,8,128]{2,1,0:T(8,128)S(1)} copy-done((f32[64,8,128]{2,1,0:T(8,128)S(1)}, f32[64,8,128]{2,1,0:T(8,128)}, u32[]{:S(2)}) %copy-start.3) | copy-done | bytes 262168
  1.6 0.7 copy-done.36
  2.3 0.7 copy-done.38
  3.0 3.4 %start.1 = (f32[16,72,128]{2,1,0:T(8,128)}, bf16[1024,1024]{1,0:T(8,128)(2,1)S(1)}, f32[64,1024]{1,0:T(8,128)S(1)}, f32[64,1024]{1,0:T(8,128)S(1)}) custom-call(s32[8,128]{1,0:T(8,128)S(1)} %copy-done.38, s32[8,128]{1,0:T(8,128)S(1)} %copy-done.36, f32[64,8,128]{2,1,0:T(8,128)S(1)} %copy-done.3, f32[16,64,1024]{2,1,0:T(8,128)} %species_ref.3), custom_call_target="tpu_custom_call" | custom-call | tf_op jit(solution)/shard_map/start/pallas_call | solution.py:358
  6.4 0.0 copy-start.5
  6.4 1.3 %copy-done.5 = bf16[1024,1024]{1,0:T(8,128)(2,1)} copy-done((bf16[1024,1024]{1,0:T(8,128)(2,1)}, bf16[1024,1024]{1,0:T(8,128)(2,1)S(1)}, u32[]{:S(2)}) %copy-start.5) | copy-done | bytes 2097176
  7.7 0.7 copy-done.22
  8.4 7.5 %all-to-all-start = ((f32[16,72,128]{2,1,0:T(8,128)}), f32[16,72,128]{2,1,0:T(8,128)S(1)}, u32[]{:S(2)}, u32[]{:S(2)}) async-start(f32[16,72,128]{2,1,0:T(8,128)} %get-tuple-element.34), calls=%async_computation | async-start | bytes 1179648 | tf_op jit(solution)/shard_map/all_to_all | solution.py:342
  16.0 0.1 copy.22
  16.0 0.1 copy.23
  16.1 0.1 copy_bitcast_fusion
  16.3 4.4 %collective-permute-start.1 = (f32[4,64,128]{2,1,0:T(8,128)S(1)}, f32[4,64,128]{2,1,0:T(8,128)S(1)}, u32[]{:S(2)}, u32[]{:S(2)}) collective-permute-start(f32[4,64,128]{2,1,0:T(8,128)S(1)} %get-tuple-element.57), channel_id=1, source_target_pairs={{1,0},{2,1},{3,2},{4,3},{5,4},{6,5},{7,6},{8,7},{9,8},{10,9},{11,1... | collective-permute-start | bytes 393224 | tf_op jit(solution)/shard_map/ppermute | solution.py:338
  20.7 0.0 collective-permute-start
  20.7 1.5 %broadcast_multiply_fusion = f32[16,16,16,16]{3,2,1,0:T(8,128)} fusion(f32[16,16]{1,0:T(8,128)S(1)} %fusion.1, f32[16,16]{1,0:T(8,128)S(1)} %copy-done.41), kind=kLoop, calls=%fused_computation | loop fusion | flops 65536 | bytes 264192 | tf_op jit(solution)/shard_map/jit(kron)/mul | solution.py:356
  22.2 2.4 %mul.47.kron_ref = f32[256,256]{1,0:T(8,128)S(1)} reshape(f32[16,16,16,16]{3,2,1,0:T(8,128)} %broadcast_multiply_fusion) | data formatting | bytes 524288 | tf_op jit(solution)/shard_map/jit(kron)/mul | solution.py:356
  24.7 0.0 copy-start.16
  24.7 0.0 copy-start.18
  24.7 0.0 copy-start.20
  24.7 0.0 copy-start.37
  24.7 0.0 copy-start.39
  24.7 4.7 %react.1.refs_1_.react_ref = f32[16,64,1024]{2,1,0:T(8,128)S(1)} custom-call(f32[16,64,1024]{2,1,0:T(8,128)} %species_ref.3, f32[64,1024]{1,0:T(8,128)S(1)} %get-tuple-element.35.trans_ref, f32[256,256]{1,0:T(8,128)S(1)} %mul.47.kron_ref), custom_call_target="tpu_custom_call" | custom-call | flops 1610612736 | bytes 8388608 | tf_op jit(solution)/shard_map/react/pallas_call | solution.py:381
  29.4 0.0 copy-start
  29.4 2.0 %copy-done = f32[16,64,1024]{2,1,0:T(8,128)} copy-done((f32[16,64,1024]{2,1,0:T(8,128)}, f32[16,64,1024]{2,1,0:T(8,128)S(1)}, u32[]{:S(2)}) %copy-start) | copy-done | bytes 4194328
  31.5 0.0 collective-permute-done.1.refs_5_
  31.5 0.0 copy-start.32
  31.5 0.6 copy-done.32
  32.1 0.8 collective-permute-done.refs_4_
  32.9 0.7 copy-done.34
  33.6 0.0 copy-done.37
  33.6 0.0 copy-done.39
  33.6 0.0 copy-start.33
  33.6 0.9 %copy-done.33 = f32[4,64,128]{2,1,0:T(8,128)S(1)} copy-done((f32[4,64,128]{2,1,0:T(8,128)S(1)}, f32[4,64,128]{2,1,0:T(8,128)}, u32[]{:S(2)}) %copy-start.33) | copy-done | bytes 131096
  34.5 0.9 %copy-done.35 = f32[4,64,128]{2,1,0:T(8,128)S(1)} copy-done((f32[4,64,128]{2,1,0:T(8,128)S(1)}, f32[4,64,128]{2,1,0:T(8,128)}, u32[]{:S(2)}) %copy-start.35) | copy-done | bytes 131096
  35.4 5.2 %tile_one.1 = (f32[64,8,128]{2,1,0:T(8,128)S(1)}, f32[64,8,128]{2,1,0:T(8,128)S(1)}, f32[64,8,128]{2,1,0:T(8,128)S(1)}, f32[64,8,128]{2,1,0:T(8,128)S(1)}, f32[1...) custom-call(f32[64,8,128]{2,1,0:T(8,128)S(1)} %copy-done.16, f32[64,8,128]{2,1,0:T(8,128)S(1)} %copy-done.18, ...), custom_call_target="tpu_custom_call" | custom-call | flops 268435456 | bytes 8388608 | tf_op jit(solution)/shard_map/tile_one/pallas_call | solution.py:391
  40.6 0.0 copy-start.6
  40.6 0.7 copy-done.6
  41.3 0.7 copy-done.12
  42.0 0.7 copy-done.28
  42.7 0.7 copy-done.30
  43.4 0.0 all-to-all-done.refs_0_
  43.4 2.3 %copy-done.1 = f32[16,64,1024]{2,1,0:T(8,128)S(1)} copy-done((f32[16,64,1024]{2,1,0:T(8,128)S(1)}, f32[16,64,1024]{2,1,0:T(8,128)}, u32[]{:S(2)}) %copy-start.1) | copy-done | bytes 4194328
  45.7 0.9 %copy-done.31 = f32[16,32,128]{2,1,0:T(8,128)S(1)} copy-done((f32[16,32,128]{2,1,0:T(8,128)S(1)}, f32[16,32,128]{2,1,0:T(8,128)}, u32[]{:S(2)}) %copy-start.31) | copy-done | bytes 262168
  46.7 2.0 %chloro.1 = (f32[16,64,128]{2,1,0:T(8,128)S(1)}, f32[64,1024]{1,0:T(8,128)S(1)}, f32[8,1024]{1,0:T(8,128)S(1)}, f32[64,1024]{1,0:T(8,128)S(1)}) custom-call(f32[16,72,128]{2,1,0:T(8,128)S(1)} %all-to-all-done.refs_0_, f32[16,64,1024]{2,1,0:T(8,128)S(1)} %copy-done.1, f32[16,64,1024]{2,1,0:T(8,128)} %species_ref.3, f32[16]{0:T(128)S(1)} %copy-done.40, ...), custom_call_target="tpu_custom_call" | custom-call | tf_op jit(solution)/shard_map/chloro/pallas_call | solution.py:402
  48.7 0.8 copy-done.21
  49.5 0.7 copy-done.24
  50.2 0.7 copy-done.26
  50.9 5.1 %all-to-all-start.1 = ((f32[16,64,128]{2,1,0:T(8,128)}), f32[16,64,128]{2,1,0:T(8,128)S(1)}, u32[]{:S(2)}, u32[]{:S(2)}) async-start(f32[16,64,128]{2,1,0:T(8,128)} %copy-done.21), calls=%async_computation.1 | async-start | bytes 1048576 | tf_op jit(solution)/shard_map/all_to_all | solution.py:342
  55.9 0.0 copy-start.7
  56.0 0.9 %copy-done.7 = f32[64,8,128]{2,1,0:T(8,128)S(1)} copy-done((f32[64,8,128]{2,1,0:T(8,128)S(1)}, f32[64,8,128]{2,1,0:T(8,128)}, u32[]{:S(2)}) %copy-start.7) | copy-done | bytes 262168
  56.9 0.9 %copy-done.10 = f32[64,8,128]{2,1,0:T(8,128)S(1)} copy-done((f32[64,8,128]{2,1,0:T(8,128)S(1)}, f32[64,8,128]{2,1,0:T(8,128)}, u32[]{:S(2)}) %copy-start.10) | copy-done | bytes 262168
  57.8 0.9 %copy-done.13 = f32[64,8,128]{2,1,0:T(8,128)S(1)} copy-done((f32[64,8,128]{2,1,0:T(8,128)S(1)}, f32[64,8,128]{2,1,0:T(8,128)}, u32[]{:S(2)}) %copy-start.13) | copy-done | bytes 262168
  58.8 0.9 %copy-done.29 = f32[64,8,128]{2,1,0:T(8,128)S(1)} copy-done((f32[64,8,128]{2,1,0:T(8,128)S(1)}, f32[64,8,128]{2,1,0:T(8,128)}, u32[]{:S(2)}) %copy-start.29) | copy-done | bytes 262168
  59.8 0.8 heat.1
  60.6 0.5 collective-permute-start.2
  61.0 4.0 %collective-permute-start.3 = (f32[4,64,128]{2,1,0:T(8,128)S(1)}, f32[4,64,128]{2,1,0:T(8,128)S(1)}, u32[]{:S(2)}, u32[]{:S(2)}) collective-permute-start(f32[4,64,128]{2,1,0:T(8,128)S(1)} %get-tuple-element.44), channel_id=1, source_target_pairs={{1,0},{2,1},{3,2},{4,3},{5,4},{6,5},{7,6},{8,7},{9,8},{10,9},{11,1... | collective-permute-start | bytes 393224 | tf_op jit(solution)/shard_map/ppermute | solution.py:338
  65.1 0.0 copy-start.11
  65.1 0.0 copy-start.14
  65.1 8.2 %tracer.1 = (f32[16,64,1024]{2,1,0:T(8,128)S(1)}, f32[16,64,1024]{2,1,0:T(8,128)}) custom-call(f32[16,64,1024]{2,1,0:T(8,128)} %species_ref.3, f32[16,64,1024]{2,1,0:T(8,128)} %copy-done, f32[64,1024]{1,0:T(8,128)S(1)} %copy-done.25, f32[64,1024]{1,0:T(8,128)S(1)} %copy-done.27, f32[64,1024]{1,0:T(8,128)S(1)} %copy-done.23, ...), custom_call_target="tpu_custom_call" | custom-call | flops 1610612736 | bytes 16777216 | tf_op jit(solution)/shard_map/tracer/pallas_call | solution.py:428
  73.3 2.0 %copy-done.2 = f32[16,64,1024]{2,1,0:T(8,128)} copy-done((f32[16,64,1024]{2,1,0:T(8,128)}, f32[16,64,1024]{2,1,0:T(8,128)S(1)}, u32[]{:S(2)}) %copy-start.2) | copy-done | bytes 4194328
  75.3 0.0 collective-permute-done.2.left_ref
  75.3 0.0 collective-permute-done.3.right_ref
  75.4 2.2 %tile_two.1 = (f32[64,8,128]{2,1,0:T(8,128)}, f32[64,8,128]{2,1,0:T(8,128)}, f32[64,8,128]{2,1,0:T(8,128)S(1)}, f32[64,8,128]{2,1,0:T(8,128)}) custom-call(f32[64,8,128]{2,1,0:T(8,128)S(1)} %copy-done.8, f32[64,8,128]{2,1,0:T(8,128)S(1)} %copy-done.11, f32[64,8,128]{2,1,0:T(8,128)S(1)} %get-tuple-element.42.t_ref, f32[64,8,128]{2,1,0:T(8,128)S(1)} %copy-done.14, ...), custom_call_target="tpu_custom_call" | custom-call | flops 3932160 | bytes 2097152 | tf_op jit(solution)/shard_map/tile_two/pallas_call | solution.py:438
  77.5 0.0 all-to-all-done.1.refs_4_.refs_5_
  77.5 7.4 %final.1 = (f32[16,64,1024]{2,1,0:T(8,128)}, f32[64,8,128]{2,1,0:T(8,128)}) custom-call(f32[16,64,1024]{2,1,0:T(8,128)} %copy-done.2, f32[16,64,1024]{2,1,0:T(8,128)} %get-tuple-element.52.refs_1_, f32[8,1024]{1,0:T(8,128)S(1)} %get-tuple-element.50.depth_ref.refs_2_, f32[16]{0:T(128)S(1)} %copy-done.40, f32[16,64,128]{2,1,0:T(8,128)S(1)} %all-to-all-done.1.refs_4_.refs_5_, ...), custom_call_target="tpu_custom_call" | custom-call | tf_op jit(solution)/shard_map/final/pallas_call | solution.py:449
  (48 shorter events, 0.2 us)
Async XLA Ops:
  0.6 1.0 %copy-start.3 = (f32[64,8,128]{2,1,0:T(8,128)S(1)}, f32[64,8,128]{2,1,0:T(8,128)}, u32[]{:S(2)}) copy-start(f32[64,8,128]{2,1,0:T(8,128)} %refs_2_.4) | copy-start | bytes 786436
  1.6 0.7 copy-start.36
  2.3 0.7 copy-start.38
  3.0 13.0 %copy-start.4 = (f32[64,8,128]{2,1,0:T(8,128)S(1)}, f32[64,8,128]{2,1,0:T(8,128)}, u32[]{:S(2)}) copy-start(f32[64,8,128]{2,1,0:T(8,128)} %refs_2_.4) | copy-start | bytes 786436
  3.0 13.1 %copy-start.15 = (f32[64,8,128]{2,1,0:T(8,128)S(1)}, f32[64,8,128]{2,1,0:T(8,128)}, u32[]{:S(2)}) copy-start(f32[64,8,128]{2,1,0:T(8,128)} %refs_0_.3) | copy-start | bytes 786436
  6.4 1.3 %copy-start.5 = (bf16[1024,1024]{1,0:T(8,128)(2,1)}, bf16[1024,1024]{1,0:T(8,128)(2,1)S(1)}, u32[]{:S(2)}) copy-start(bf16[1024,1024]{1,0:T(8,128)(2,1)S(1)} %get-tuple-element.31.refs_9_) | copy-start | bytes 6291460
  7.7 0.7 copy-start.22
  8.4 7.7 %copy-start.17 = (f32[64,8,128]{2,1,0:T(8,128)S(1)}, f32[64,8,128]{2,1,0:T(8,128)}, u32[]{:S(2)}) copy-start(f32[64,8,128]{2,1,0:T(8,128)} %refs_1_.3) | copy-start | bytes 786436
  8.4 7.7 %copy-start.19 = (f32[64,8,128]{2,1,0:T(8,128)S(1)}, f32[64,8,128]{2,1,0:T(8,128)}, u32[]{:S(2)}) copy-start(f32[64,8,128]{2,1,0:T(8,128)} %refs_3_.6) | copy-start | bytes 786436
  8.4 12.3 %copy-start.41 = (f32[16,16]{1,0:T(8,128)S(1)}, f32[16,16]{1,0:T(8,128)}, u32[]{:S(2)}) copy-start(f32[16,16]{1,0:T(8,128)} %param.16) | copy-start | bytes 3076
  8.4 35.0 %all-to-all-start = ((f32[16,72,128]{2,1,0:T(8,128)}), f32[16,72,128]{2,1,0:T(8,128)S(1)}, u32[]{:S(2)}, u32[]{:S(2)}) async-start(f32[16,72,128]{2,1,0:T(8,128)} %get-tuple-element.34), calls=%async_computation | async-start | bytes 1179648 | tf_op jit(solution)/shard_map/all_to_all | solution.py:342
  16.3 15.2 %collective-permute-start.1 = (f32[4,64,128]{2,1,0:T(8,128)S(1)}, f32[4,64,128]{2,1,0:T(8,128)S(1)}, u32[]{:S(2)}, u32[]{:S(2)}) collective-permute-start(f32[4,64,128]{2,1,0:T(8,128)S(1)} %get-tuple-element.57), channel_id=1, source_target_pairs={{1,0},{2,1},{3,2},{4,3},{5,4},{6,5},{7,6},{8,7},{9,8},{10,9},{11,1... | collective-permute-start | bytes 393224 | tf_op jit(solution)/shard_map/ppermute | solution.py:338
  20.7 12.2 %collective-permute-start = (f32[4,64,128]{2,1,0:T(8,128)S(1)}, f32[4,64,128]{2,1,0:T(8,128)S(1)}, u32[]{:S(2)}, u32[]{:S(2)}) collective-permute-start(f32[4,64,128]{2,1,0:T(8,128)S(1)} %get-tuple-element.58), channel_id=1, source_target_pairs={{0,1},{1,2},{2,3},{3,4},{4,5},{5,6},{6,7},{7,8},{8,9},{9,10},{10,1... | collective-permute-start | bytes 393224 | tf_op jit(solution)/shard_map/ppermute | solution.py:338
  24.7 8.9 %copy-start.16 = (f32[64,8,128]{2,1,0:T(8,128)S(1)}, f32[64,8,128]{2,1,0:T(8,128)}, u32[]{:S(2)}) copy-start(f32[64,8,128]{2,1,0:T(8,128)} %refs_0_.3) | copy-start | bytes 786436
  24.7 8.9 %copy-start.18 = (f32[64,8,128]{2,1,0:T(8,128)S(1)}, f32[64,8,128]{2,1,0:T(8,128)}, u32[]{:S(2)}) copy-start(f32[64,8,128]{2,1,0:T(8,128)} %refs_1_.3) | copy-start | bytes 786436
  24.7 8.9 %copy-start.20 = (f32[64,8,128]{2,1,0:T(8,128)S(1)}, f32[64,8,128]{2,1,0:T(8,128)}, u32[]{:S(2)}) copy-start(f32[64,8,128]{2,1,0:T(8,128)} %refs_3_.6) | copy-start | bytes 786436
  24.7 8.9 %copy-start.37 = (s32[8,128]{1,0:T(8,128)S(1)}, s32[8,128]{1,0:T(8,128)}, u32[]{:S(2)}) copy-start(s32[8,128]{1,0:T(8,128)} %refs_7_.1) | copy-start | bytes 12292
  24.7 8.9 %copy-start.39 = (s32[8,128]{1,0:T(8,128)S(1)}, s32[8,128]{1,0:T(8,128)}, u32[]{:S(2)}) copy-start(s32[8,128]{1,0:T(8,128)} %refs_8_.1) | copy-start | bytes 12292
  29.4 2.0 %copy-start = (f32[16,64,1024]{2,1,0:T(8,128)}, f32[16,64,1024]{2,1,0:T(8,128)S(1)}, u32[]{:S(2)}) copy-start(f32[16,64,1024]{2,1,0:T(8,128)S(1)} %react.1.refs_1_.react_ref) | copy-start | bytes 12582916
  31.4 12.0 %copy-start.40 = (f32[16]{0:T(128)S(1)}, f32[16]{0:T(128)}, u32[]{:S(2)}) copy-start(f32[16]{0:T(128)} %refs_3_.9) | copy-start | bytes 196
  31.5 0.7 copy-start.32
  32.9 0.7 copy-start.34
  33.6 0.9 %copy-start.33 = (f32[4,64,128]{2,1,0:T(8,128)S(1)}, f32[4,64,128]{2,1,0:T(8,128)}, u32[]{:S(2)}) copy-start(f32[4,64,128]{2,1,0:T(8,128)} %copy-done.32) | copy-start | bytes 393220
  34.5 0.9 %copy-start.35 = (f32[4,64,128]{2,1,0:T(8,128)S(1)}, f32[4,64,128]{2,1,0:T(8,128)}, u32[]{:S(2)}) copy-start(f32[4,64,128]{2,1,0:T(8,128)} %copy-done.34) | copy-start | bytes 393220
  40.6 0.7 copy-start.6
  41.3 0.7 copy-start.12
  42.0 0.7 copy-start.28
  42.7 0.7 copy-start.30
  43.4 5.2 %copy-start.9 = (f32[64,8,128]{2,1,0:T(8,128)}, f32[64,8,128]{2,1,0:T(8,128)S(1)}, u32[]{:S(2)}) copy-start(f32[64,8,128]{2,1,0:T(8,128)S(1)} %get-tuple-element.33.refs_5_.v_ref) | copy-start | bytes 786436
  43.4 2.3 %copy-start.1 = (f32[16,64,1024]{2,1,0:T(8,128)S(1)}, f32[16,64,1024]{2,1,0:T(8,128)}, u32[]{:S(2)}) copy-start(f32[16,64,1024]{2,1,0:T(8,128)} %copy-done) | copy-start | bytes 12582916
  45.7 0.9 %copy-start.31 = (f32[16,32,128]{2,1,0:T(8,128)S(1)}, f32[16,32,128]{2,1,0:T(8,128)}, u32[]{:S(2)}) copy-start(f32[16,32,128]{2,1,0:T(8,128)} %copy-done.30) | copy-start | bytes 786436
  48.7 0.8 copy-start.21
  49.5 0.7 copy-start.24
  50.2 0.7 copy-start.26
  50.9 26.6 %all-to-all-start.1 = ((f32[16,64,128]{2,1,0:T(8,128)}), f32[16,64,128]{2,1,0:T(8,128)S(1)}, u32[]{:S(2)}, u32[]{:S(2)}) async-start(f32[16,64,128]{2,1,0:T(8,128)} %copy-done.21), calls=%async_computation.1 | async-start | bytes 1048576 | tf_op jit(solution)/shard_map/all_to_all | solution.py:342
  55.9 1.0 %copy-start.7 = (f32[64,8,128]{2,1,0:T(8,128)S(1)}, f32[64,8,128]{2,1,0:T(8,128)}, u32[]{:S(2)}) copy-start(f32[64,8,128]{2,1,0:T(8,128)} %copy-done.6) | copy-start | bytes 786436
  56.9 0.9 %copy-start.10 = (f32[64,8,128]{2,1,0:T(8,128)S(1)}, f32[64,8,128]{2,1,0:T(8,128)}, u32[]{:S(2)}) copy-start(f32[64,8,128]{2,1,0:T(8,128)} %copy-done.9) | copy-start | bytes 786436
  57.8 0.9 %copy-start.13 = (f32[64,8,128]{2,1,0:T(8,128)S(1)}, f32[64,8,128]{2,1,0:T(8,128)}, u32[]{:S(2)}) copy-start(f32[64,8,128]{2,1,0:T(8,128)} %copy-done.12) | copy-start | bytes 786436
  58.8 0.9 %copy-start.29 = (f32[64,8,128]{2,1,0:T(8,128)S(1)}, f32[64,8,128]{2,1,0:T(8,128)}, u32[]{:S(2)}) copy-start(f32[64,8,128]{2,1,0:T(8,128)} %copy-done.28) | copy-start | bytes 786436
  59.7 5.3 %copy-start.23 = (f32[64,1024]{1,0:T(8,128)S(1)}, f32[64,1024]{1,0:T(8,128)}, u32[]{:S(2)}) copy-start(f32[64,1024]{1,0:T(8,128)} %copy-done.22) | copy-start | bytes 786436
  59.7 5.3 %copy-start.25 = (f32[64,1024]{1,0:T(8,128)S(1)}, f32[64,1024]{1,0:T(8,128)}, u32[]{:S(2)}) copy-start(f32[64,1024]{1,0:T(8,128)} %copy-done.24) | copy-start | bytes 786436
  59.7 5.3 %copy-start.27 = (f32[64,1024]{1,0:T(8,128)S(1)}, f32[64,1024]{1,0:T(8,128)}, u32[]{:S(2)}) copy-start(f32[64,1024]{1,0:T(8,128)} %copy-done.26) | copy-start | bytes 786436
  60.6 14.8 %collective-permute-start.2 = (f32[4,64,128]{2,1,0:T(8,128)S(1)}, f32[4,64,128]{2,1,0:T(8,128)S(1)}, u32[]{:S(2)}, u32[]{:S(2)}) collective-permute-start(f32[4,64,128]{2,1,0:T(8,128)S(1)} %get-tuple-element.43), channel_id=1, source_target_pairs={{0,1},{1,2},{2,3},{3,4},{4,5},{5,6},{6,7},{7,8},{8,9},{9,10},{10,1... | collective-permute-start | bytes 393224 | tf_op jit(solution)/shard_map/ppermute | solution.py:338
  61.0 14.3 %collective-permute-start.3 = (f32[4,64,128]{2,1,0:T(8,128)S(1)}, f32[4,64,128]{2,1,0:T(8,128)S(1)}, u32[]{:S(2)}, u32[]{:S(2)}) collective-permute-start(f32[4,64,128]{2,1,0:T(8,128)S(1)} %get-tuple-element.44), channel_id=1, source_target_pairs={{1,0},{2,1},{3,2},{4,3},{5,4},{6,5},{7,6},{8,7},{9,8},{10,9},{11,1... | collective-permute-start | bytes 393224 | tf_op jit(solution)/shard_map/ppermute | solution.py:338
  65.1 10.3 %copy-start.8 = (f32[64,8,128]{2,1,0:T(8,128)S(1)}, f32[64,8,128]{2,1,0:T(8,128)}, u32[]{:S(2)}) copy-start(f32[64,8,128]{2,1,0:T(8,128)} %copy-done.6) | copy-start | bytes 786436
  65.1 10.3 %copy-start.11 = (f32[64,8,128]{2,1,0:T(8,128)S(1)}, f32[64,8,128]{2,1,0:T(8,128)}, u32[]{:S(2)}) copy-start(f32[64,8,128]{2,1,0:T(8,128)} %copy-done.9) | copy-start | bytes 786436
  65.1 10.3 %copy-start.14 = (f32[64,8,128]{2,1,0:T(8,128)S(1)}, f32[64,8,128]{2,1,0:T(8,128)}, u32[]{:S(2)}) copy-start(f32[64,8,128]{2,1,0:T(8,128)} %copy-done.12) | copy-start | bytes 786436
  73.3 2.0 %copy-start.2 = (f32[16,64,1024]{2,1,0:T(8,128)}, f32[16,64,1024]{2,1,0:T(8,128)S(1)}, u32[]{:S(2)}) copy-start(f32[16,64,1024]{2,1,0:T(8,128)S(1)} %get-tuple-element.51.refs_0_) | copy-start | bytes 12582916
where the time goes:
time: 85.9 us; the launch traced here: 85 us
  Pallas kernels  33.9 us (39%)
  local copies, waits for them, and re-layouts  26.2 us (31%)
  starting transfers between devices  21.5 us (25%)
  other arithmetic  1.6 us (2%)
  between operations  0.97 us (1%)
    unnamed x86, local copies, waits for them, and re-layouts  23.7 us
    all_to_all x2, starting transfers between devices, exchange(): return lax.all_to_all(pay, AXES, split_axis=0, concat_axis=0, tiled=True)  12.6 us
    ppermute x2, starting transfers between devices, halo(): lax.ppermute(left_edge, AXES, [(b, a) for a, b in ahead])  8.47 us
    pallas_call x1, Pallas kernels, body(): pl.pallas_call(tracer_kernel, grid=grid, out_shape=[shape(tracers, levels...  8.23 us
    pallas_call x1, Pallas kernels, body(): pl.pallas_call(lambda *refs: final_kernel(cpair, *refs), grid=grid, out_s...  7.45 us
    pallas_call x1, Pallas kernels, body(): pl.pallas_call(lambda *refs: first_tile_kernel(cpair, *refs), out_shape=[...  5.21 us
    pallas_call x1, Pallas kernels, body(): pl.pallas_call(react_kernel, grid=grid, out_shape=shape(tracers, levels,...  4.66 us
    pallas_call x1, Pallas kernels, body(): pl.pallas_call(lambda *refs: start_kernel(cpair, *refs), out_shape=[shape...  3.42 us
  transfers between devices with their start and end apart: 6, of which 1 were waited for; matrix products, arithmetic and copies ran while one was open for 5% of the time, Pallas kernels for 25%

commit v1 on v0

v1 whole, which is shorter than its diff:
```python
import jax
import jax.numpy as jnp
from jax import lax
from jax.experimental import pallas as pl
from jax.experimental.pallas import tpu as pltpu
from jax.sharding import PartitionSpec as P

SUBS = 2
AXES = ("cols", "comp")
F32 = jnp.float32
BF16 = jnp.bfloat16
MIB = 1024 * 1024
BLOCK = 256


def split(x):
    hi = x.astype(BF16)
    return hi, (x - hi.astype(F32)).astype(BF16)


def split3(x):
    hi = x.astype(BF16)
    rest = x - hi.astype(F32)
    mid = rest.astype(BF16)
    return hi, mid, (rest - mid.astype(F32)).astype(BF16)


def mxu(a, b):
    return jnp.dot(a, b, preferred_element_type=F32)


def iota(shape, dim):
    return lax.broadcasted_iota(jnp.int32, shape, dim)


def pack(out_ref, row, x, cpair):
    groups = 128 // cpair
    rows = x.shape[0] // groups
    lane_group = iota((rows, 128), 1) // cpair
    for e in range(x.shape[1] // 128):
        part = x[:, e * 128 : (e + 1) * 128]
        for o in range(groups):
            out = None
            for g in range(groups):
                piece = part[g * rows : (g + 1) * rows]
                shift = (g - o) * cpair % 128
                if shift:
                    piece = pltpu.roll(piece, shift, 1)
                out = piece if out is None else jnp.where(lane_group == g, piece, out)
            out_ref[e * groups + o, row : row + rows, :] = out


def unpack(in_ref, row, rows, cpair, first, blocks):
    groups = 128 // cpair
    lane_group = iota((rows, 128), 1) // cpair
    columns = []
    for e in range(blocks):
        levels = []
        for g in range(groups):
            out = None
            for o in range(groups):
                piece = in_ref[first + e * groups + o, row : row + rows, :]
                shift = (o - g) * cpair % 128
                if shift:
                    piece = pltpu.roll(piece, shift, 1)
                out = piece if out is None else jnp.where(lane_group == o, piece, out)
            levels.append(out)
        columns.append(jnp.concatenate(levels, axis=0))
    return jnp.concatenate(columns, axis=1)


def light(chloro):
    levels = chloro.shape[0]
    absorbed = (0.5 + 0.1 * chloro * chloro) * (1.0 / levels)
    lower = (iota((levels, levels), 1) <= iota((levels, levels), 0)).astype(F32).astype(BF16)
    total = mxu(jnp.concatenate([lower] * 3, axis=1), jnp.concatenate(split3(absorbed), axis=0))
    trans = jnp.exp(-total)
    above = jnp.where(iota(trans.shape, 0) == 0, 1.0, pltpu.roll(trans, 1, 0))
    return trans, levels * (above - trans)


def sink(amounts, fraction):
    for _ in range(SUBS):
        flux = fraction * amounts
        amounts = amounts - flux + pltpu.roll(flux, 1, 0)
    return amounts


def split_kron(coupling, span):
    tracers = coupling.shape[0]
    size = tracers * span
    tall = (iota((size, tracers), 0) // span == iota((size, tracers), 1)).astype(F32).astype(BF16)
    wide = (iota((tracers, size), 1) // span == iota((tracers, size), 0)).astype(F32).astype(BF16)
    same = iota((size, size), 0) % span == iota((size, size), 1) % span
    terms = [jnp.where(same, mxu(mxu(tall, term).astype(BF16), wide), 0.0).astype(BF16) for term in split(coupling)]
    return jnp.concatenate(terms, axis=0)


def mix(kron_ref, tracers):
    rows = tracers.shape[0]
    hi, lo = split(tracers)
    both = mxu(kron_ref[...], hi)
    return both[:rows] + both[rows:] + mxu(kron_ref[:rows, :], lo)


def mix_levels(kron_ref, tracers_ref, scale_ref, out_ref, k):
    tracers, _, columns = tracers_ref.shape
    size = kron_ref.shape[1]
    span = size // tracers

    def block(i, _):
        at = pl.ds(pl.multiple_of(i * BLOCK, BLOCK), BLOCK)
        mixed = mix(kron_ref, tracers_ref[:, k : k + span, at].reshape(size, BLOCK))
        out_ref[:, k : k + span, at] = mixed.reshape(tracers, span, BLOCK) * scale_ref[k : k + span, at][None]
        return 0

    lax.fori_loop(0, columns // BLOCK, block, 0)


def sink_all(species_ref, warm_ref, react_ref, depth_ref, settling_ref, wet, below, out_ref, before, after):
    tracers, levels, columns = species_ref.shape
    level = iota((levels, columns), 0).astype(F32)
    depth = depth_ref[0:1, :]
    wet[...] = jnp.where(level < depth, 1.0, 0.0)
    below[...] = jnp.where(level + 1.0 < depth, 1.0, 0.0)

    def one(n, _):
        before(n)
        fraction = settling_ref[n]
        for c in range(0, columns, 128):
            at = slice(c, c + 128)
            amounts = species_ref[n, :, at] + warm_ref[:, at] * react_ref[n, :, at]
            out_ref[n, :, at] = sink(amounts, fraction * below[:, at]) * wet[:, at]
        after(n)
        return 0

    lax.fori_loop(0, tracers, one, 0)


def place_columns(order, onehot, cpair):
    lons, lats = order.shape
    target = iota((lats, lons * lats), 1)
    across = buckets(order, cpair).astype(F32).T.astype(jnp.int32)
    for r in range(lons):
        onehot[r * lats : (r + 1) * lats, :] = jnp.where(target == across[:, r : r + 1], 1.0, 0.0).astype(BF16)


def buckets(order, cpair):
    ctile = order.shape[0] * order.shape[1]
    return (order >> (ctile.bit_length() - 1)) * cpair + (order & (cpair - 1))


def start_kernel(cpair, order_hbm, depth_hbm, temp_hbm, species_hbm, pay_hbm, scale_ref, heat_ref, order, depths, temp, chloro, pay, place, lhs, sems):
    levels, lons, lats = temp.shape
    copies = [
        pltpu.make_async_copy(src, dst, sems.at[i])
        for i, (src, dst) in enumerate(((order_hbm, order), (depth_hbm, depths), (species_hbm.at[0], chloro), (temp_hbm, temp)))
    ]
    for copy in copies:
        copy.start()
    rows = levels * cpair // 128
    copies[0].wait()
    place_columns(order[...], place, cpair)
    copies[1].wait()
    depth = depths[...].astype(F32)
    copies[2].wait()
    trans, heat = light(chloro[...])
    heat_ref[...] = heat
    scale_ref[...] = 0.2 * trans
    pack(pay, 0, heat, cpair)
    send_heat = pltpu.make_async_copy(pay.at[:, 0:rows], pay_hbm.at[:, 0:rows], sems.at[4])
    send_heat.start()
    copies[3].wait()
    for r in range(lons):
        hi, lo = split(temp[:, r, :])
        at = slice(r * lats, (r + 1) * lats)
        lhs[0:levels, at] = hi
        lhs[levels : 2 * levels, at] = lo
        lhs[2 * levels : 2 * levels + 16, at] = jnp.broadcast_to(depth[r : r + 1], (16, lats)).astype(BF16)
    sent = mxu(lhs[...], place[...])
    pack(pay, rows, sent[0:levels] + sent[levels : 2 * levels], cpair)
    deep = sent[2 * levels : 2 * levels + 8]
    for d in range(pay.shape[0]):
        e, o = divmod(d * cpair, 128)
        part = deep[:, e * 128 : (e + 1) * 128]
        pay[d, 2 * rows : 2 * rows + 8, :] = pltpu.roll(part, 128 - o, 1) if o else part
    send_temp = pltpu.make_async_copy(pay.at[:, rows : 2 * rows + 8], pay_hbm.at[:, rows : 2 * rows + 8], sems.at[5])
    send_temp.start()
    send_heat.wait()
    send_temp.wait()


def react_kernel(species_hbm, scale_ref, coupling_ref, react_hbm, first_ref, kron_ref, species, react, sems, out_sems):
    tracers, levels, columns = species.shape
    span = 256 // tracers
    parts = [slice(k, k + span) for k in range(0, levels, span)]
    copies = [pltpu.make_async_copy(species_hbm.at[:, at], species.at[:, at], sems.at[i]) for i, at in enumerate(parts)]
    sends = [pltpu.make_async_copy(react.at[:, at], react_hbm.at[:, at], out_sems.at[i]) for i, at in enumerate(parts)]
    for copy in copies:
        copy.start()
    kron_ref[...] = split_kron(coupling_ref[...], span)
    for copy, send, at in zip(copies, sends, parts):
        copy.wait()
        mix_levels(kron_ref, species, scale_ref, react, at.start)
        send.start()
    first_ref[0] = species[0]
    first_ref[1] = react[0]
    for send in sends:
        send.wait()


def tile_levels(fields, left_ref, right_ref, depth_ref, fcor_ref, outs):
    levels, lons, lats = fields[0].shape
    shape = (lons, lats)
    lon, lat = iota(shape, 0), iota(shape, 1)
    first_lon, last_lon, first_lat, last_lat = lon == 0, lon == lons - 1, lat == 0, lat == lats - 1
    depth = depth_ref[...]
    turn = jnp.broadcast_to(0.2 * fcor_ref[...], shape)

    def neighbours(f, lower, upper):
        return (
            jnp.where(first_lon, lower, pltpu.roll(f, 1, 0)),
            jnp.where(last_lon, upper, pltpu.roll(f, lons - 1, 0)),
            jnp.where(first_lat, 0.0, pltpu.roll(f, 1, 1)),
            jnp.where(last_lat, 0.0, pltpu.roll(f, lats - 1, 1)),
        )

    def eight(i, carry):
        at = pl.ds(pl.multiple_of(i * 8, 8), 8)
        lefts = [left_ref[n, at, :] for n in range(4)]
        rights = [right_ref[n, at, :] for n in range(4)]
        for j in range(8):
            k = i * 8 + j
            u, v, t, s = (f[k] for f in fields)
            lu, lv, lt, ls = (jnp.broadcast_to(x[j : j + 1], shape) for x in lefts)
            ru, rv, rt, rs = (jnp.broadcast_to(x[j : j + 1], shape) for x in rights)
            load, load_left, load_right = carry
            load = load + (0.8 * s - 0.2 * t)
            load_left = load_left + (0.8 * ls - 0.2 * lt)
            load_right = load_right + (0.8 * rs - 0.2 * rt)
            carry = (load, load_left, load_right)
            wet = k < depth
            p0, p1, p2, p3 = neighbours(load, load_left, load_right)
            u0, u1, u2, u3 = neighbours(u, lu, ru)
            v0, v1, v2, v3 = neighbours(v, lv, rv)
            t0, t1, t2, t3 = neighbours(t, lt, rt)
            s0, s1, s2, s3 = neighbours(s, ls, rs)
            half_u, half_v = 0.1 * u, 0.1 * v
            new_u = 0.92 * u + turn * v - 0.01 * (p1 - p0) + 0.02 * ((u0 + u1) + (u2 + u3))
            new_v = 0.92 * v - turn * u - 0.01 * (p3 - p2) + 0.02 * ((v0 + v1) + (v2 + v3))
            new_t = 0.92 * t - half_u * (t1 - t0) - half_v * (t3 - t2) + 0.02 * ((t0 + t1) + (t2 + t3))
            new_s = 0.92 * s - half_u * (s1 - s0) - half_v * (s3 - s2) + 0.02 * ((s0 + s1) + (s2 + s3))
            for out, new in zip(outs, (new_u, new_v, new_t, new_s)):
                out[k] = jnp.where(wet, new, 0.0)
        return carry

    zero = jnp.zeros(shape, F32)
    lax.fori_loop(0, levels // 8, eight, (zero, zero, zero))


def first_tile_kernel(cpair, u_ref, v_ref, t_ref, s_ref, left_ref, right_ref, depth_ref, fcor_ref, order_ref,
                      pay_hbm, out_u, out_v, out_t, out_s, pay, place, lhs, sem):
    levels, lons, lats = t_ref.shape
    rows = levels * cpair // 128
    tile_levels((u_ref, v_ref, t_ref, s_ref), left_ref, right_ref, depth_ref, fcor_ref, (out_u, out_v, out_t, out_s))
    place_columns(order_ref[...], place, cpair)
    for r in range(lons):
        at = slice(r * lats, (r + 1) * lats)
        lhs[0:levels, at], lhs[levels : 2 * levels, at] = split(out_t[:, r, :])
    sent = mxu(lhs[...], place[...])
    pack(pay, 0, sent[0:levels] + sent[levels : 2 * levels], cpair)
    send = pltpu.make_async_copy(pay, pay_hbm.at[:, 0:rows], sem.at[0])
    send.start()
    send.wait()


def chloro_kernel(cpair, recv_ref, settling_ref, first_ref, pay_in, pay_hbm, warm_ref, depth_ref, scale_ref, pay, sem):
    levels, columns = warm_ref.shape
    rows = levels * cpair // 128
    groups = 128 // cpair
    lane_group = iota((8, 128), 1) // cpair
    for e in range(columns // 128):
        out = None
        for o in range(groups):
            piece = recv_ref[e * groups + o, 2 * rows : 2 * rows + 8, :]
            if o:
                piece = pltpu.roll(piece, o * cpair, 1)
            out = piece if out is None else jnp.where(lane_group == o, piece, out)
        depth_ref[:, e * 128 : (e + 1) * 128] = out
    warm = jnp.exp(0.15 * unpack(recv_ref, rows, rows, cpair, 0, columns // 128))
    warm_ref[...] = warm
    level = iota((levels, columns), 0).astype(F32)
    depth = depth_ref[0:1, :]
    amounts = first_ref[0] + warm * first_ref[1]
    amounts = sink(amounts, jnp.where(level + 1.0 < depth, settling_ref[0], 0.0))
    trans, heat = light(jnp.where(level < depth, amounts, 0.0))
    scale_ref[...] = 0.2 * trans
    pack(pay, 0, heat, cpair)
    send = pltpu.make_async_copy(pay, pay_hbm.at[:, rows : 2 * rows], sem.at[0])
    send.start()
    send.wait()


def heat_kernel(cpair, recv_ref, order_ref, depth_ref, u_ref, v_ref, x_ref, s_ref, back_hbm, out_t, left_ref, right_ref, back, sem):
    levels, lons, lats = x_ref.shape
    rows = levels * cpair // 128
    ctile = lons * lats
    bucket = buckets(order_ref[...], cpair)
    source = iota((ctile, lats), 0)
    for r in range(lons):
        back[:, r * lats : (r + 1) * lats] = jnp.where(source == bucket[r : r + 1], 1.0, 0.0).astype(BF16)
    save = pltpu.make_async_copy(back, back_hbm, sem.at[0])
    save.start()
    heat = unpack(recv_ref, 0, rows, cpair, 0, ctile // 128)
    placed = mxu(jnp.concatenate(split(heat), axis=0), back[...])
    placed = 0.2 * (placed[:levels] + placed[levels:])
    level = iota((levels, lats), 0)
    for r in range(lons):
        part = placed[:, r * lats : (r + 1) * lats]
        out_t[:, r, :] = x_ref[:, r, :] + jnp.where(level < depth_ref[r : r + 1, :], part, 0.0)
    for n, field in enumerate((u_ref, v_ref, out_t, s_ref)):
        left_ref[n] = field[:, 0, :]
        right_ref[n] = field[:, lons - 1, :]
    save.wait()


def tracer_kernel(species_hbm, react_hbm, warm_ref, scale_ref, heat_ref, depth_ref, kron_ref, settling_ref, out_hbm, next_hbm,
                  species, react, wet, below, in_sems, out_sems, next_sems):
    tracers, levels, columns = species.shape
    span = 256 // tracers

    def fetch(n):
        return (
            pltpu.make_async_copy(species_hbm.at[n], species.at[n], in_sems.at[2 * n]),
            pltpu.make_async_copy(react_hbm.at[n], react.at[n], in_sems.at[2 * n + 1]),
        )

    def save(n):
        return pltpu.make_async_copy(species.at[n], out_hbm.at[n], out_sems.at[n])

    for n in range(tracers):
        for copy in fetch(n):
            copy.start()

    def before(n):
        for copy in fetch(n):
            copy.wait()

    sink_all(species, warm_ref, react, depth_ref, settling_ref, wet, below, species, before, lambda n: save(n).start())
    below[...] = scale_ref[...] * jnp.exp(0.03 * (wet[...] * heat_ref[...]))
    parts = [slice(k, k + span) for k in range(0, levels, span)]
    sends = [pltpu.make_async_copy(react.at[:, at], next_hbm.at[:, at], next_sems.at[i]) for i, at in enumerate(parts)]
    for send, at in zip(sends, parts):
        mix_levels(kron_ref, species, below, react, at.start)
        send.start()
    for n in range(tracers):
        save(n).wait()
    for send in sends:
        send.wait()


def second_tile_kernel(u_ref, v_ref, t_ref, s_ref, left_ref, right_ref, depth_ref, fcor_ref, out_u, out_v, out_t, out_s):
    tile_levels((u_ref, v_ref, t_ref, s_ref), left_ref, right_ref, depth_ref, fcor_ref, (out_u, out_v, out_t, out_s))


def final_kernel(cpair, species_hbm, react_hbm, back_hbm, depth_ref, settling_ref, recv_ref, wet_ref, part_ref, out_hbm, t_hbm,
                 species, react, back, t, warm, wet, below, in_sems, out_sems, sems):
    tracers, levels, columns = species.shape
    _, lons, lats = part_ref.shape
    rows = levels * cpair // 128

    def fetch(n):
        return (
            pltpu.make_async_copy(species_hbm.at[n], species.at[n], in_sems.at[2 * n]),
            pltpu.make_async_copy(react_hbm.at[n], react.at[n], in_sems.at[2 * n + 1]),
        )

    def send(n):
        return pltpu.make_async_copy(species.at[n], out_hbm.at[n], out_sems.at[n])

    for copy in fetch(0):
        copy.start()
    fetch_back = pltpu.make_async_copy(back_hbm, back, sems.at[0])
    fetch_back.start()
    for n in range(1, tracers):
        for copy in fetch(n):
            copy.start()

    def before(n):
        for copy in fetch(n):
            copy.wait()

    warm[...] = jnp.exp(0.15 * unpack(recv_ref, 0, rows, cpair, 0, columns // 128))
    heat = jnp.concatenate(split(unpack(recv_ref, rows, rows, cpair, 0, columns // 128)), axis=0)
    fetch_back.wait()
    placed = mxu(heat, back[...])
    placed = 0.2 * (placed[:levels] + placed[levels:])
    level = iota((levels, lats), 0)
    for r in range(lons):
        part = placed[:, r * lats : (r + 1) * lats]
        t[:, r, :] = part_ref[:, r, :] + jnp.where(level < wet_ref[r : r + 1, :], part, 0.0)
    send_t = pltpu.make_async_copy(t, t_hbm, sems.at[1])
    send_t.start()
    sink_all(species, warm, react, depth_ref, settling_ref, wet, below, species, before, lambda n: send(n).start())
    for n in range(tracers):
        send(n).wait()
    send_t.wait()


def whole(count):
    return [pl.BlockSpec(memory_space=pltpu.VMEM)] * count


def in_hbm(x):
    return pltpu.with_memory_space_constraint(x, pltpu.HBM)


ANY = pl.BlockSpec(memory_space=pl.ANY)
SMEM = pl.BlockSpec(memory_space=pltpu.SMEM)


def params(mib):
    return pltpu.CompilerParams(vmem_limit_bytes=mib * MIB)


def cost(flops, moved):
    return pl.CostEstimate(flops=flops, bytes_accessed=moved, transcendentals=0)


def halo(left_edge, right_edge):
    count = lax.axis_size(AXES)
    ahead = [(i, (i + 1) % count) for i in range(count)]
    return lax.ppermute(right_edge, AXES, ahead), lax.ppermute(left_edge, AXES, [(b, a) for a, b in ahead])


def exchange(pay):
    return lax.all_to_all(pay, AXES, split_axis=0, concat_axis=0, tiled=True)


def body(u, v, temp, salt, species, wet_layers, order, coupling, settling):
    levels, lons, lats = temp.shape
    tracers, _, ctile = species.shape
    tiles = lax.axis_size(AXES)
    cpair = ctile // tiles
    rows = levels * cpair // 128
    field = jax.ShapeDtypeStruct((levels, lons, lats), F32)
    edge = jax.ShapeDtypeStruct((4, levels, lats), F32)
    column = jax.ShapeDtypeStruct((levels, ctile), F32)
    patch = pltpu.HBM((tracers, levels, ctile), F32)
    fcor = (0.8 * jnp.sin(jnp.pi * (jnp.arange(lats, dtype=F32) + 0.5) / lats - jnp.pi / 2))[None]
    sem = pltpu.SemaphoreType.DMA
    mix_flops = 6 * 256 * levels * tracers * ctile
    patch_scratch = pltpu.VMEM((tracers, levels, ctile), F32)
    column_scratch = pltpu.VMEM((levels, ctile), F32)
    onehot_scratch = pltpu.VMEM((ctile, ctile), BF16)

    pay, scale1, heat1 = pl.pallas_call(
        lambda *refs: start_kernel(cpair, *refs),
        out_shape=[pltpu.HBM((tiles, 2 * rows + 8, 128), F32), column, column],
        in_specs=[ANY] * 4,
        out_specs=[ANY] + whole(2),
        scratch_shapes=[
            pltpu.VMEM((lons, lats), jnp.int32),
            pltpu.VMEM((lons, lats), jnp.int32),
            pltpu.VMEM((levels, lons, lats), F32),
            column_scratch,
            pltpu.VMEM((tiles, 2 * rows + 8, 128), F32),
            onehot_scratch,
            pltpu.VMEM((2 * levels + 16, ctile), BF16),
            sem((6,)),
        ],
        compiler_params=params(12),
        name="start",
    )(in_hbm(order), in_hbm(wet_layers), in_hbm(temp), in_hbm(species))
    recv_a = exchange(pay)

    stacked = jnp.stack([u, v, temp, salt])
    left, right = halo(stacked[:, :, 0], stacked[:, :, lons - 1])
    groups = levels * tracers // 256
    react1, first, kron = pl.pallas_call(
        react_kernel,
        out_shape=[patch, jax.ShapeDtypeStruct((2, levels, ctile), F32), jax.ShapeDtypeStruct((512, 256), BF16)],
        in_specs=[ANY] + whole(2),
        out_specs=[ANY] + whole(2),
        scratch_shapes=[patch_scratch, patch_scratch, sem((groups,)), sem((groups,))],
        compiler_params=params(16),
        cost_estimate=cost(mix_flops, 8 * MIB),
        name="react",
    )(in_hbm(species), scale1, coupling)
    pay, u1, v1, x0, s1 = pl.pallas_call(
        lambda *refs: first_tile_kernel(cpair, *refs),
        out_shape=[pltpu.HBM((tiles, 2 * rows, 128), F32)] + [field] * 4,
        in_specs=whole(9),
        out_specs=[ANY] + whole(4),
        scratch_shapes=[pltpu.VMEM((tiles, rows, 128), F32), onehot_scratch, pltpu.VMEM((2 * levels, ctile), BF16), sem((1,))],
        compiler_params=params(12),
        cost_estimate=cost(4 * levels * ctile * ctile, 2 * MIB),
        name="tile_one",
    )(u, v, temp, salt, left, right, wet_layers, fcor, order)

    pay, warm, depth, scale2 = pl.pallas_call(
        lambda *refs: chloro_kernel(cpair, *refs),
        out_shape=[pltpu.HBM(pay.shape, F32), column, jax.ShapeDtypeStruct((8, ctile), F32), column],
        in_specs=[*whole(1), SMEM, *whole(1), ANY],
        out_specs=[ANY, *whole(3)],
        scratch_shapes=[pltpu.VMEM((tiles, rows, 128), F32), sem((1,))],
        input_output_aliases={3: 0},
        compiler_params=params(8),
        name="chloro",
    )(recv_a, settling, first, in_hbm(pay))
    recv_b = exchange(pay)

    recv_a, _ = lax.optimization_barrier((recv_a, pay))
    back, t1, *edges = pl.pallas_call(
        lambda *refs: heat_kernel(cpair, *refs),
        out_shape=[pltpu.HBM((ctile, ctile), BF16), field, edge, edge],
        in_specs=whole(7),
        out_specs=[ANY] + whole(3),
        scratch_shapes=[onehot_scratch, sem((1,))],
        compiler_params=params(12),
        cost_estimate=cost(4 * levels * ctile * ctile, 4 * MIB),
        name="heat",
    )(recv_a, order, wet_layers, u1, v1, x0, s1)
    left, right = halo(*edges)
    species1, react2 = pl.pallas_call(
        tracer_kernel,
        out_shape=[patch, patch],
        in_specs=[ANY] * 2 + whole(5) + [SMEM],
        out_specs=[ANY] * 2,
        scratch_shapes=[patch_scratch] * 2 + [column_scratch] * 2 + [sem((2 * tracers,)), sem((tracers,)), sem((groups,))],
        compiler_params=params(16),
        cost_estimate=cost(mix_flops, 16 * MIB),
        name="tracer",
    )(in_hbm(species), in_hbm(react1), warm, scale2, heat1, depth, kron, settling)
    u2, v2, t2, s2 = pl.pallas_call(
        second_tile_kernel,
        out_shape=[field] * 4,
        in_specs=whole(8),
        out_specs=whole(4),
        compiler_params=params(8),
        cost_estimate=cost(60 * levels * ctile, 2 * MIB),
        name="tile_two",
    )(u1, v1, t1, s1, left, right, wet_layers, fcor)

    species2, t2 = pl.pallas_call(
        lambda *refs: final_kernel(cpair, *refs),
        out_shape=[patch, pltpu.HBM(field.shape, F32)],
        in_specs=[ANY] * 3 + whole(1) + [SMEM] + whole(3),
        out_specs=[ANY] * 2,
        scratch_shapes=[
            patch_scratch,
            patch_scratch,
            onehot_scratch,
            pltpu.VMEM(field.shape, F32),
            column_scratch,
            column_scratch,
            column_scratch,
            sem((2 * tracers,)),
            sem((tracers,)),
            sem((2,)),
        ],
        compiler_params=params(20),
        name="final",
    )(in_hbm(species1), in_hbm(react2), in_hbm(back), depth, settling, recv_b, wet_layers, t2)
    return u2, v2, t2, s2, species2


def solution(mesh):
    tile = P(None, ("groups", "cols", "comp"), None)
    patch = P(None, None, ("groups", "cols", "comp"))
    index = P(("groups", "cols", "comp"), None)
    return jax.shard_map(
        body,
        mesh=mesh,
        in_specs=(tile, tile, tile, tile, patch, index, index, P(), P()),
        out_specs=(tile, tile, tile, tile, patch),
        check_vma=False,
    )
```

time: 85.9 us -> 67.6 us (0.79)
  local copies, waits for them, and re-layouts: 26.2 us -> 1.89 us
  Pallas kernels: 33.9 us -> 38.6 us
  waiting for transfers between devices: 0.78 us -> 5.45 us
  other arithmetic: 1.6 us -> 0.07 us
  starting transfers between devices: 21.5 us -> 20.4 us
    unnamed x86 -> x22, local copies, waits for them, and re-layouts: 23.7 us -> 1.79 us
    pallas_call x6, Pallas kernels: 26.6 us -> 33 us  [the longest x1 10.8 us: body(): pl.pallas_call(tracer_kernel, out_shape=[patch, patch], in_specs=[ANY] *...]
    ppermute x2, waiting for transfers between devices: 0.77 us -> 5.44 us  [halo(): lax.ppermute(right_edge, AXES, ahead)]
    mul x1 -> x0, local copies, waits for them, and re-layouts: 2.44 us -> none  [body(): kron = jnp.kron(coupling, jnp.eye(256 // tracers, dtype=F32))]
    pallas_call x1, Pallas kernels: 5.21 us -> 3.46 us  [body(): pl.pallas_call(lambda *refs: first_tile_kernel(cpair, *refs), out_shape=[...]
    mul x1 -> x0, other arithmetic: 1.52 us -> none  [body(): kron = jnp.kron(coupling, jnp.eye(256 // tracers, dtype=F32))]
    all_to_all x2, starting transfers between devices: 12.6 us -> 11.4 us  [exchange(): return lax.all_to_all(pay, AXES, split_axis=0, concat_axis=0, tiled=True)]
  transfers between devices with their start and end apart: 6 -> 6, of which waited for: 1 -> 1; matrix products, arithmetic and copies ran while one was open for 5% -> 0% of each run, Pallas kernels for 25% -> 38%
where the time goes in v1:
time: 67.6 us; the launch traced here: 67.2 us
  Pallas kernels  38.6 us (57%)
  starting transfers between devices  20.4 us (30%)
  waiting for transfers between devices  5.45 us (8%)
  local copies, waits for them, and re-layouts  1.89 us (3%)
  between operations  0.86 us (1%)
    all_to_all x2, starting transfers between devices, exchange(): return lax.all_to_all(pay, AXES, split_axis=0, concat_axis=0, tiled=True)  11.4 us
    pallas_call x1, Pallas kernels, body(): pl.pallas_call(tracer_kernel, out_shape=[patch, patch], in_specs=[ANY] *...  10.8 us
    ppermute x2, starting transfers between devices, halo(): lax.ppermute(left_edge, AXES, [(b, a) for a, b in ahead])  8.08 us
    pallas_call x1, Pallas kernels, body(): pl.pallas_call(lambda *refs: final_kernel(cpair, *refs), out_shape=[patch...  7.15 us
    pallas_call x1, Pallas kernels, body(): pl.pallas_call(react_kernel, out_shape=[patch, jax.ShapeDtypeStruct((2, l...  6.62 us
    ppermute x2, waiting for transfers between devices, halo(): lax.ppermute(right_edge, AXES, ahead)  5.44 us
    pallas_call x1, Pallas kernels, body(): pl.pallas_call(lambda *refs: start_kernel(cpair, *refs), out_shape=[pltpu...  3.89 us
    pallas_call x1, Pallas kernels, body(): pl.pallas_call(lambda *refs: first_tile_kernel(cpair, *refs), out_shape=[...  3.46 us
  transfers between devices with their start and end apart: 6, of which 1 were waited for; matrix products, arithmetic and copies ran while one was open for 0% of the time, Pallas kernels for 38%

profile of v1, /device:TPU:0, one launch (start us, length us, event | category | flops | bytes accessed | tf_op | source)
XLA Modules:
  0.0 67.2 jit_solution(5749255148637679693)
XLA Ops:
  0.6 0.0 copy-start
  0.6 0.0 copy-start.1
  0.7 0.0 copy-start.2
  0.7 0.0 copy-start.3
  0.7 0.0 copy-start.9
  0.7 3.9 %start.1 = (f32[16,72,128]{2,1,0:T(8,128)}, f32[64,1024]{1,0:T(8,128)S(1)}, f32[64,1024]{1,0:T(8,128)S(1)}) custom-call(s32[8,128]{1,0:T(8,128)} %refs_1_.7, s32[8,128]{1,0:T(8,128)} %refs_6_.3, f32[64,8,128]{2,1,0:T(8,128)} %refs_2_.4, f32[16,64,1024]{2,1,0:T(8,128)} %species_hbm.3), custom_call_target="tpu_custom_call" | custom-call | tf_op jit(solution)/shard_map/start/pallas_call | solution.py:457
  4.6 7.4 %all-to-all-start = ((f32[16,72,128]{2,1,0:T(8,128)}), f32[16,72,128]{2,1,0:T(8,128)S(1)}, u32[]{:S(2)}, u32[]{:S(2)}) async-start(f32[16,72,128]{2,1,0:T(8,128)} %get-tuple-element.35), calls=%async_computation | async-start | bytes 1179648 | tf_op jit(solution)/shard_map/all_to_all | solution.py:437
  12.0 0.0 copy-done
  12.0 0.1 copy.23
  12.1 0.0 copy-done.1
  12.1 0.1 copy.24
  12.1 0.0 copy-done.2
  12.1 0.0 copy-done.3
  12.1 0.0 copy-start.6
  12.2 0.0 copy-start.7
  12.2 0.1 copy_bitcast_fusion
  12.3 0.0 copy-start.8
  12.3 0.5 collective-permute-start
  12.8 4.0 %collective-permute-start.1 = (f32[4,64,128]{2,1,0:T(8,128)S(1)}, f32[4,64,128]{2,1,0:T(8,128)S(1)}, u32[]{:S(2)}, u32[]{:S(2)}) collective-permute-start(f32[4,64,128]{2,1,0:T(8,128)S(1)} %get-tuple-element.61), channel_id=1, source_target_pairs={{1,0},{2,1},{3,2},{4,3},{5,4},{6,5},{7,6},{8,7},{9,8},{10,9},{11,1... | collective-permute-start | bytes 393224 | tf_op jit(solution)/shard_map/ppermute | solution.py:433
  16.8 0.0 copy-done.9
  16.8 6.6 %react.1 = (f32[16,64,1024]{2,1,0:T(8,128)}, f32[2,64,1024]{2,1,0:T(8,128)S(1)}, bf16[512,256]{1,0:T(8,128)(2,1)S(1)}) custom-call(f32[16,64,1024]{2,1,0:T(8,128)} %species_hbm.3, f32[64,1024]{1,0:T(8,128)S(1)} %get-tuple-element.36.scale_ref, f32[16,16]{1,0:T(8,128)S(1)} %copy-done.9), custom_call_target="tpu_custom_call" | custom-call | flops 1610612736 | bytes 8388608 | tf_op jit(solution)/shard_map/react/pallas_call | solution.py:480
  23.4 0.1 sine_multiply_fusion.refs_7_.fcor_ref
  23.5 5.4 %collective-permute-done.refs_4_ = f32[4,64,128]{2,1,0:T(8,128)S(1)} collective-permute-done((f32[4,64,128]{2,1,0:T(8,128)S(1)}, f32[4,64,128]{2,1,0:T(8,128)S(1)}, u32[]{:S(2)}, u32[]{:S(2)}) %collective-permute-start) | collective-permute-done | bytes 131104 | tf_op jit(solution)/shard_map/ppermute | solution.py:433
  28.9 0.0 collective-permute-done.1.refs_5_
  28.9 0.0 copy-done.6
  28.9 0.0 copy-done.7
  28.9 3.5 %tile_one.1 = (f32[16,64,128]{2,1,0:T(8,128)}, f32[64,8,128]{2,1,0:T(8,128)S(1)}, f32[64,8,128]{2,1,0:T(8,128)S(1)}, f32[64,8,128]{2,1,0:T(8,128)S(1)}, f32[64,8,128]{2,1,0:T(8,128)S(1)}) custom-call(f32[64,8,128]{2,1,0:T(8,128)S(1)} %copy-done.1, f32[64,8,128]{2,1,0:T(8,128)S(1)} %copy-done.2, f32[64,8,128]{2,1,0:T(8,128)S(1)} %copy-done, ...), custom_call_target="tpu_custom_call" | custom-call | flops 268435456 | bytes 2097152 | tf_op jit(solution)/shard_map/tile_one/pallas_call | solution.py:490
  32.4 0.0 copy-start.4
  32.4 0.7 %copy-done.4 = f32[64,8,128]{2,1,0:T(8,128)} copy-done((f32[64,8,128]{2,1,0:T(8,128)}, f32[64,8,128]{2,1,0:T(8,128)S(1)}, u32[]{:S(2)}) %copy-start.4) | copy-done | bytes 262168
  33.1 0.0 all-to-all-done.refs_0_
  33.1 0.0 copy-done.8
  33.1 1.9 %chloro.1 = (f32[16,64,128]{2,1,0:T(8,128)}, f32[64,1024]{1,0:T(8,128)S(1)}, f32[8,1024]{1,0:T(8,128)S(1)}, f32[64,1024]{1,0:T(8,128)S(1)}) custom-call(f32[16,72,128]{2,1,0:T(8,128)S(1)} %all-to-all-done.refs_0_, f32[16]{0:T(128)S(1)} %copy-done.8, f32[2,64,1024]{2,1,0:T(8,128)S(1)} %get-tuple-element.37.refs_2_, ...), custom_call_target="tpu_custom_call", output_to_operand_aliasing={{0}: (3, {})} | custom-call | tf_op jit(solution)/shard_map/chloro/pallas_call | solution.py:501
  35.0 4.0 %all-to-all-start.1 = ((f32[16,64,128]{2,1,0:T(8,128)}), f32[16,64,128]{2,1,0:T(8,128)S(1)}, u32[]{:S(2)}, u32[]{:S(2)}) async-start(f32[16,64,128]{2,1,0:T(8,128)} %get-tuple-element.39), calls=%async_computation.1 | async-start | bytes 1048576 | tf_op jit(solution)/shard_map/all_to_all | solution.py:437
  39.0 0.0 copy-start.5
  39.0 0.9 %copy-done.5 = f32[64,8,128]{2,1,0:T(8,128)S(1)} copy-done((f32[64,8,128]{2,1,0:T(8,128)S(1)}, f32[64,8,128]{2,1,0:T(8,128)}, u32[]{:S(2)}) %copy-start.5) | copy-done | bytes 262168
  40.0 2.6 %heat.1 = (bf16[1024,1024]{1,0:T(8,128)(2,1)}, f32[64,8,128]{2,1,0:T(8,128)S(1)}, f32[4,64,128]{2,1,0:T(8,128)S(1)}, f32[4,64,128]{2,1,0:T(8,128)S(1)}) custom-call(f32[16,72,128]{2,1,0:T(8,128)S(1)} %all-to-all-done.refs_0_, s32[8,128]{1,0:T(8,128)S(1)} %copy-done.7, s32[8,128]{1,0:T(8,128)S(1)} %copy-done.6, ...), custom_call_target="tpu_custom_call" | custom-call | flops 268435456 | bytes 4194304 | tf_op jit(solution)/shard_map/heat/pallas_call | solution.py:514
  42.6 0.5 collective-permute-start.2
  43.1 4.0 %collective-permute-start.3 = (f32[4,64,128]{2,1,0:T(8,128)S(1)}, f32[4,64,128]{2,1,0:T(8,128)S(1)}, u32[]{:S(2)}, u32[]{:S(2)}) collective-permute-start(f32[4,64,128]{2,1,0:T(8,128)S(1)} %get-tuple-element.45), channel_id=1, source_target_pairs={{1,0},{2,1},{3,2},{4,3},{5,4},{6,5},{7,6},{8,7},{9,8},{10,9},{11,1... | collective-permute-start | bytes 393224 | tf_op jit(solution)/shard_map/ppermute | solution.py:433
  47.1 10.8 %tracer.1 = (f32[16,64,1024]{2,1,0:T(8,128)}, f32[16,64,1024]{2,1,0:T(8,128)}) custom-call(f32[16,64,1024]{2,1,0:T(8,128)} %species_hbm.3, f32[16,64,1024]{2,1,0:T(8,128)} %get-tuple-element.48.react_hbm, f32[64,1024]{1,0:T(8,128)S(1)} %get-tuple-element.49.warm_ref, f32[64,1024]{1,0:T(8,128)S(1)} %get-tuple-element.50.scale_ref, ...), custom_call_target="tpu_custom_call" | custom-call | flops 1610612736 | bytes 16777216 | tf_op jit(solution)/shard_map/tracer/pallas_call | solution.py:525
  57.9 0.0 collective-permute-done.2.left_ref
  57.9 0.0 collective-permute-done.3.right_ref
  57.9 2.2 %tile_two.1 = (f32[64,8,128]{2,1,0:T(8,128)}, f32[64,8,128]{2,1,0:T(8,128)}, f32[64,8,128]{2,1,0:T(8,128)S(1)}, f32[64,8,128]{2,1,0:T(8,128)}) custom-call(f32[64,8,128]{2,1,0:T(8,128)S(1)} %get-tuple-element.33.refs_3_.u_ref, f32[64,8,128]{2,1,0:T(8,128)S(1)} %get-tuple-element.34.refs_4_.v_ref, f32[64,8,128]{2,1,0:T(8,128)S(1)} %get-tuple-element.43.t_ref, ...), custom_call_target="tpu_custom_call" | custom-call | flops 3932160 | bytes 2097152 | tf_op jit(solution)/shard_map/tile_two/pallas_call | solution.py:535
  60.1 0.0 all-to-all-done.1.refs_5_
  60.1 7.1 %final.1 = (f32[16,64,1024]{2,1,0:T(8,128)}, f32[64,8,128]{2,1,0:T(8,128)}) custom-call(f32[16,64,1024]{2,1,0:T(8,128)} %get-tuple-element.54.refs_0_, f32[16,64,1024]{2,1,0:T(8,128)} %get-tuple-element.55.refs_1_, bf16[1024,1024]{1,0:T(8,128)(2,1)} %get-tuple-element.56.refs_2_, f32[8,1024]{1,0:T(8,128)S(1)} %get-tuple-element.52.depth_ref.refs_3_, ...), custom_call_target="tpu_custom_call" | custom-call | tf_op jit(solution)/shard_map/final/pallas_call | solution.py:545
  (1 shorter events, 0.0 us)
Async XLA Ops:
  0.6 11.4 %copy-start = (f32[64,8,128]{2,1,0:T(8,128)S(1)}, f32[64,8,128]{2,1,0:T(8,128)}, u32[]{:S(2)}) copy-start(f32[64,8,128]{2,1,0:T(8,128)} %refs_2_.4) | copy-start | bytes 786436
  0.6 11.4 %copy-start.1 = (f32[64,8,128]{2,1,0:T(8,128)S(1)}, f32[64,8,128]{2,1,0:T(8,128)}, u32[]{:S(2)}) copy-start(f32[64,8,128]{2,1,0:T(8,128)} %refs_0_.2) | copy-start | bytes 786436
  0.7 11.5 %copy-start.2 = (f32[64,8,128]{2,1,0:T(8,128)S(1)}, f32[64,8,128]{2,1,0:T(8,128)}, u32[]{:S(2)}) copy-start(f32[64,8,128]{2,1,0:T(8,128)} %refs_1_.4) | copy-start | bytes 786436
  0.7 11.5 %copy-start.3 = (f32[64,8,128]{2,1,0:T(8,128)S(1)}, f32[64,8,128]{2,1,0:T(8,128)}, u32[]{:S(2)}) copy-start(f32[64,8,128]{2,1,0:T(8,128)} %refs_3_.2) | copy-start | bytes 786436
  0.7 16.1 %copy-start.9 = (f32[16,16]{1,0:T(8,128)S(1)}, f32[16,16]{1,0:T(8,128)}, u32[]{:S(2)}) copy-start(f32[16,16]{1,0:T(8,128)} %coupling_ref.1) | copy-start | bytes 3076
  4.6 28.5 %all-to-all-start = ((f32[16,72,128]{2,1,0:T(8,128)}), f32[16,72,128]{2,1,0:T(8,128)S(1)}, u32[]{:S(2)}, u32[]{:S(2)}) async-start(f32[16,72,128]{2,1,0:T(8,128)} %get-tuple-element.35), calls=%async_computation | async-start | bytes 1179648 | tf_op jit(solution)/shard_map/all_to_all | solution.py:437
  12.1 16.8 %copy-start.6 = (s32[8,128]{1,0:T(8,128)S(1)}, s32[8,128]{1,0:T(8,128)}, u32[]{:S(2)}) copy-start(s32[8,128]{1,0:T(8,128)} %refs_6_.3) | copy-start | bytes 12292
  12.2 16.8 %copy-start.7 = (s32[8,128]{1,0:T(8,128)S(1)}, s32[8,128]{1,0:T(8,128)}, u32[]{:S(2)}) copy-start(s32[8,128]{1,0:T(8,128)} %refs_1_.7) | copy-start | bytes 12292
  12.3 20.8 %copy-start.8 = (f32[16]{0:T(128)S(1)}, f32[16]{0:T(128)}, u32[]{:S(2)}) copy-start(f32[16]{0:T(128)} %refs_4_.1) | copy-start | bytes 196
  12.3 16.6 %collective-permute-start = (f32[4,64,128]{2,1,0:T(8,128)S(1)}, f32[4,64,128]{2,1,0:T(8,128)S(1)}, u32[]{:S(2)}, u32[]{:S(2)}) collective-permute-start(f32[4,64,128]{2,1,0:T(8,128)S(1)} %get-tuple-element.62), channel_id=1, source_target_pairs={{0,1},{1,2},{2,3},{3,4},{4,5},{5,6},{6,7},{7,8},{8,9},{9,10},{10,1... | collective-permute-start | bytes 393224 | tf_op jit(solution)/shard_map/ppermute | solution.py:433
  12.8 16.2 %collective-permute-start.1 = (f32[4,64,128]{2,1,0:T(8,128)S(1)}, f32[4,64,128]{2,1,0:T(8,128)S(1)}, u32[]{:S(2)}, u32[]{:S(2)}) collective-permute-start(f32[4,64,128]{2,1,0:T(8,128)S(1)} %get-tuple-element.61), channel_id=1, source_target_pairs={{1,0},{2,1},{3,2},{4,3},{5,4},{6,5},{7,6},{8,7},{9,8},{10,9},{11,1... | collective-permute-start | bytes 393224 | tf_op jit(solution)/shard_map/ppermute | solution.py:433
  32.4 0.7 %copy-start.4 = (f32[64,8,128]{2,1,0:T(8,128)}, f32[64,8,128]{2,1,0:T(8,128)S(1)}, u32[]{:S(2)}) copy-start(f32[64,8,128]{2,1,0:T(8,128)S(1)} %get-tuple-element.41.refs_5_) | copy-start | bytes 786436
  35.0 25.1 %all-to-all-start.1 = ((f32[16,64,128]{2,1,0:T(8,128)}), f32[16,64,128]{2,1,0:T(8,128)S(1)}, u32[]{:S(2)}, u32[]{:S(2)}) async-start(f32[16,64,128]{2,1,0:T(8,128)} %get-tuple-element.39), calls=%async_computation.1 | async-start | bytes 1048576 | tf_op jit(solution)/shard_map/all_to_all | solution.py:437
  39.0 1.0 %copy-start.5 = (f32[64,8,128]{2,1,0:T(8,128)S(1)}, f32[64,8,128]{2,1,0:T(8,128)}, u32[]{:S(2)}) copy-start(f32[64,8,128]{2,1,0:T(8,128)} %copy-done.4) | copy-start | bytes 786436
  42.6 15.3 %collective-permute-start.2 = (f32[4,64,128]{2,1,0:T(8,128)S(1)}, f32[4,64,128]{2,1,0:T(8,128)S(1)}, u32[]{:S(2)}, u32[]{:S(2)}) collective-permute-start(f32[4,64,128]{2,1,0:T(8,128)S(1)} %get-tuple-element.44), channel_id=1, source_target_pairs={{0,1},{1,2},{2,3},{3,4},{4,5},{5,6},{6,7},{7,8},{8,9},{9,10},{10,1... | collective-permute-start | bytes 393224 | tf_op jit(solution)/shard_map/ppermute | solution.py:433
  43.1 14.8 %collective-permute-start.3 = (f32[4,64,128]{2,1,0:T(8,128)S(1)}, f32[4,64,128]{2,1,0:T(8,128)S(1)}, u32[]{:S(2)}, u32[]{:S(2)}) collective-permute-start(f32[4,64,128]{2,1,0:T(8,128)S(1)} %get-tuple-element.45), channel_id=1, source_target_pairs={{1,0},{2,1},{3,2},{4,3},{5,4},{6,5},{7,6},{8,7},{9,8},{10,9},{11,1... | collective-permute-start | bytes 393224 | tf_op jit(solution)/shard_map/ppermute | solution.py:433

commit v2 on v1

v2 whole, which is shorter than its diff:
```python
import jax
import jax.numpy as jnp
from jax import lax
from jax.experimental import pallas as pl
from jax.experimental.pallas import tpu as pltpu
from jax.sharding import PartitionSpec as P

SUBS = 2
AXES = ("cols", "comp")
F32 = jnp.float32
BF16 = jnp.bfloat16
MIB = 1024 * 1024
BLOCK = 1024


def split(x):
    hi = x.astype(BF16)
    return hi, (x - hi.astype(F32)).astype(BF16)


def split3(x):
    hi = x.astype(BF16)
    rest = x - hi.astype(F32)
    mid = rest.astype(BF16)
    return hi, mid, (rest - mid.astype(F32)).astype(BF16)


def mxu(a, b):
    return jnp.dot(a, b, preferred_element_type=F32)


def iota(shape, dim):
    return lax.broadcasted_iota(jnp.int32, shape, dim)


def pack(out_ref, row, x, cpair):
    groups = 128 // cpair
    rows = x.shape[0] // groups
    lane_group = iota((rows, 128), 1) // cpair
    for e in range(x.shape[1] // 128):
        part = x[:, e * 128 : (e + 1) * 128]
        for o in range(groups):
            out = None
            for g in range(groups):
                piece = part[g * rows : (g + 1) * rows]
                shift = (g - o) * cpair % 128
                if shift:
                    piece = pltpu.roll(piece, shift, 1)
                out = piece if out is None else jnp.where(lane_group == g, piece, out)
            out_ref[e * groups + o, row : row + rows, :] = out


def unpack(in_ref, row, rows, cpair, first, blocks):
    groups = 128 // cpair
    lane_group = iota((rows, 128), 1) // cpair
    columns = []
    for e in range(blocks):
        levels = []
        for g in range(groups):
            out = None
            for o in range(groups):
                piece = in_ref[first + e * groups + o, row : row + rows, :]
                shift = (o - g) * cpair % 128
                if shift:
                    piece = pltpu.roll(piece, shift, 1)
                out = piece if out is None else jnp.where(lane_group == o, piece, out)
            levels.append(out)
        columns.append(jnp.concatenate(levels, axis=0))
    return jnp.concatenate(columns, axis=1)


def running_total(x):
    levels = x.shape[0]
    lower = (iota((levels, levels), 1) <= iota((levels, levels), 0)).astype(F32).astype(BF16)
    return mxu(jnp.concatenate([lower] * 3, axis=1), jnp.concatenate(split3(x), axis=0))


def light(chloro):
    levels = chloro.shape[0]
    trans = jnp.exp(-running_total((0.5 + 0.1 * chloro * chloro) * (1.0 / levels)))
    above = jnp.where(iota(trans.shape, 0) == 0, 1.0, pltpu.roll(trans, 1, 0))
    return trans, levels * (above - trans)


def sink(amounts, fraction):
    for _ in range(SUBS):
        flux = fraction * amounts
        amounts = amounts - flux + pltpu.roll(flux, 1, 0)
    return amounts


def split_kron(coupling):
    tracers = coupling.shape[0]
    size = tracers * 8
    tall = (iota((size, tracers), 0) // 8 == iota((size, tracers), 1)).astype(F32).astype(BF16)
    wide = (iota((tracers, size), 1) // 8 == iota((tracers, size), 0)).astype(F32).astype(BF16)
    same = iota((size, size), 0) % 8 == iota((size, size), 1) % 8
    hi, lo = (jnp.where(same, mxu(mxu(tall, term).astype(BF16), wide), 0.0).astype(BF16) for term in split(coupling))
    return jnp.concatenate([jnp.concatenate([hi, hi], axis=1), jnp.concatenate([lo, jnp.zeros_like(lo)], axis=1)], axis=0)


def mix_levels(kron_ref, tracers_ref, scale_ref, out_ref, first, last):
    tracers, _, columns = tracers_ref.shape
    size = 8 * tracers

    def block(i, _):
        at = pl.ds(pl.multiple_of(i * BLOCK, BLOCK), BLOCK)
        for k in range(first, last, 8):
            hi, lo = split(tracers_ref[:, k : k + 8, at].reshape(size, BLOCK))
            both = mxu(kron_ref[...], jnp.concatenate([hi, lo], axis=0))
            mixed = both[:size] + both[size:]
            out_ref[:, k : k + 8, at] = mixed.reshape(tracers, 8, BLOCK) * scale_ref[k : k + 8, at][None]
        return 0

    lax.fori_loop(0, columns // BLOCK, block, 0)


def sink_all(species_ref, warm_ref, react_ref, depth_ref, settling_ref, wet, below, out_ref, before, after):
    tracers, levels, columns = species_ref.shape
    level = iota((levels, columns), 0).astype(F32)
    depth = depth_ref[0:1, :]
    wet[...] = jnp.where(level < depth, 1.0, 0.0)
    below[...] = jnp.where(level + 1.0 < depth, 1.0, 0.0)

    def one(n, _):
        before(n)
        fraction = settling_ref[n]
        for c in range(0, columns, 128):
            at = slice(c, c + 128)
            amounts = species_ref[n, :, at] + warm_ref[:, at] * react_ref[n, :, at]
            out_ref[n, :, at] = sink(amounts, fraction * below[:, at]) * wet[:, at]
        after(n)
        return 0

    lax.fori_loop(0, tracers, one, 0)


def place_columns(order, onehot, cpair):
    lons, lats = order.shape
    target = iota((lats, lons * lats), 1)
    across = buckets(order, cpair).astype(F32).T.astype(jnp.int32)
    for r in range(lons):
        onehot[r * lats : (r + 1) * lats, :] = jnp.where(target == across[:, r : r + 1], 1.0, 0.0).astype(BF16)


def buckets(order, cpair):
    ctile = order.shape[0] * order.shape[1]
    return (order >> (ctile.bit_length() - 1)) * cpair + (order & (cpair - 1))


def start_kernel(cpair, order_hbm, depth_hbm, temp_hbm, species_hbm, pay_hbm, scale_ref, order, depths, temp, chloro, pay, place, lhs, sems):
    levels, lons, lats = temp.shape
    copies = [
        pltpu.make_async_copy(src, dst, sems.at[i])
        for i, (src, dst) in enumerate(((order_hbm, order), (depth_hbm, depths), (species_hbm.at[0], chloro), (temp_hbm, temp)))
    ]
    for copy in copies:
        copy.start()
    rows = levels * cpair // 128
    copies[0].wait()
    place_columns(order[...], place, cpair)
    copies[1].wait()
    depth = depths[...].astype(F32)
    copies[2].wait()
    trans, heat = light(chloro[...])
    scale_ref[...] = 0.2 * trans
    pack(pay, 0, heat, cpair)
    send_heat = pltpu.make_async_copy(pay.at[:, 0:rows], pay_hbm.at[:, 0:rows], sems.at[4])
    send_heat.start()
    copies[3].wait()
    for r in range(lons):
        hi, lo = split(temp[:, r, :])
        at = slice(r * lats, (r + 1) * lats)
        lhs[0:levels, at] = hi
        lhs[levels : 2 * levels, at] = lo
        lhs[2 * levels : 2 * levels + 16, at] = jnp.broadcast_to(depth[r : r + 1], (16, lats)).astype(BF16)
    sent = mxu(lhs[...], place[...])
    pack(pay, rows, sent[0:levels] + sent[levels : 2 * levels], cpair)
    deep = sent[2 * levels : 2 * levels + 8]
    for d in range(pay.shape[0]):
        e, o = divmod(d * cpair, 128)
        part = deep[:, e * 128 : (e + 1) * 128]
        pay[d, 2 * rows : 2 * rows + 8, :] = pltpu.roll(part, 128 - o, 1) if o else part
    send_temp = pltpu.make_async_copy(pay.at[:, rows : 2 * rows + 8], pay_hbm.at[:, rows : 2 * rows + 8], sems.at[5])
    send_temp.start()
    send_heat.wait()
    send_temp.wait()


def react_kernel(species_hbm, scale_ref, coupling_ref, react_hbm, first_ref, kron_ref, species, react, sems, out_sems):
    tracers, levels, columns = species.shape
    span = 256 // tracers
    parts = [slice(k, k + span) for k in range(0, levels, span)]
    copies = [pltpu.make_async_copy(species_hbm.at[:, at], species.at[:, at], sems.at[i]) for i, at in enumerate(parts)]
    sends = [pltpu.make_async_copy(react.at[:, at], react_hbm.at[:, at], out_sems.at[i]) for i, at in enumerate(parts)]
    for copy in copies:
        copy.start()
    kron_ref[...] = split_kron(coupling_ref[...])
    for copy, send, at in zip(copies, sends, parts):
        copy.wait()
        mix_levels(kron_ref, species, scale_ref, react, at.start, at.stop)
        send.start()
    first_ref[0] = species[0]
    first_ref[1] = react[0]
    for send in sends:
        send.wait()


def tile_levels(fields, depth_ref, fcor_ref, outs):
    levels, lons, lats = fields[0].shape
    shape = (lons, lats)
    lon, lat = iota(shape, 0), iota(shape, 1)
    first_lon, last_lon, first_lat, last_lat = lon == 0, lon == lons - 1, lat == 0, lat == lats - 1
    depth = depth_ref[...]
    turn = jnp.broadcast_to(0.2 * fcor_ref[...], shape)

    def neighbours(f):
        return (
            jnp.where(first_lon, 0.0, pltpu.roll(f, 1, 0)),
            jnp.where(last_lon, 0.0, pltpu.roll(f, lons - 1, 0)),
            jnp.where(first_lat, 0.0, pltpu.roll(f, 1, 1)),
            jnp.where(last_lat, 0.0, pltpu.roll(f, lats - 1, 1)),
        )

    def eight(i, load):
        for j in range(8):
            k = i * 8 + j
            u, v, t, s = (f[k] for f in fields)
            load = load + (0.8 * s - 0.2 * t)
            wet = k < depth
            p0, p1, p2, p3 = neighbours(load)
            u0, u1, u2, u3 = neighbours(u)
            v0, v1, v2, v3 = neighbours(v)
            t0, t1, t2, t3 = neighbours(t)
            s0, s1, s2, s3 = neighbours(s)
            half_u, half_v = 0.1 * u, 0.1 * v
            new_u = 0.92 * u + turn * v - 0.01 * (p1 - p0) + 0.02 * ((u0 + u1) + (u2 + u3))
            new_v = 0.92 * v - turn * u - 0.01 * (p3 - p2) + 0.02 * ((v0 + v1) + (v2 + v3))
            new_t = 0.92 * t - half_u * (t1 - t0) - half_v * (t3 - t2) + 0.02 * ((t0 + t1) + (t2 + t3))
            new_s = 0.92 * s - half_u * (s1 - s0) - half_v * (s3 - s2) + 0.02 * ((s0 + s1) + (s2 + s3))
            for out, new in zip(outs, (new_u, new_v, new_t, new_s)):
                out[k] = jnp.where(wet, new, 0.0)
        return load

    lax.fori_loop(0, levels // 8, eight, jnp.zeros(shape, F32))


def tracer_term(halo, own, depth, sign):
    return jnp.where(iota(halo.shape, 0) < depth, (0.02 + sign * 0.1 * own) * halo, 0.0)


def edge_terms(halo_ref, own, depth, sign):
    wet = iota(own.shape, 0) < depth
    load = running_total(0.8 * halo_ref[3] - 0.2 * halo_ref[2])
    return (
        jnp.where(wet, 0.02 * halo_ref[0] + sign * 0.01 * load, 0.0),
        jnp.where(wet, 0.02 * halo_ref[1], 0.0),
        tracer_term(halo_ref[2], own, depth, sign),
        tracer_term(halo_ref[3], own, depth, sign),
    )


def first_tile_kernel(cpair, u_ref, v_ref, t_ref, s_ref, depth_ref, fcor_ref, order_ref, fields_hbm, sent_ref, edge_ref, fields, place, lhs, sem):
    levels, lons, lats = t_ref.shape
    ctile = lons * lats
    tile_levels((u_ref, v_ref, t_ref, s_ref), depth_ref, fcor_ref, [fields.at[n] for n in range(4)])
    save = pltpu.make_async_copy(fields, fields_hbm, sem.at[0])
    save.start()
    place_columns(order_ref[...], place, cpair)
    edge_ref[0:lats, :] = place[0:lats, :]
    edge_ref[lats : 2 * lats, :] = place[ctile - lats : ctile, :]
    for r in range(lons):
        at = slice(r * lats, (r + 1) * lats)
        lhs[0:levels, at], lhs[levels : 2 * levels, at] = split(fields[2, :, r, :])
    sent = mxu(lhs[...], place[...])
    sent_ref[...] = sent[0:levels] + sent[levels : 2 * levels]
    save.wait()


def chloro_kernel(cpair, recv_ref, settling_ref, first_ref, sent_ref, edge_ref, left_ref, right_ref, first_lon_ref, last_lon_ref, wet_ref,
                  pay_hbm, warm_ref, depth_ref, scale_ref, pay, sems):
    levels, columns = warm_ref.shape
    lons, lats = wet_ref.shape
    rows = levels * cpair // 128
    groups = 128 // cpair
    lane_group = iota((8, 128), 1) // cpair
    for e in range(columns // 128):
        out = None
        for o in range(groups):
            piece = recv_ref[e * groups + o, 2 * rows : 2 * rows + 8, :]
            if o:
                piece = pltpu.roll(piece, o * cpair, 1)
            out = piece if out is None else jnp.where(lane_group == o, piece, out)
        depth_ref[:, e * 128 : (e + 1) * 128] = out
    warm = jnp.exp(0.15 * unpack(recv_ref, rows, rows, cpair, 0, columns // 128))
    warm_ref[...] = warm
    level = iota((levels, columns), 0).astype(F32)
    depth = depth_ref[0:1, :]
    amounts = first_ref[0] + warm * first_ref[1]
    amounts = sink(amounts, jnp.where(level + 1.0 < depth, settling_ref[0], 0.0))
    trans, heat = light(jnp.where(level < depth, amounts, 0.0))
    scale_ref[...] = 0.2 * trans
    pack(pay, rows, heat, cpair)
    send_heat = pltpu.make_async_copy(pay.at[:, rows : 2 * rows], pay_hbm.at[:, rows : 2 * rows], sems.at[0])
    send_heat.start()
    terms = [
        split(tracer_term(halo[2], own[0], wet_ref[lon : lon + 1, :], sign))
        for halo, own, lon, sign in ((left_ref, first_lon_ref, 0, 1.0), (right_ref, last_lon_ref, lons - 1, -1.0))
    ]
    extra = mxu(jnp.concatenate([jnp.concatenate(term, axis=0) for term in terms], axis=1), edge_ref[...])
    pack(pay, 0, sent_ref[...] + (extra[:levels] + extra[levels:]), cpair)
    send_x = pltpu.make_async_copy(pay.at[:, 0:rows], pay_hbm.at[:, 0:rows], sems.at[1])
    send_x.start()
    send_heat.wait()
    send_x.wait()


def back_columns(order, onehot, cpair):
    lons, lats = order.shape
    bucket = buckets(order, cpair)
    source = iota((lons * lats, lats), 0)
    for r in range(lons):
        onehot[:, r * lats : (r + 1) * lats] = jnp.where(source == bucket[r : r + 1], 1.0, 0.0).astype(BF16)


def finish_tile(cpair, recv_ref, row, back_ref, depth_ref, left_ref, right_ref, first_lon_ref, last_lon_ref, fields, out):
    _, levels, lons, lats = out.shape
    ctile = lons * lats
    heat = unpack(recv_ref, row, levels * cpair // 128, cpair, 0, ctile // 128)
    placed = mxu(jnp.concatenate(split(heat), axis=0), back_ref[...])
    placed = 0.2 * (placed[:levels] + placed[levels:])
    for n in (0, 1, 3):
        out[n] = fields[n]
    level = iota((levels, lats), 0)
    for r in range(lons):
        part = placed[:, r * lats : (r + 1) * lats]
        out[2, :, r, :] = fields[2, :, r, :] + jnp.where(level < depth_ref[r : r + 1, :], part, 0.0)
    for halo, own, lon, sign in ((left_ref, first_lon_ref, 0, 1.0), (right_ref, last_lon_ref, lons - 1, -1.0)):
        for n, term in enumerate(edge_terms(halo, own[0], depth_ref[lon : lon + 1, :], sign)):
            out[n, :, lon, :] = out[n, :, lon, :] + term


def heat_kernel(cpair, fields_hbm, recv_ref, order_ref, depth_ref, left_ref, right_ref, first_lon_ref, last_lon_ref,
                out_ref, left_edge_ref, right_edge_ref, fields, back, sem):
    fetch = pltpu.make_async_copy(fields_hbm, fields, sem.at[0])
    fetch.start()
    lons = order_ref.shape[0]
    back_columns(order_ref[...], back, cpair)
    fetch.wait()
    finish_tile(cpair, recv_ref, 0, back, depth_ref, left_ref, right_ref, first_lon_ref, last_lon_ref, fields, out_ref)
    for n in range(4):
        left_edge_ref[n] = out_ref[n, :, 0, :]
        right_edge_ref[n] = out_ref[n, :, lons - 1, :]


def tracer_kernel(species_hbm, react_hbm, warm_ref, scale_ref, depth_ref, kron_ref, settling_ref, out_hbm, next_hbm,
                  species, react, heat, wet, below, in_sems, out_sems, next_sems):
    tracers, levels, columns = species.shape
    span = 256 // tracers

    def fetch(n):
        return (
            pltpu.make_async_copy(species_hbm.at[n], species.at[n], in_sems.at[2 * n]),
            pltpu.make_async_copy(react_hbm.at[n], react.at[n], in_sems.at[2 * n + 1]),
        )

    def save(n):
        return pltpu.make_async_copy(species.at[n], out_hbm.at[n], out_sems.at[n])

    for n in range(tracers):
        for copy in fetch(n):
            copy.start()

    def before(n):
        for copy in fetch(n):
            copy.wait()

        @pl.when(n == 0)
        def _():
            heat[...] = light(species[0])[1]

    sink_all(species, warm_ref, react, depth_ref, settling_ref, wet, below, species, before, lambda n: save(n).start())
    below[...] = scale_ref[...] * jnp.exp(0.03 * (wet[...] * heat[...]))
    parts = [slice(k, k + span) for k in range(0, levels, span)]
    sends = [pltpu.make_async_copy(react.at[:, at], next_hbm.at[:, at], next_sems.at[i]) for i, at in enumerate(parts)]
    for send, at in zip(sends, parts):
        mix_levels(kron_ref, species, below, react, at.start, at.stop)
        send.start()
    for n in range(tracers):
        save(n).wait()
    for send in sends:
        send.wait()


def second_tile_kernel(fields, depth_ref, fcor_ref, out):
    tile_levels([fields.at[n] for n in range(4)], depth_ref, fcor_ref, [out.at[n] for n in range(4)])


def final_kernel(cpair, species_hbm, react_hbm, depth_ref, settling_ref, recv_ref, order_ref, wet_ref, left_ref, right_ref, first_lon_ref, last_lon_ref,
                 fields, out_hbm, *rest):
    field_hbms, (species, react, back, tile, warm, wet, below, in_sems, out_sems, sems) = rest[:4], rest[4:]
    tracers, levels, columns = species.shape
    rows = levels * cpair // 128

    def fetch(n):
        return (
            pltpu.make_async_copy(species_hbm.at[n], species.at[n], in_sems.at[2 * n]),
            pltpu.make_async_copy(react_hbm.at[n], react.at[n], in_sems.at[2 * n + 1]),
        )

    def send(n):
        return pltpu.make_async_copy(species.at[n], out_hbm.at[n], out_sems.at[n])

    for n in range(tracers):
        for copy in fetch(n):
            copy.start()

    def before(n):
        for copy in fetch(n):
            copy.wait()

    back_columns(order_ref[...], back, cpair)
    finish_tile(cpair, recv_ref, rows, back, wet_ref, left_ref, right_ref, first_lon_ref, last_lon_ref, fields, tile)
    sends = [pltpu.make_async_copy(tile.at[n], field_hbms[n], sems.at[n]) for n in range(4)]
    for copy in sends:
        copy.start()
    warm[...] = jnp.exp(0.15 * unpack(recv_ref, 0, rows, cpair, 0, columns // 128))
    sink_all(species, warm, react, depth_ref, settling_ref, wet, below, species, before, lambda n: send(n).start())
    for n in range(tracers):
        send(n).wait()
    for copy in sends:
        copy.wait()


def whole(count):
    return [pl.BlockSpec(memory_space=pltpu.VMEM)] * count


def in_hbm(x):
    return pltpu.with_memory_space_constraint(x, pltpu.HBM)


ANY = pl.BlockSpec(memory_space=pl.ANY)
SMEM = pl.BlockSpec(memory_space=pltpu.SMEM)


def params(mib):
    return pltpu.CompilerParams(vmem_limit_bytes=mib * MIB)


def cost(flops, moved):
    return pl.CostEstimate(flops=flops, bytes_accessed=moved, transcendentals=0)


def halo(left_edge, right_edge):
    count = lax.axis_size(AXES)
    ahead = [(i, (i + 1) % count) for i in range(count)]
    return lax.ppermute(right_edge, AXES, ahead), lax.ppermute(left_edge, AXES, [(b, a) for a, b in ahead])


def exchange(pay):
    return lax.all_to_all(pay, AXES, split_axis=0, concat_axis=0, tiled=True)


def body(u, v, temp, salt, species, wet_layers, order, coupling, settling):
    levels, lons, lats = temp.shape
    tracers, _, ctile = species.shape
    tiles = lax.axis_size(AXES)
    cpair = ctile // tiles
    rows = levels * cpair // 128
    edge = jax.ShapeDtypeStruct((4, levels, lats), F32)
    column = jax.ShapeDtypeStruct((levels, ctile), F32)
    patch = pltpu.HBM((tracers, levels, ctile), F32)
    fcor = (0.8 * jnp.sin(jnp.pi * (jnp.arange(lats, dtype=F32) + 0.5) / lats - jnp.pi / 2))[None]
    sem = pltpu.SemaphoreType.DMA
    mix_flops = 6 * 256 * levels * tracers * ctile
    patch_scratch = pltpu.VMEM((tracers, levels, ctile), F32)
    column_scratch = pltpu.VMEM((levels, ctile), F32)
    onehot_scratch = pltpu.VMEM((ctile, ctile), BF16)

    fields_scratch = pltpu.VMEM((4, levels, lons, lats), F32)

    pay, scale1 = pl.pallas_call(
        lambda *refs: start_kernel(cpair, *refs),
        out_shape=[pltpu.HBM((tiles, 2 * rows + 8, 128), F32), column],
        in_specs=[ANY] * 4,
        out_specs=[ANY] + whole(1),
        scratch_shapes=[
            pltpu.VMEM((lons, lats), jnp.int32),
            pltpu.VMEM((lons, lats), jnp.int32),
            pltpu.VMEM((levels, lons, lats), F32),
            column_scratch,
            pltpu.VMEM((tiles, 2 * rows + 8, 128), F32),
            onehot_scratch,
            pltpu.VMEM((2 * levels + 16, ctile), BF16),
            sem((6,)),
        ],
        compiler_params=params(12),
        name="start",
    )(in_hbm(order), in_hbm(wet_layers), in_hbm(temp), in_hbm(species))
    recv_a = exchange(pay)

    stacked = jnp.stack([u, v, temp, salt])
    edges = stacked[:, :, 0], stacked[:, :, lons - 1]
    left, right = halo(*edges)
    groups = levels * tracers // 256
    react1, first, kron = pl.pallas_call(
        react_kernel,
        out_shape=[patch, jax.ShapeDtypeStruct((2, levels, ctile), F32), jax.ShapeDtypeStruct((16 * tracers, 16 * tracers), BF16)],
        in_specs=[ANY] + whole(2),
        out_specs=[ANY] + whole(2),
        scratch_shapes=[patch_scratch, patch_scratch, sem((groups,)), sem((groups,))],
        compiler_params=params(16),
        cost_estimate=cost(mix_flops, 8 * MIB),
        name="react",
    )(in_hbm(species), scale1, coupling)
    fields1, sent, edge_place = pl.pallas_call(
        lambda *refs: first_tile_kernel(cpair, *refs),
        out_shape=[pltpu.HBM((4, levels, lons, lats), F32), column, jax.ShapeDtypeStruct((2 * lats, ctile), BF16)],
        in_specs=whole(7),
        out_specs=[ANY] + whole(2),
        scratch_shapes=[fields_scratch, onehot_scratch, pltpu.VMEM((2 * levels, ctile), BF16), sem((1,))],
        compiler_params=params(12),
        cost_estimate=cost(4 * levels * ctile * ctile, 2 * MIB),
        name="tile_one",
    )(u, v, temp, salt, wet_layers, fcor, order)

    pay, warm, depth, scale2 = pl.pallas_call(
        lambda *refs: chloro_kernel(cpair, *refs),
        out_shape=[pltpu.HBM((tiles, 2 * rows, 128), F32), column, jax.ShapeDtypeStruct((8, ctile), F32), column],
        in_specs=[*whole(1), SMEM, *whole(8)],
        out_specs=[ANY, *whole(3)],
        scratch_shapes=[pltpu.VMEM((tiles, 2 * rows, 128), F32), sem((2,))],
        compiler_params=params(8),
        name="chloro",
    )(recv_a, settling, first, sent, edge_place, left, right, *edges, wet_layers)
    recv_b = exchange(pay)

    recv_a, _ = lax.optimization_barrier((recv_a, pay))
    fields1, *edges = pl.pallas_call(
        lambda *refs: heat_kernel(cpair, *refs),
        out_shape=[jax.ShapeDtypeStruct((4, levels, lons, lats), F32), edge, edge],
        in_specs=[ANY] + whole(7),
        out_specs=whole(3),
        scratch_shapes=[fields_scratch, onehot_scratch, sem((1,))],
        compiler_params=params(12),
        cost_estimate=cost(4 * levels * ctile * ctile, 4 * MIB),
        name="heat",
    )(in_hbm(fields1), recv_a, order, wet_layers, left, right, *edges)
    left, right = halo(*edges)
    species1, react2 = pl.pallas_call(
        tracer_kernel,
        out_shape=[patch, patch],
        in_specs=[ANY] * 2 + whole(4) + [SMEM],
        out_specs=[ANY] * 2,
        scratch_shapes=[patch_scratch] * 2 + [column_scratch] * 3 + [sem((2 * tracers,)), sem((tracers,)), sem((groups,))],
        compiler_params=params(16),
        cost_estimate=cost(mix_flops, 16 * MIB),
        name="tracer",
    )(in_hbm(species), in_hbm(react1), warm, scale2, depth, kron, settling)
    fields2 = pl.pallas_call(
        second_tile_kernel,
        out_shape=jax.ShapeDtypeStruct((4, levels, lons, lats), F32),
        in_specs=whole(3),
        out_specs=whole(1)[0],
        compiler_params=params(8),
        cost_estimate=cost(60 * levels * ctile, 2 * MIB),
        name="tile_two",
    )(fields1, wet_layers, fcor)

    species2, u2, v2, t2, s2 = pl.pallas_call(
        lambda *refs: final_kernel(cpair, *refs),
        out_shape=[patch] + [pltpu.HBM((levels, lons, lats), F32)] * 4,
        in_specs=[ANY] * 2 + whole(1) + [SMEM] + whole(8),
        out_specs=[ANY] * 5,
        scratch_shapes=[
            patch_scratch,
            patch_scratch,
            onehot_scratch,
            fields_scratch,
            column_scratch,
            column_scratch,
            column_scratch,
            sem((2 * tracers,)),
            sem((tracers,)),
            sem((4,)),
        ],
        compiler_params=params(20),
        name="final",
    )(in_hbm(species1), in_hbm(react2), depth, settling, recv_b, order, wet_layers, left, right, *edges, fields2)
    return u2, v2, t2, s2, species2


def solution(mesh):
    tile = P(None, ("groups", "cols", "comp"), None)
    patch = P(None, None, ("groups", "cols", "comp"))
    index = P(("groups", "cols", "comp"), None)
    return jax.shard_map(
        body,
        mesh=mesh,
        in_specs=(tile, tile, tile, tile, patch, index, index, P(), P()),
        out_specs=(tile, tile, tile, tile, patch),
        check_vma=False,
    )
```

time: 67.6 us -> 59.9 us (0.89)
  Pallas kernels: 38.6 us -> 32 us
  local copies, waits for them, and re-layouts: 1.89 us -> 0.24 us
    pallas_call x1, Pallas kernels: 10.8 us -> 7.99 us  [body(): pl.pallas_call(tracer_kernel, out_shape=[patch, patch], in_specs=[ANY] *...]
    pallas_call x1, Pallas kernels: 6.62 us -> 4.1 us  [body(): pl.pallas_call(react_kernel, out_shape=[patch, jax.ShapeDtypeStruct((2, l...]
    unnamed x22 -> x18, local copies, waits for them, and re-layouts: 1.79 us -> 0.14 us
    pallas_call x2, Pallas kernels: 4.8 us -> 3.7 us  [the longest x1 2.42 us: body(): pl.pallas_call(lambda *refs: heat_kernel(cpair, *refs), out_shape=[jax.Sh...]
  transfers between devices with their start and end apart: 6 -> 6, of which waited for: 1 -> 2; matrix products, arithmetic and copies ran while one was open for 0% -> 0% of each run, Pallas kernels for 38% -> 31%
where the time goes in v2:
time: 59.9 us; the launch traced here: 59.5 us
  Pallas kernels  32 us (53%)
  starting transfers between devices  20.9 us (35%)
  waiting for transfers between devices  5.21 us (9%)
  between operations  1.04 us (2%)
    all_to_all x2, starting transfers between devices, exchange(): return lax.all_to_all(pay, AXES, split_axis=0, concat_axis=0, tiled=True)  11.8 us
    ppermute x2, starting transfers between devices, halo(): lax.ppermute(left_edge, AXES, [(b, a) for a, b in ahead])  8.65 us
    pallas_call x1, Pallas kernels, body(): pl.pallas_call(tracer_kernel, out_shape=[patch, patch], in_specs=[ANY] *...  7.99 us
    pallas_call x1, Pallas kernels, body(): pl.pallas_call(lambda *refs: final_kernel(cpair, *refs), out_shape=[patch...  7.53 us
    ppermute x2, waiting for transfers between devices, halo(): lax.ppermute(right_edge, AXES, ahead)  4.98 us
    pallas_call x1, Pallas kernels, body(): pl.pallas_call(react_kernel, out_shape=[patch, jax.ShapeDtypeStruct((2, l...  4.1 us
    pallas_call x1, Pallas kernels, body(): pl.pallas_call(lambda *refs: start_kernel(cpair, *refs), out_shape=[pltpu...  3.82 us
    pallas_call x1, Pallas kernels, body(): pl.pallas_call(lambda *refs: first_tile_kernel(cpair, *refs), out_shape=[...  2.81 us
  transfers between devices with their start and end apart: 6, of which 2 were waited for; matrix products, arithmetic and copies ran while one was open for 0% of the time, Pallas kernels for 31%

profile of v2, /device:TPU:0, one launch (start us, length us, event | category | flops | bytes accessed | tf_op | source)
XLA Modules:
  0.0 59.5 jit_solution(11153700571557641294)
XLA Ops:
  0.6 0.0 copy-start.4
  0.6 0.0 copy-start.5
  0.7 0.0 copy-start
  0.7 0.0 copy-start.1
  0.7 0.0 copy-start.3
  0.7 0.0 copy-start.2
  0.7 0.0 copy-start.7
  0.7 3.8 %start.1 = (f32[16,72,128]{2,1,0:T(8,128)}, f32[64,1024]{1,0:T(8,128)S(1)}) custom-call(s32[8,128]{1,0:T(8,128)} %refs_5_.1, s32[8,128]{1,0:T(8,128)} %refs_6_.3, f32[64,8,128]{2,1,0:T(8,128)} %refs_2_.4, f32[16,64,1024]{2,1,0:T(8,128)} %species_hbm.3), custom_call_target="tpu_custom_call" | custom-call | tf_op jit(solution)/shard_map/start/pallas_call | solution.py:483
  4.5 7.4 %all-to-all-start = ((f32[16,72,128]{2,1,0:T(8,128)}), f32[16,72,128]{2,1,0:T(8,128)S(1)}, u32[]{:S(2)}, u32[]{:S(2)}) async-start(f32[16,72,128]{2,1,0:T(8,128)} %get-tuple-element.30), calls=%async_computation | async-start | bytes 1179648 | tf_op jit(solution)/shard_map/all_to_all | solution.py:462
  11.9 0.0 copy-done
  11.9 0.1 copy.22
  12.0 0.0 copy-done.1
  12.0 0.1 copy.23
  12.1 0.0 copy-done.3
  12.1 0.0 copy-done.2
  12.1 0.1 copy_bitcast_fusion
  12.2 0.0 copy-start.6
  12.2 4.4 %collective-permute-start.1 = (f32[4,64,128]{2,1,0:T(8,128)S(1)}, f32[4,64,128]{2,1,0:T(8,128)S(1)}, u32[]{:S(2)}, u32[]{:S(2)}) collective-permute-start(f32[4,64,128]{2,1,0:T(8,128)S(1)} %get-tuple-element.51.refs_7_.refs_6_), channel_id=1, source_target_pairs={{1,0},{2,1},{3,2},{4,3},{5,4},{6,5},{7,6},{8,7},{9,8},{10,9},{11,1... | collective-permute-start | bytes 393224 | tf_op jit(solution)/shard_map/ppermute | solution.py:458
  16.7 0.0 collective-permute-start
  16.7 0.0 copy-done.4
  16.7 0.0 copy-done.5
  16.7 2.8 %tile_one.1 = (f32[4,64,8,128]{3,2,1,0:T(8,128)}, f32[64,1024]{1,0:T(8,128)S(1)}, bf16[256,1024]{1,0:T(8,128)(2,1)S(1)}) custom-call(f32[64,8,128]{2,1,0:T(8,128)S(1)} %copy-done.1, f32[64,8,128]{2,1,0:T(8,128)S(1)} %copy-done.2, f32[64,8,128]{2,1,0:T(8,128)S(1)} %copy-done, f32[64,8,128]{2,1,0:T(8,128)S(1)} %copy-done.3, s32[8,128]{1,0:T(8,128)S(1)} %copy-done.4, ...), custom_call_target="tpu_custom_call" | custom-call | flops 268435456 | bytes 2097152 | tf_op jit(solution)/shard_map/tile_one/pallas_call | solution.py:517
  19.6 0.0 copy-done.7
  19.6 4.1 %react.1 = (f32[16,64,1024]{2,1,0:T(8,128)}, f32[2,64,1024]{2,1,0:T(8,128)S(1)}, bf16[256,256]{1,0:T(8,128)(2,1)S(1)}) custom-call(f32[16,64,1024]{2,1,0:T(8,128)} %species_hbm.3, f32[64,1024]{1,0:T(8,128)S(1)} %get-tuple-element.28.scale_ref, f32[16,16]{1,0:T(8,128)S(1)} %copy-done.7), custom_call_target="tpu_custom_call" | custom-call | flops 1610612736 | bytes 8388608 | tf_op jit(solution)/shard_map/react/pallas_call | solution.py:507
  23.7 0.2 collective-permute-done.1.refs_6_.refs_5_
  23.9 5.0 %collective-permute-done.refs_5_.refs_4_ = f32[4,64,128]{2,1,0:T(8,128)S(1)} collective-permute-done((f32[4,64,128]{2,1,0:T(8,128)S(1)}, f32[4,64,128]{2,1,0:T(8,128)S(1)}, u32[]{:S(2)}, u32[]{:S(2)}) %collective-permute-start) | collective-permute-done | bytes 131104 | tf_op jit(solution)/shard_map/ppermute | solution.py:458
  28.9 0.0 all-to-all-done.refs_0_.refs_1_
  28.9 0.0 copy-done.6
  28.9 2.1 %chloro.1 = (f32[16,64,128]{2,1,0:T(8,128)}, f32[64,1024]{1,0:T(8,128)S(1)}, f32[8,1024]{1,0:T(8,128)S(1)}, f32[64,1024]{1,0:T(8,128)S(1)}) custom-call(f32[16,72,128]{2,1,0:T(8,128)S(1)} %all-to-all-done.refs_0_.refs_1_, f32[16]{0:T(128)S(1)} %copy-done.6, f32[2,64,1024]{2,1,0:T(8,128)S(1)} %get-tuple-element.31.refs_2_, ...), custom_call_target="tpu_custom_call" | custom-call | tf_op jit(solution)/shard_map/chloro/pallas_call | solution.py:528
  31.0 4.4 %all-to-all-start.1 = ((f32[16,64,128]{2,1,0:T(8,128)}), f32[16,64,128]{2,1,0:T(8,128)S(1)}, u32[]{:S(2)}, u32[]{:S(2)}) async-start(f32[16,64,128]{2,1,0:T(8,128)} %get-tuple-element.40), calls=%async_computation.1 | async-start | bytes 1048576 | tf_op jit(solution)/shard_map/all_to_all | solution.py:462
  35.4 2.4 %heat.1 = (f32[4,64,8,128]{3,2,1,0:T(8,128)S(1)}, f32[4,64,128]{2,1,0:T(8,128)S(1)}, f32[4,64,128]{2,1,0:T(8,128)S(1)}) custom-call(f32[4,64,8,128]{3,2,1,0:T(8,128)} %get-tuple-element.41.refs_0_, f32[16,72,128]{2,1,0:T(8,128)S(1)} %all-to-all-done.refs_0_.refs_1_, s32[8,128]{1,0:T(8,128)S(1)} %copy-done.5, s32[8,128]{1,0:T(8,128)S(1)} %copy-done.4, ...), custom_call_target="tpu_custom_call" | custom-call | flops 268435456 | bytes 4194304 | tf_op jit(solution)/shard_map/heat/pallas_call | solution.py:540
  37.8 0.5 collective-permute-start.2
  38.3 4.2 %collective-permute-start.3 = (f32[4,64,128]{2,1,0:T(8,128)S(1)}, f32[4,64,128]{2,1,0:T(8,128)S(1)}, u32[]{:S(2)}, u32[]{:S(2)}) collective-permute-start(f32[4,64,128]{2,1,0:T(8,128)S(1)} %get-tuple-element.44.refs_9_), channel_id=1, source_target_pairs={{1,0},{2,1},{3,2},{4,3},{5,4},{6,5},{7,6},{8,7},{9,8},{10,9},{11,1... | collective-permute-start | bytes 393224 | tf_op jit(solution)/shard_map/ppermute | solution.py:458
  42.5 1.3 %tile_two.1.refs_11_ = f32[4,64,8,128]{3,2,1,0:T(8,128)S(1)} custom-call(f32[4,64,8,128]{3,2,1,0:T(8,128)S(1)} %get-tuple-element.45.fields, s32[8,128]{1,0:T(8,128)S(1)} %copy-done.4, f32[1,128]{1,0:T(1,128)S(1)} %sine_multiply_fusion.refs_5_.fcor_ref), custom_call_target="tpu_custom_call" | custom-call | flops 3932160 | bytes 2097152 | tf_op jit(solution)/shard_map/tile_two/pallas_call | solution.py:561
  43.8 8.0 %tracer.1 = (f32[16,64,1024]{2,1,0:T(8,128)}, f32[16,64,1024]{2,1,0:T(8,128)}) custom-call(f32[16,64,1024]{2,1,0:T(8,128)} %species_hbm.3, f32[16,64,1024]{2,1,0:T(8,128)} %get-tuple-element.29.react_hbm, f32[64,1024]{1,0:T(8,128)S(1)} %get-tuple-element.34.warm_ref, f32[64,1024]{1,0:T(8,128)S(1)} %get-tuple-element.35.scale_ref, ...), custom_call_target="tpu_custom_call" | custom-call | flops 1610612736 | bytes 16777216 | tf_op jit(solution)/shard_map/tracer/pallas_call | solution.py:551
  51.8 0.0 collective-permute-done.2.refs_7_
  51.8 0.0 collective-permute-done.3.refs_8_
  51.8 0.0 all-to-all-done.1.refs_4_
  51.8 7.5 %final.1 = (f32[16,64,1024]{2,1,0:T(8,128)}, f32[64,8,128]{2,1,0:T(8,128)}, f32[64,8,128]{2,1,0:T(8,128)}, f32[64,8,128]{2,1,0:T(8,128)}, f32[64,8,128]{2,1,0:T(8,128)}) custom-call(f32[16,64,1024]{2,1,0:T(8,128)} %get-tuple-element.38.refs_0_, f32[16,64,1024]{2,1,0:T(8,128)} %get-tuple-element.39.refs_1_, ...), custom_call_target="tpu_custom_call" | custom-call | tf_op jit(solution)/shard_map/final/pallas_call | solution.py:571
  (2 shorter events, 0.1 us)
Async XLA Ops:
  0.6 16.1 %copy-start.4 = (s32[8,128]{1,0:T(8,128)S(1)}, s32[8,128]{1,0:T(8,128)}, u32[]{:S(2)}) copy-start(s32[8,128]{1,0:T(8,128)} %refs_6_.3) | copy-start | bytes 12292
  0.6 16.1 %copy-start.5 = (s32[8,128]{1,0:T(8,128)S(1)}, s32[8,128]{1,0:T(8,128)}, u32[]{:S(2)}) copy-start(s32[8,128]{1,0:T(8,128)} %refs_5_.1) | copy-start | bytes 12292
  0.7 11.3 %copy-start = (f32[64,8,128]{2,1,0:T(8,128)S(1)}, f32[64,8,128]{2,1,0:T(8,128)}, u32[]{:S(2)}) copy-start(f32[64,8,128]{2,1,0:T(8,128)} %refs_2_.4) | copy-start | bytes 786436
  0.7 11.3 %copy-start.1 = (f32[64,8,128]{2,1,0:T(8,128)S(1)}, f32[64,8,128]{2,1,0:T(8,128)}, u32[]{:S(2)}) copy-start(f32[64,8,128]{2,1,0:T(8,128)} %refs_0_.3) | copy-start | bytes 786436
  0.7 11.4 %copy-start.3 = (f32[64,8,128]{2,1,0:T(8,128)S(1)}, f32[64,8,128]{2,1,0:T(8,128)}, u32[]{:S(2)}) copy-start(f32[64,8,128]{2,1,0:T(8,128)} %refs_3_.5) | copy-start | bytes 786436
  0.7 11.4 %copy-start.2 = (f32[64,8,128]{2,1,0:T(8,128)S(1)}, f32[64,8,128]{2,1,0:T(8,128)}, u32[]{:S(2)}) copy-start(f32[64,8,128]{2,1,0:T(8,128)} %refs_1_.4) | copy-start | bytes 786436
  0.7 18.9 %copy-start.7 = (f32[16,16]{1,0:T(8,128)S(1)}, f32[16,16]{1,0:T(8,128)}, u32[]{:S(2)}) copy-start(f32[16,16]{1,0:T(8,128)} %coupling_ref.1) | copy-start | bytes 3076
  4.5 24.4 %all-to-all-start = ((f32[16,72,128]{2,1,0:T(8,128)}), f32[16,72,128]{2,1,0:T(8,128)S(1)}, u32[]{:S(2)}, u32[]{:S(2)}) async-start(f32[16,72,128]{2,1,0:T(8,128)} %get-tuple-element.30), calls=%async_computation | async-start | bytes 1179648 | tf_op jit(solution)/shard_map/all_to_all | solution.py:462
  12.2 16.7 %copy-start.6 = (f32[16]{0:T(128)S(1)}, f32[16]{0:T(128)}, u32[]{:S(2)}) copy-start(f32[16]{0:T(128)} %refs_3_.7) | copy-start | bytes 196
  12.2 11.7 %collective-permute-start.1 = (f32[4,64,128]{2,1,0:T(8,128)S(1)}, f32[4,64,128]{2,1,0:T(8,128)S(1)}, u32[]{:S(2)}, u32[]{:S(2)}) collective-permute-start(f32[4,64,128]{2,1,0:T(8,128)S(1)} %get-tuple-element.51.refs_7_.refs_6_), channel_id=1, source_target_pairs={{1,0},{2,1},{3,2},{4,3},{5,4},{6,5},{7,6},{8,7},{9,8},{10,9},{11,1... | collective-permute-start | bytes 393224 | tf_op jit(solution)/shard_map/ppermute | solution.py:458
  16.7 12.2 %collective-permute-start = (f32[4,64,128]{2,1,0:T(8,128)S(1)}, f32[4,64,128]{2,1,0:T(8,128)S(1)}, u32[]{:S(2)}, u32[]{:S(2)}) collective-permute-start(f32[4,64,128]{2,1,0:T(8,128)S(1)} %get-tuple-element.52.refs_8_.refs_7_), channel_id=1, source_target_pairs={{0,1},{1,2},{2,3},{3,4},{4,5},{5,6},{6,7},{7,8},{8,9},{9,10},{10,1... | collective-permute-start | bytes 393224 | tf_op jit(solution)/shard_map/ppermute | solution.py:458
  31.0 20.9 %all-to-all-start.1 = ((f32[16,64,128]{2,1,0:T(8,128)}), f32[16,64,128]{2,1,0:T(8,128)S(1)}, u32[]{:S(2)}, u32[]{:S(2)}) async-start(f32[16,64,128]{2,1,0:T(8,128)} %get-tuple-element.40), calls=%async_computation.1 | async-start | bytes 1048576 | tf_op jit(solution)/shard_map/all_to_all | solution.py:462
  37.8 14.0 %collective-permute-start.2 = (f32[4,64,128]{2,1,0:T(8,128)S(1)}, f32[4,64,128]{2,1,0:T(8,128)S(1)}, u32[]{:S(2)}, u32[]{:S(2)}) collective-permute-start(f32[4,64,128]{2,1,0:T(8,128)S(1)} %get-tuple-element.43.refs_10_), channel_id=1, source_target_pairs={{0,1},{1,2},{2,3},{3,4},{4,5},{5,6},{6,7},{7,8},{8,9},{9,10},{10,1... | collective-permute-start | bytes 393224 | tf_op jit(solution)/shard_map/ppermute | solution.py:458
  38.3 13.5 %collective-permute-start.3 = (f32[4,64,128]{2,1,0:T(8,128)S(1)}, f32[4,64,128]{2,1,0:T(8,128)S(1)}, u32[]{:S(2)}, u32[]{:S(2)}) collective-permute-start(f32[4,64,128]{2,1,0:T(8,128)S(1)} %get-tuple-element.44.refs_9_), channel_id=1, source_target_pairs={{1,0},{2,1},{3,2},{4,3},{5,4},{6,5},{7,6},{8,7},{9,8},{10,9},{11,1... | collective-permute-start | bytes 393224 | tf_op jit(solution)/shard_map/ppermute | solution.py:458

commit v3 on v2

--- a/solution.py
+++ b/solution.py
@@ -10,7 +10,7 @@
 F32 = jnp.float32
 BF16 = jnp.bfloat16
 MIB = 1024 * 1024
-BLOCK = 1024
+GROUP = 32
 
 
 def split(x):
@@ -99,48 +99,45 @@
     return jnp.concatenate([jnp.concatenate([hi, hi], axis=1), jnp.concatenate([lo, jnp.zeros_like(lo)], axis=1)], axis=0)
 
 
-def mix_levels(kron_ref, tracers_ref, scale_ref, out_ref, first, last):
+def mix(kron_ref, tracers_ref, out_ref, at):
     tracers, _, columns = tracers_ref.shape
     size = 8 * tracers
-
-    def block(i, _):
-        at = pl.ds(pl.multiple_of(i * BLOCK, BLOCK), BLOCK)
-        for k in range(first, last, 8):
-            hi, lo = split(tracers_ref[:, k : k + 8, at].reshape(size, BLOCK))
-            both = mxu(kron_ref[...], jnp.concatenate([hi, lo], axis=0))
-            mixed = both[:size] + both[size:]
-            out_ref[:, k : k + 8, at] = mixed.reshape(tracers, 8, BLOCK) * scale_ref[k : k + 8, at][None]
+    for k in range(at.start, at.stop, 8):
+        hi, lo = split(tracers_ref[:, k : k + 8, :].reshape(size, columns))
+        both = mxu(kron_ref[...], jnp.concatenate([hi, lo], axis=0))
+        out_ref[:, k : k + 8, :] = (both[:size] + both[size:]).reshape(tracers, 8, columns)
+
+
+def react_and_sink(species, mixed, growth, below, wet, rates_ref, after):
+    tracers, _, columns = species.shape
+
+    def one(n, _):
+        fraction = rates_ref[n, 0:1, :]
+        for c in range(0, columns, 128):
+            col = slice(c, c + 128)
+            amounts = sink(species[n, :, col] + growth[:, col] * mixed[n, :, col], fraction * below[:, col])
+            species[n, :, col] = amounts if wet is None else amounts * wet[:, col]
         return 0
 
-    lax.fori_loop(0, columns // BLOCK, block, 0)
-
-
-def sink_all(species_ref, warm_ref, react_ref, depth_ref, settling_ref, wet, below, out_ref, before, after):
-    tracers, levels, columns = species_ref.shape
-    level = iota((levels, columns), 0).astype(F32)
-    depth = depth_ref[0:1, :]
-    wet[...] = jnp.where(level < depth, 1.0, 0.0)
-    below[...] = jnp.where(level + 1.0 < depth, 1.0, 0.0)
-
-    def one(n, _):
-        before(n)
-        fraction = settling_ref[n]
-        for c in range(0, columns, 128):
-            at = slice(c, c + 128)
-            amounts = species_ref[n, :, at] + warm_ref[:, at] * react_ref[n, :, at]
-            out_ref[n, :, at] = sink(amounts, fraction * below[:, at]) * wet[:, at]
-        after(n)
-        return 0
-
-    lax.fori_loop(0, tracers, one, 0)
+    for i, (first, last) in enumerate(groups(tracers)):
+        lax.fori_loop(first, last, one, 0)
+        after(i)
+
+
+def groups(tracers):
+    cuts = [0, tracers * 3 // 8, tracers * 11 // 16, tracers * 7 // 8, tracers]
+    return list(zip(cuts[:-1], cuts[1:]))
 
 
 def place_columns(order, onehot, cpair):
     lons, lats = order.shape
-    target = iota((lats, lons * lats), 1)
     across = buckets(order, cpair).astype(F32).T.astype(jnp.int32)
+    lane = iota((lats, 128), 1)
+    one, zero = jnp.ones((lats, 128), BF16), jnp.zeros((lats, 128), BF16)
     for r in range(lons):
-        onehot[r * lats : (r + 1) * lats, :] = jnp.where(target == across[:, r : r + 1], 1.0, 0.0).astype(BF16)
+        own = (jnp.broadcast_to(across[:, r : r + 1], (lats, 128)) - lane).astype(jnp.int16)
+        for e in range(0, lons * lats, 128):
+            onehot[r * lats : (r + 1) * lats, e : e + 128] = jnp.where(own == jnp.int16(e), one, zero)
 
 
 def buckets(order, cpair):
@@ -187,23 +184,19 @@
     send_temp.wait()
 
 
-def react_kernel(species_hbm, scale_ref, coupling_ref, react_hbm, first_ref, kron_ref, species, react, sems, out_sems):
+def react_kernel(species_hbm, scale_ref, coupling_ref, first_ref, species, sems):
     tracers, levels, columns = species.shape
-    span = 256 // tracers
-    parts = [slice(k, k + span) for k in range(0, levels, span)]
-    copies = [pltpu.make_async_copy(species_hbm.at[:, at], species.at[:, at], sems.at[i]) for i, at in enumerate(parts)]
-    sends = [pltpu.make_async_copy(react.at[:, at], react_hbm.at[:, at], out_sems.at[i]) for i, at in enumerate(parts)]
+    copies = [pltpu.make_async_copy(species_hbm.at[n], species.at[n], sems.at[n]) for n in range(tracers)]
     for copy in copies:
         copy.start()
-    kron_ref[...] = split_kron(coupling_ref[...])
-    for copy, send, at in zip(copies, sends, parts):
+    for n, copy in enumerate(copies):
         copy.wait()
-        mix_levels(kron_ref, species, scale_ref, react, at.start, at.stop)
-        send.start()
+        for c in range(0, columns, 128):
+            col = slice(c, c + 128)
+            term = coupling_ref[0, n] * species[n, :, col]
+            first_ref[1, :, col] = first_ref[1, :, col] + term if n else term
     first_ref[0] = species[0]
-    first_ref[1] = react[0]
-    for send in sends:
-        send.wait()
+    first_ref[1] = scale_ref[...] * first_ref[1]
 
 
 def tile_levels(fields, depth_ref, fcor_ref, outs):
@@ -277,9 +270,9 @@
     save.wait()
 
 
-def chloro_kernel(cpair, recv_ref, settling_ref, first_ref, sent_ref, edge_ref, left_ref, right_ref, first_lon_ref, last_lon_ref, wet_ref,
-                  pay_hbm, warm_ref, depth_ref, scale_ref, pay, sems):
-    levels, columns = warm_ref.shape
+def chloro_kernel(cpair, recv_ref, rates_ref, first_ref, sent_ref, edge_ref, left_ref, right_ref, first_lon_ref, last_lon_ref, wet_ref,
+                  pay_hbm, light_hbm, depth_ref, pay, light_ref, sems):
+    _, levels, columns = light_ref.shape
     lons, lats = wet_ref.shape
     rows = levels * cpair // 128
     groups = 128 // cpair
@@ -293,13 +286,13 @@
             out = piece if out is None else jnp.where(lane_group == o, piece, out)
         depth_ref[:, e * 128 : (e + 1) * 128] = out
     warm = jnp.exp(0.15 * unpack(recv_ref, rows, rows, cpair, 0, columns // 128))
-    warm_ref[...] = warm
+    light_ref[0] = warm
     level = iota((levels, columns), 0).astype(F32)
     depth = depth_ref[0:1, :]
     amounts = first_ref[0] + warm * first_ref[1]
-    amounts = sink(amounts, jnp.where(level + 1.0 < depth, settling_ref[0], 0.0))
+    amounts = sink(amounts, jnp.where(level + 1.0 < depth, rates_ref[0, 0:1, 0:1], 0.0))
     trans, heat = light(jnp.where(level < depth, amounts, 0.0))
-    scale_ref[...] = 0.2 * trans
+    light_ref[1] = 0.2 * trans
     pack(pay, rows, heat, cpair)
     send_heat = pltpu.make_async_copy(pay.at[:, rows : 2 * rows], pay_hbm.at[:, rows : 2 * rows], sems.at[0])
     send_heat.start()
@@ -311,124 +304,113 @@
     pack(pay, 0, sent_ref[...] + (extra[:levels] + extra[levels:]), cpair)
     send_x = pltpu.make_async_copy(pay.at[:, 0:rows], pay_hbm.at[:, 0:rows], sems.at[1])
     send_x.start()
+    save = pltpu.make_async_copy(light_ref, light_hbm, sems.at[2])
+    save.start()
     send_heat.wait()
     send_x.wait()
+    save.wait()
 
 
 def back_columns(order, onehot, cpair):
     lons, lats = order.shape
     bucket = buckets(order, cpair)
-    source = iota((lons * lats, lats), 0)
+    row = iota((16, lats), 0)
+    one, zero = jnp.ones((16, lats), BF16), jnp.zeros((16, lats), BF16)
     for r in range(lons):
-        onehot[:, r * lats : (r + 1) * lats] = jnp.where(source == bucket[r : r + 1], 1.0, 0.0).astype(BF16)
-
-
-def finish_tile(cpair, recv_ref, row, back_ref, depth_ref, left_ref, right_ref, first_lon_ref, last_lon_ref, fields, out):
-    _, levels, lons, lats = out.shape
-    ctile = lons * lats
-    heat = unpack(recv_ref, row, levels * cpair // 128, cpair, 0, ctile // 128)
+        own = (jnp.broadcast_to(bucket[r : r + 1], (16, lats)) - row).astype(jnp.int16)
+        for b in range(0, lons * lats, 16):
+            onehot[b : b + 16, r * lats : (r + 1) * lats] = jnp.where(own == jnp.int16(b), one, zero)
+
+
+def place_heat(cpair, recv_ref, row, back_ref, depth_ref, levels):
+    lons, lats = depth_ref.shape
+    heat = unpack(recv_ref, row, levels * cpair // 128, cpair, 0, lons * lats // 128)
     placed = mxu(jnp.concatenate(split(heat), axis=0), back_ref[...])
     placed = 0.2 * (placed[:levels] + placed[levels:])
-    for n in (0, 1, 3):
-        out[n] = fields[n]
     level = iota((levels, lats), 0)
-    for r in range(lons):
-        part = placed[:, r * lats : (r + 1) * lats]
-        out[2, :, r, :] = fields[2, :, r, :] + jnp.where(level < depth_ref[r : r + 1, :], part, 0.0)
+    return [jnp.where(level < depth_ref[r : r + 1, :], placed[:, r * lats : (r + 1) * lats], 0.0) for r in range(lons)]
+
+
+def add_edges(depth_ref, left_ref, right_ref, first_lon_ref, last_lon_ref, out):
+    lons = depth_ref.shape[0]
     for halo, own, lon, sign in ((left_ref, first_lon_ref, 0, 1.0), (right_ref, last_lon_ref, lons - 1, -1.0)):
         for n, term in enumerate(edge_terms(halo, own[0], depth_ref[lon : lon + 1, :], sign)):
             out[n, :, lon, :] = out[n, :, lon, :] + term
 
 
 def heat_kernel(cpair, fields_hbm, recv_ref, order_ref, depth_ref, left_ref, right_ref, first_lon_ref, last_lon_ref,
-                out_ref, left_edge_ref, right_edge_ref, fields, back, sem):
-    fetch = pltpu.make_async_copy(fields_hbm, fields, sem.at[0])
+                out_ref, left_edge_ref, right_edge_ref, back, sems):
+    lons, lats = order_ref.shape
+    fetch = pltpu.make_async_copy(fields_hbm, out_ref, sems.at[0])
     fetch.start()
-    lons = order_ref.shape[0]
     back_columns(order_ref[...], back, cpair)
+    parts = place_heat(cpair, recv_ref, 0, back, depth_ref, out_ref.shape[1])
     fetch.wait()
-    finish_tile(cpair, recv_ref, 0, back, depth_ref, left_ref, right_ref, first_lon_ref, last_lon_ref, fields, out_ref)
+    add_edges(depth_ref, left_ref, right_ref, first_lon_ref, last_lon_ref, out_ref)
+    for r in range(lons):
+        out_ref[2, :, r, :] = out_ref[2, :, r, :] + parts[r]
     for n in range(4):
         left_edge_ref[n] = out_ref[n, :, 0, :]
         right_edge_ref[n] = out_ref[n, :, lons - 1, :]
 
 
-def tracer_kernel(species_hbm, react_hbm, warm_ref, scale_ref, depth_ref, kron_ref, settling_ref, out_hbm, next_hbm,
-                  species, react, heat, wet, below, in_sems, out_sems, next_sems):
+def tracer_copies(species_hbm, species, out_hbm, in_sems, out_sems):
+    ats = [slice(k, k + GROUP) for k in range(0, species.shape[1], GROUP)]
+    copies = [pltpu.make_async_copy(species_hbm.at[:, at], species.at[:, at], in_sems.at[i]) for i, at in enumerate(ats)]
+    parts = [slice(first, last) for first, last in groups(species.shape[0])]
+    sends = [pltpu.make_async_copy(species.at[part], out_hbm.at[part], out_sems.at[i]) for i, part in enumerate(parts)]
+    return ats, copies, sends
+
+
+def tracer_kernel(species_hbm, light_hbm, depth_ref, coupling_ref, rates_ref, fields_ref, wet_ref, fcor_ref,
+                  out_hbm, growth_ref, kron_ref, next_fields_ref, species, mixed, light_ref, below, wet, in_sems, out_sems):
     tracers, levels, columns = species.shape
-    span = 256 // tracers
-
-    def fetch(n):
-        return (
-            pltpu.make_async_copy(species_hbm.at[n], species.at[n], in_sems.at[2 * n]),
-            pltpu.make_async_copy(react_hbm.at[n], react.at[n], in_sems.at[2 * n + 1]),
-        )
-
-    def save(n):
-        return pltpu.make_async_copy(species.at[n], out_hbm.at[n], out_sems.at[n])
-
-    for n in range(tracers):
-        for copy in fetch(n):
-            copy.start()
-
-    def before(n):
-        for copy in fetch(n):
-            copy.wait()
-
-        @pl.when(n == 0)
-        def _():
-            heat[...] = light(species[0])[1]
-
-    sink_all(species, warm_ref, react, depth_ref, settling_ref, wet, below, species, before, lambda n: save(n).start())
-    below[...] = scale_ref[...] * jnp.exp(0.03 * (wet[...] * heat[...]))
-    parts = [slice(k, k + span) for k in range(0, levels, span)]
-    sends = [pltpu.make_async_copy(react.at[:, at], next_hbm.at[:, at], next_sems.at[i]) for i, at in enumerate(parts)]
-    for send, at in zip(sends, parts):
-        mix_levels(kron_ref, species, below, react, at.start, at.stop)
-        send.start()
-    for n in range(tracers):
-        save(n).wait()
+    ats, copies, sends = tracer_copies(species_hbm, species, out_hbm, in_sems, out_sems)
+    fetch_light = pltpu.make_async_copy(light_hbm, light_ref, in_sems.at[len(ats)])
+    fetch_light.start()
+    for copy in copies:
+        copy.start()
+    kron_ref[...] = split_kron(coupling_ref[...])
+    level = iota((levels, columns), 0).astype(F32)
+    depth = depth_ref[0:1, :]
+    below[...] = jnp.where(level + 1.0 < depth, 1.0, 0.0)
+    wet[...] = jnp.where(level < depth, 1.0, 0.0)
+    tile_levels([fields_ref.at[n] for n in range(4)], wet_ref, fcor_ref, [next_fields_ref.at[n] for n in range(4)])
+    fetch_light.wait()
+    for copy, at in zip(copies, ats):
+        copy.wait()
+        mix(kron_ref, species, mixed, at)
+    trans, heat = light(species[0])
+    light_ref[0] = 0.2 * trans * light_ref[0]
+    growth_ref[...] = wet[...] * (light_ref[1] * jnp.exp(0.03 * (wet[...] * heat)))
+    react_and_sink(species, mixed, light_ref.at[0], below, wet, rates_ref, lambda i: sends[i].start())
     for send in sends:
         send.wait()
 
 
-def second_tile_kernel(fields, depth_ref, fcor_ref, out):
-    tile_levels([fields.at[n] for n in range(4)], depth_ref, fcor_ref, [out.at[n] for n in range(4)])
-
-
-def final_kernel(cpair, species_hbm, react_hbm, depth_ref, settling_ref, recv_ref, order_ref, wet_ref, left_ref, right_ref, first_lon_ref, last_lon_ref,
-                 fields, out_hbm, *rest):
-    field_hbms, (species, react, back, tile, warm, wet, below, in_sems, out_sems, sems) = rest[:4], rest[4:]
+def final_kernel(cpair, species_hbm, growth_ref, depth_ref, kron_ref, rates_ref, recv_ref, order_ref, wet_ref, left_ref, right_ref,
+                 first_lon_ref, last_lon_ref, fields, out_hbm, *rest):
+    field_hbms, (species, mixed, back, tile, growth, below, in_sems, out_sems, sems) = rest[:4], rest[4:]
     tracers, levels, columns = species.shape
     rows = levels * cpair // 128
-
-    def fetch(n):
-        return (
-            pltpu.make_async_copy(species_hbm.at[n], species.at[n], in_sems.at[2 * n]),
-            pltpu.make_async_copy(react_hbm.at[n], react.at[n], in_sems.at[2 * n + 1]),
-        )
-
-    def send(n):
-        return pltpu.make_async_copy(species.at[n], out_hbm.at[n], out_sems.at[n])
-
-    for n in range(tracers):
-        for copy in fetch(n):
-            copy.start()
-
-    def before(n):
-        for copy in fetch(n):
-            copy.wait()
-
+    ats, copies, sends = tracer_copies(species_hbm, species, out_hbm, in_sems, out_sems)
+    for copy in copies:
+        copy.start()
+    tile[...] = fields[...]
+    add_edges(wet_ref, left_ref, right_ref, first_lon_ref, last_lon_ref, tile)
+    field_sends = [pltpu.make_async_copy(tile.at[n], field_hbms[n], sems.at[n]) for n in range(4)]
+    below[...] = jnp.where(iota((levels, columns), 0).astype(F32) + 1.0 < depth_ref[0:1, :], 1.0, 0.0)
+    growth[...] = growth_ref[...] * jnp.exp(0.15 * unpack(recv_ref, 0, rows, cpair, 0, columns // 128))
     back_columns(order_ref[...], back, cpair)
-    finish_tile(cpair, recv_ref, rows, back, wet_ref, left_ref, right_ref, first_lon_ref, last_lon_ref, fields, tile)
-    sends = [pltpu.make_async_copy(tile.at[n], field_hbms[n], sems.at[n]) for n in range(4)]
-    for copy in sends:
+    for r, part in enumerate(place_heat(cpair, recv_ref, rows, back, wet_ref, levels)):
+        tile[2, :, r, :] = tile[2, :, r, :] + part
+    for copy, at in zip(copies, ats):
+        copy.wait()
+        mix(kron_ref, species, mixed, at)
+    for copy in field_sends:
         copy.start()
-    warm[...] = jnp.exp(0.15 * unpack(recv_ref, 0, rows, cpair, 0, columns // 128))
-    sink_all(species, warm, react, depth_ref, settling_ref, wet, below, species, before, lambda n: send(n).start())
-    for n in range(tracers):
-        send(n).wait()
-    for copy in sends:
+    react_and_sink(species, mixed, growth, below, None, rates_ref, lambda i: sends[i].start())
+    for copy in sends + field_sends:
         copy.wait()
 
 
@@ -472,6 +454,7 @@
     column = jax.ShapeDtypeStruct((levels, ctile), F32)
     patch = pltpu.HBM((tracers, levels, ctile), F32)
     fcor = (0.8 * jnp.sin(jnp.pi * (jnp.arange(lats, dtype=F32) + 0.5) / lats - jnp.pi / 2))[None]
+    rates = jnp.broadcast_to(settling[:, None, None], (tracers, 8, 128))
     sem = pltpu.SemaphoreType.DMA
     mix_flops = 6 * 256 * levels * tracers * ctile
     patch_scratch = pltpu.VMEM((tracers, levels, ctile), F32)
@@ -503,15 +486,14 @@
     stacked = jnp.stack([u, v, temp, salt])
     edges = stacked[:, :, 0], stacked[:, :, lons - 1]
     left, right = halo(*edges)
-    groups = levels * tracers // 256
-    react1, first, kron = pl.pallas_call(
+    first = pl.pallas_call(
         react_kernel,
-        out_shape=[patch, jax.ShapeDtypeStruct((2, levels, ctile), F32), jax.ShapeDtypeStruct((16 * tracers, 16 * tracers), BF16)],
-        in_specs=[ANY] + whole(2),
-        out_specs=[ANY] + whole(2),
-        scratch_shapes=[patch_scratch, patch_scratch, sem((groups,)), sem((groups,))],
-        compiler_params=params(16),
-        cost_estimate=cost(mix_flops, 8 * MIB),
+        out_shape=jax.ShapeDtypeStruct((2, levels, ctile), F32),
+        in_specs=[ANY] + whole(1) + [SMEM],
+        out_specs=whole(1)[0],
+        scratch_shapes=[patch_scratch, sem((tracers,))],
+        compiler_params=params(12),
+        cost_estimate=cost(2 * levels * tracers * ctile, 4 * MIB),
         name="react",
     )(in_hbm(species), scale1, coupling)
     fields1, sent, edge_place = pl.pallas_call(
@@ -525,15 +507,15 @@
         name="tile_one",
     )(u, v, temp, salt, wet_layers, fcor, order)
 
-    pay, warm, depth, scale2 = pl.pallas_call(
+    pay, light2, depth = pl.pallas_call(
         lambda *refs: chloro_kernel(cpair, *refs),
-        out_shape=[pltpu.HBM((tiles, 2 * rows, 128), F32), column, jax.ShapeDtypeStruct((8, ctile), F32), column],
-        in_specs=[*whole(1), SMEM, *whole(8)],
-        out_specs=[ANY, *whole(3)],
-        scratch_shapes=[pltpu.VMEM((tiles, 2 * rows, 128), F32), sem((2,))],
+        out_shape=[pltpu.HBM((tiles, 2 * rows, 128), F32), pltpu.HBM((2, levels, ctile), F32), jax.ShapeDtypeStruct((8, ctile), F32)],
+        in_specs=whole(10),
+        out_specs=[ANY, ANY, *whole(1)],
+        scratch_shapes=[pltpu.VMEM((tiles, 2 * rows, 128), F32), pltpu.VMEM((2, levels, ctile), F32), sem((3,))],
         compiler_params=params(8),
         name="chloro",
-    )(recv_a, settling, first, sent, edge_place, left, right, *edges, wet_layers)
+    )(recv_a, rates, first, sent, edge_place, left, right, *edges, wet_layers)
     recv_b = exchange(pay)
 
     recv_a, _ = lax.optimization_barrier((recv_a, pay))
@@ -542,36 +524,41 @@
         out_shape=[jax.ShapeDtypeStruct((4, levels, lons, lats), F32), edge, edge],
         in_specs=[ANY] + whole(7),
         out_specs=whole(3),
-        scratch_shapes=[fields_scratch, onehot_scratch, sem((1,))],
+        scratch_shapes=[onehot_scratch, sem((1,))],
         compiler_params=params(12),
         cost_estimate=cost(4 * levels * ctile * ctile, 4 * MIB),
         name="heat",
     )(in_hbm(fields1), recv_a, order, wet_layers, left, right, *edges)
     left, right = halo(*edges)
-    species1, react2 = pl.pallas_call(
+    steps = levels // GROUP
+    species1, growth, kron, fields2 = pl.pallas_call(
         tracer_kernel,
-        out_shape=[patch, patch],
-        in_specs=[ANY] * 2 + whole(4) + [SMEM],
-        out_specs=[ANY] * 2,
-        scratch_shapes=[patch_scratch] * 2 + [column_scratch] * 3 + [sem((2 * tracers,)), sem((tracers,)), sem((groups,))],
+        out_shape=[
+            patch,
+            column,
+            jax.ShapeDtypeStruct((16 * tracers, 16 * tracers), BF16),
+            jax.ShapeDtypeStruct((4, levels, lons, lats), F32),
+        ],
+        in_specs=[ANY] * 2 + whole(6),
+        out_specs=[ANY] + whole(3),
+        scratch_shapes=[
+            patch_scratch,
+            patch_scratch,
+            pltpu.VMEM((2, levels, ctile), F32),
+            column_scratch,
+            column_scratch,
+            sem((steps + 1,)),
+            sem((len(groups(tracers)),)),
+        ],
         compiler_params=params(16),
-        cost_estimate=cost(mix_flops, 16 * MIB),
+        cost_estimate=cost(mix_flops, 8 * MIB),
         name="tracer",
-    )(in_hbm(species), in_hbm(react1), warm, scale2, depth, kron, settling)
-    fields2 = pl.pallas_call(
-        second_tile_kernel,
-        out_shape=jax.ShapeDtypeStruct((4, levels, lons, lats), F32),
-        in_specs=whole(3),
-        out_specs=whole(1)[0],
-        compiler_params=params(8),
-        cost_estimate=cost(60 * levels * ctile, 2 * MIB),
-        name="tile_two",
-    )(fields1, wet_layers, fcor)
+    )(in_hbm(species), in_hbm(light2), depth, coupling, rates, fields1, wet_layers, fcor)
 
     species2, u2, v2, t2, s2 = pl.pallas_call(
         lambda *refs: final_kernel(cpair, *refs),
         out_shape=[patch] + [pltpu.HBM((levels, lons, lats), F32)] * 4,
-        in_specs=[ANY] * 2 + whole(1) + [SMEM] + whole(8),
+        in_specs=[ANY] + whole(12),
         out_specs=[ANY] * 5,
         scratch_shapes=[
             patch_scratch,
@@ -580,14 +567,13 @@
             fields_scratch,
             column_scratch,
             column_scratch,
-            column_scratch,
-            sem((2 * tracers,)),
-            sem((tracers,)),
+            sem((steps,)),
+            sem((len(groups(tracers)),)),
             sem((4,)),
         ],
         compiler_params=params(20),
         name="final",
-    )(in_hbm(species1), in_hbm(react2), depth, settling, recv_b, order, wet_layers, left, right, *edges, fields2)
+    )(in_hbm(species1), growth, depth, kron, rates, recv_b, order, wet_layers, left, right, *edges, fields2)
     return u2, v2, t2, s2, species2
 
 

time: 59.9 us -> 58.2 us (0.972)
  Pallas kernels: 32 us -> 26.8 us
  waiting for transfers between devices: 5.21 us -> 8.74 us
    pallas_call x3 -> x2, Pallas kernels: 13.4 us -> 9.43 us  [the longest x1 6.41 us: body(): pl.pallas_call(tracer_kernel, out_shape=[patch, column, jax.ShapeDtypeStr...]
    ppermute x2, waiting for transfers between devices: 4.98 us -> 7.54 us  [halo(): lax.ppermute(right_edge, AXES, ahead)]
    ppermute x2, waiting for transfers between devices: 0.23 us -> 1.19 us  [halo(): lax.ppermute(left_edge, AXES, [(b, a) for a, b in ahead])]
    pallas_call x1, Pallas kernels: 7.53 us -> 6.8 us  [body(): pl.pallas_call(lambda *refs: final_kernel(cpair, *refs), out_shape=[patch...]
  transfers between devices with their start and end apart: 6 -> 6, of which waited for: 2 -> 3; matrix products, arithmetic and copies ran while one was open for 0% -> 0% of each run, Pallas kernels for 31% -> 25%
where the time goes in v3:
time: 58.2 us; the launch traced here: 57.8 us
  Pallas kernels  26.8 us (46%)
  starting transfers between devices  20.9 us (36%)
  waiting for transfers between devices  8.74 us (15%)
  between operations  1 us (2%)
    all_to_all x2, starting transfers between devices, exchange(): return lax.all_to_all(pay, AXES, split_axis=0, concat_axis=0, tiled=True)  11.8 us
    ppermute x2, starting transfers between devices, halo(): lax.ppermute(left_edge, AXES, [(b, a) for a, b in ahead])  8.65 us
    ppermute x2, waiting for transfers between devices, halo(): lax.ppermute(right_edge, AXES, ahead)  7.54 us
    pallas_call x1, Pallas kernels, body(): pl.pallas_call(lambda *refs: final_kernel(cpair, *refs), out_shape=[patch...  6.8 us
    pallas_call x1, Pallas kernels, body(): pl.pallas_call(tracer_kernel, out_shape=[patch, column, jax.ShapeDtypeStr...  6.41 us
    pallas_call x1, Pallas kernels, body(): pl.pallas_call(lambda *refs: start_kernel(cpair, *refs), out_shape=[pltpu...  3.73 us
    pallas_call x1, Pallas kernels, body(): pl.pallas_call(react_kernel, out_shape=jax.ShapeDtypeStruct((2, levels, c...  3.02 us
    pallas_call x1, Pallas kernels, body(): pl.pallas_call(lambda *refs: first_tile_kernel(cpair, *refs), out_shape=[...  2.91 us
  transfers between devices with their start and end apart: 6, of which 3 were waited for; matrix products, arithmetic and copies ran while one was open for 0% of the time, Pallas kernels for 25%

profile of v3, /device:TPU:0, one launch (start us, length us, event | category | flops | bytes accessed | tf_op | source)
XLA Modules:
  0.0 57.8 jit_solution(10554300411192821443)
XLA Ops:
  0.6 0.0 copy-start
  0.6 0.0 copy-start.1
  0.7 0.0 copy-start.3
  0.7 0.0 copy-start.2
  0.7 0.0 copy-start.6
  0.7 3.7 %start.1 = (f32[16,72,128]{2,1,0:T(8,128)}, f32[64,1024]{1,0:T(8,128)S(1)}) custom-call(s32[8,128]{1,0:T(8,128)} %refs_6_.3, s32[8,128]{1,0:T(8,128)} %refs_7_.1, f32[64,8,128]{2,1,0:T(8,128)} %refs_2_.4, f32[16,64,1024]{2,1,0:T(8,128)} %species_hbm.3), custom_call_target="tpu_custom_call" | custom-call | tf_op jit(solution)/shard_map/start/pallas_call | solution.py:466
  4.4 7.4 %all-to-all-start = ((f32[16,72,128]{2,1,0:T(8,128)}), f32[16,72,128]{2,1,0:T(8,128)S(1)}, u32[]{:S(2)}, u32[]{:S(2)}) async-start(f32[16,72,128]{2,1,0:T(8,128)} %get-tuple-element.26), calls=%async_computation | async-start | bytes 1179648 | tf_op jit(solution)/shard_map/all_to_all | solution.py:444
  11.8 0.0 copy-done
  11.8 0.0 copy-start.4
  11.9 0.0 copy-start.5
  11.9 0.1 copy.22
  11.9 0.0 copy-done.1
  11.9 0.1 copy.23
  12.0 0.0 copy-done.3
  12.0 0.0 copy-done.2
  12.0 0.0 copy-start.7
  12.0 0.1 copy_bitcast_fusion
  12.2 4.4 %collective-permute-start.1 = (f32[4,64,128]{2,1,0:T(8,128)S(1)}, f32[4,64,128]{2,1,0:T(8,128)S(1)}, u32[]{:S(2)}, u32[]{:S(2)}) collective-permute-start(f32[4,64,128]{2,1,0:T(8,128)S(1)} %get-tuple-element.47.refs_7_.refs_6_), channel_id=1, source_target_pairs={{1,0},{2,1},{3,2},{4,3},{5,4},{6,5},{7,6},{8,7},{9,8},{10,9},{11,1... | collective-permute-start | bytes 393224 | tf_op jit(solution)/shard_map/ppermute | solution.py:440
  16.6 0.0 collective-permute-start
  16.6 0.0 copy-done.6
  16.6 3.0 %react.1.refs_2_ = f32[2,64,1024]{2,1,0:T(8,128)S(1)} custom-call(f32[16,64,1024]{2,1,0:T(8,128)} %species_hbm.3, f32[64,1024]{1,0:T(8,128)S(1)} %get-tuple-element.27.scale_ref, f32[16,16]{1,0:T(8,128)S(1)} %copy-done.6), custom_call_target="tpu_custom_call" | custom-call | flops 2097152 | bytes 4194304 | tf_op jit(solution)/shard_map/react/pallas_call | solution.py:489
  19.6 0.1 sine_multiply_fusion.refs_5_.fcor_ref
  19.7 0.0 copy-done.4
  19.7 0.0 copy-done.5
  19.7 2.9 %tile_one.1 = (f32[4,64,8,128]{3,2,1,0:T(8,128)}, f32[64,1024]{1,0:T(8,128)S(1)}, bf16[256,1024]{1,0:T(8,128)(2,1)S(1)}) custom-call(f32[64,8,128]{2,1,0:T(8,128)S(1)} %copy-done.1, f32[64,8,128]{2,1,0:T(8,128)S(1)} %copy-done.2, f32[64,8,128]{2,1,0:T(8,128)S(1)} %copy-done, f32[64,8,128]{2,1,0:T(8,128)S(1)} %copy-done.3, s32[8,128]{1,0:T(8,128)S(1)} %copy-done.4, ...), custom_call_target="tpu_custom_call" | custom-call | flops 268435456 | bytes 2097152 | tf_op jit(solution)/shard_map/tile_one/pallas_call | solution.py:499
  22.6 1.2 %collective-permute-done.1.refs_6_.refs_5_ = f32[4,64,128]{2,1,0:T(8,128)S(1)} collective-permute-done((f32[4,64,128]{2,1,0:T(8,128)S(1)}, f32[4,64,128]{2,1,0:T(8,128)S(1)}, u32[]{:S(2)}, u32[]{:S(2)}) %collective-permute-start.1) | collective-permute-done | bytes 131104 | tf_op jit(solution)/shard_map/ppermute | solution.py:440
  23.8 5.0 %collective-permute-done.refs_5_.refs_4_ = f32[4,64,128]{2,1,0:T(8,128)S(1)} collective-permute-done((f32[4,64,128]{2,1,0:T(8,128)S(1)}, f32[4,64,128]{2,1,0:T(8,128)S(1)}, u32[]{:S(2)}, u32[]{:S(2)}) %collective-permute-start) | collective-permute-done | bytes 131104 | tf_op jit(solution)/shard_map/ppermute | solution.py:440
  28.8 0.0 all-to-all-done.refs_0_.refs_1_
  28.8 0.0 copy-done.7
  28.8 0.1 broadcast_in_dim.2.refs_1_.rates_ref.refs_4_
  28.9 1.7 %chloro.1 = (f32[16,64,128]{2,1,0:T(8,128)}, f32[2,64,1024]{2,1,0:T(8,128)}, f32[8,1024]{1,0:T(8,128)S(1)}) custom-call(f32[16,72,128]{2,1,0:T(8,128)S(1)} %all-to-all-done.refs_0_.refs_1_, f32[16,8,128]{2,1,0:T(8,128)S(1)} %broadcast_in_dim.2.refs_1_.rates_ref.refs_4_, f32[2,64,1024]{2,1,0:T(8,128)S(1)} %react.1.refs_2_, ...), custom_call_target="tpu_custom_call" | custom-call | tf_op jit(solution)/shard_map/chloro/pallas_call | solution.py:510
  30.6 4.4 %all-to-all-start.1 = ((f32[16,64,128]{2,1,0:T(8,128)}), f32[16,64,128]{2,1,0:T(8,128)S(1)}, u32[]{:S(2)}, u32[]{:S(2)}) async-start(f32[16,64,128]{2,1,0:T(8,128)} %get-tuple-element.33), calls=%async_computation.1 | async-start | bytes 1048576 | tf_op jit(solution)/shard_map/all_to_all | solution.py:444
  35.0 2.2 %heat.1 = (f32[4,64,8,128]{3,2,1,0:T(8,128)S(1)}, f32[4,64,128]{2,1,0:T(8,128)S(1)}, f32[4,64,128]{2,1,0:T(8,128)S(1)}) custom-call(f32[4,64,8,128]{3,2,1,0:T(8,128)} %get-tuple-element.32.refs_0_, f32[16,72,128]{2,1,0:T(8,128)S(1)} %all-to-all-done.refs_0_.refs_1_, s32[8,128]{1,0:T(8,128)S(1)} %copy-done.5, s32[8,128]{1,0:T(8,128)S(1)} %copy-done.4, ...), custom_call_target="tpu_custom_call" | custom-call | flops 268435456 | bytes 4194304 | tf_op jit(solution)/shard_map/heat/pallas_call | solution.py:522
  37.2 0.5 collective-permute-start.2
  37.7 4.2 %collective-permute-start.3 = (f32[4,64,128]{2,1,0:T(8,128)S(1)}, f32[4,64,128]{2,1,0:T(8,128)S(1)}, u32[]{:S(2)}, u32[]{:S(2)}) collective-permute-start(f32[4,64,128]{2,1,0:T(8,128)S(1)} %get-tuple-element.40.refs_10_), channel_id=1, source_target_pairs={{1,0},{2,1},{3,2},{4,3},{5,4},{6,5},{7,6},{8,7},{9,8},{10,9},{11,1... | collective-permute-start | bytes 393224 | tf_op jit(solution)/shard_map/ppermute | solution.py:440
  41.9 6.4 %tracer.1 = (f32[16,64,1024]{2,1,0:T(8,128)}, f32[64,1024]{1,0:T(8,128)S(1)}, bf16[256,256]{1,0:T(8,128)(2,1)S(1)}, f32[4,64,8,128]{3,2,1,0:T(8,128)S(1)}) custom-call(f32[16,64,1024]{2,1,0:T(8,128)} %species_hbm.3, f32[2,64,1024]{2,1,0:T(8,128)} %get-tuple-element.30.light_hbm, f32[8,1024]{1,0:T(8,128)S(1)} %get-tuple-element.31.depth_ref.refs_2_, ...), custom_call_target="tpu_custom_call" | custom-call | flops 1610612736 | bytes 8388608 | tf_op jit(solution)/shard_map/tracer/pallas_call | solution.py:534
  48.3 2.6 %collective-permute-done.2.refs_8_ = f32[4,64,128]{2,1,0:T(8,128)S(1)} collective-permute-done((f32[4,64,128]{2,1,0:T(8,128)S(1)}, f32[4,64,128]{2,1,0:T(8,128)S(1)}, u32[]{:S(2)}, u32[]{:S(2)}) %collective-permute-start.2) | collective-permute-done | bytes 131104 | tf_op jit(solution)/shard_map/ppermute | solution.py:440
  50.9 0.0 collective-permute-done.3.refs_9_
  50.9 0.0 all-to-all-done.1.refs_5_
  50.9 6.8 %final.1 = (f32[16,64,1024]{2,1,0:T(8,128)}, f32[64,8,128]{2,1,0:T(8,128)}, f32[64,8,128]{2,1,0:T(8,128)}, f32[64,8,128]{2,1,0:T(8,128)}, f32[64,8,128]{2,1,0:T(8,128)}) custom-call(f32[16,64,1024]{2,1,0:T(8,128)} %get-tuple-element.36.refs_0_, f32[64,1024]{1,0:T(8,128)S(1)} %get-tuple-element.37.refs_1_, f32[8,1024]{1,0:T(8,128)S(1)} %get-tuple-element.31.depth_ref.refs_2_, ...), custom_call_target="tpu_custom_call" | custom-call | tf_op jit(solution)/shard_map/final/pallas_call | solution.py:558
  (1 shorter events, 0.0 us)
Async XLA Ops:
  0.6 11.2 %copy-start = (f32[64,8,128]{2,1,0:T(8,128)S(1)}, f32[64,8,128]{2,1,0:T(8,128)}, u32[]{:S(2)}) copy-start(f32[64,8,128]{2,1,0:T(8,128)} %refs_2_.4) | copy-start | bytes 786436
  0.6 11.3 %copy-start.1 = (f32[64,8,128]{2,1,0:T(8,128)S(1)}, f32[64,8,128]{2,1,0:T(8,128)}, u32[]{:S(2)}) copy-start(f32[64,8,128]{2,1,0:T(8,128)} %refs_0_.3) | copy-start | bytes 786436
  0.7 11.3 %copy-start.3 = (f32[64,8,128]{2,1,0:T(8,128)S(1)}, f32[64,8,128]{2,1,0:T(8,128)}, u32[]{:S(2)}) copy-start(f32[64,8,128]{2,1,0:T(8,128)} %refs_3_.4) | copy-start | bytes 786436
  0.7 11.3 %copy-start.2 = (f32[64,8,128]{2,1,0:T(8,128)S(1)}, f32[64,8,128]{2,1,0:T(8,128)}, u32[]{:S(2)}) copy-start(f32[64,8,128]{2,1,0:T(8,128)} %refs_1_.3) | copy-start | bytes 786436
  0.7 15.9 %copy-start.6 = (f32[16,16]{1,0:T(8,128)S(1)}, f32[16,16]{1,0:T(8,128)}, u32[]{:S(2)}) copy-start(f32[16,16]{1,0:T(8,128)} %coupling_ref.3) | copy-start | bytes 3076
  4.4 24.4 %all-to-all-start = ((f32[16,72,128]{2,1,0:T(8,128)}), f32[16,72,128]{2,1,0:T(8,128)S(1)}, u32[]{:S(2)}, u32[]{:S(2)}) async-start(f32[16,72,128]{2,1,0:T(8,128)} %get-tuple-element.26), calls=%async_computation | async-start | bytes 1179648 | tf_op jit(solution)/shard_map/all_to_all | solution.py:444
  11.8 7.8 %copy-start.4 = (s32[8,128]{1,0:T(8,128)S(1)}, s32[8,128]{1,0:T(8,128)}, u32[]{:S(2)}) copy-start(s32[8,128]{1,0:T(8,128)} %refs_7_.1) | copy-start | bytes 12292
  11.9 7.8 %copy-start.5 = (s32[8,128]{1,0:T(8,128)S(1)}, s32[8,128]{1,0:T(8,128)}, u32[]{:S(2)}) copy-start(s32[8,128]{1,0:T(8,128)} %refs_6_.3) | copy-start | bytes 12292
  12.0 16.8 %copy-start.7 = (f32[16]{0:T(128)S(1)}, f32[16]{0:T(128)}, u32[]{:S(2)}) copy-start(f32[16]{0:T(128)} %param.17) | copy-start | bytes 196
  12.2 11.6 %collective-permute-start.1 = (f32[4,64,128]{2,1,0:T(8,128)S(1)}, f32[4,64,128]{2,1,0:T(8,128)S(1)}, u32[]{:S(2)}, u32[]{:S(2)}) collective-permute-start(f32[4,64,128]{2,1,0:T(8,128)S(1)} %get-tuple-element.47.refs_7_.refs_6_), channel_id=1, source_target_pairs={{1,0},{2,1},{3,2},{4,3},{5,4},{6,5},{7,6},{8,7},{9,8},{10,9},{11,1... | collective-permute-start | bytes 393224 | tf_op jit(solution)/shard_map/ppermute | solution.py:440
  16.6 12.2 %collective-permute-start = (f32[4,64,128]{2,1,0:T(8,128)S(1)}, f32[4,64,128]{2,1,0:T(8,128)S(1)}, u32[]{:S(2)}, u32[]{:S(2)}) collective-permute-start(f32[4,64,128]{2,1,0:T(8,128)S(1)} %get-tuple-element.48.refs_8_.refs_7_), channel_id=1, source_target_pairs={{0,1},{1,2},{2,3},{3,4},{4,5},{5,6},{6,7},{7,8},{8,9},{9,10},{10,1... | collective-permute-start | bytes 393224 | tf_op jit(solution)/shard_map/ppermute | solution.py:440
  30.6 20.3 %all-to-all-start.1 = ((f32[16,64,128]{2,1,0:T(8,128)}), f32[16,64,128]{2,1,0:T(8,128)S(1)}, u32[]{:S(2)}, u32[]{:S(2)}) async-start(f32[16,64,128]{2,1,0:T(8,128)} %get-tuple-element.33), calls=%async_computation.1 | async-start | bytes 1048576 | tf_op jit(solution)/shard_map/all_to_all | solution.py:444
  37.2 13.7 %collective-permute-start.2 = (f32[4,64,128]{2,1,0:T(8,128)S(1)}, f32[4,64,128]{2,1,0:T(8,128)S(1)}, u32[]{:S(2)}, u32[]{:S(2)}) collective-permute-start(f32[4,64,128]{2,1,0:T(8,128)S(1)} %get-tuple-element.39.refs_11_), channel_id=1, source_target_pairs={{0,1},{1,2},{2,3},{3,4},{4,5},{5,6},{6,7},{7,8},{8,9},{9,10},{10,1... | collective-permute-start | bytes 393224 | tf_op jit(solution)/shard_map/ppermute | solution.py:440
  37.7 13.2 %collective-permute-start.3 = (f32[4,64,128]{2,1,0:T(8,128)S(1)}, f32[4,64,128]{2,1,0:T(8,128)S(1)}, u32[]{:S(2)}, u32[]{:S(2)}) collective-permute-start(f32[4,64,128]{2,1,0:T(8,128)S(1)} %get-tuple-element.40.refs_10_), channel_id=1, source_target_pairs={{1,0},{2,1},{3,2},{4,3},{5,4},{6,5},{7,6},{8,7},{9,8},{10,9},{11,1... | collective-permute-start | bytes 393224 | tf_op jit(solution)/shard_map/ppermute | solution.py:440

commit v4 on v3

--- a/solution.py
+++ b/solution.py
@@ -10,6 +10,7 @@
 F32 = jnp.float32
 BF16 = jnp.bfloat16
 MIB = 1024 * 1024
+FIELDS_AFTER = 1
 GROUP = 32
 
 
@@ -108,7 +109,7 @@
         out_ref[:, k : k + 8, :] = (both[:size] + both[size:]).reshape(tracers, 8, columns)
 
 
-def react_and_sink(species, mixed, growth, below, wet, rates_ref, after):
+def react_and_sink(species, mixed, growth, below, wet, rates_ref, before, after):
     tracers, _, columns = species.shape
 
     def one(n, _):
@@ -120,12 +121,13 @@
         return 0
 
     for i, (first, last) in enumerate(groups(tracers)):
+        before(i)
         lax.fori_loop(first, last, one, 0)
         after(i)
 
 
 def groups(tracers):
-    cuts = [0, tracers * 3 // 8, tracers * 11 // 16, tracers * 7 // 8, tracers]
+    cuts = [tracers * n // 16 for n in (0, 4, 7, 10, 12, 14, 16)]
     return list(zip(cuts[:-1], cuts[1:]))
 
 
@@ -354,18 +356,22 @@
         right_edge_ref[n] = out_ref[n, :, lons - 1, :]
 
 
-def tracer_copies(species_hbm, species, out_hbm, in_sems, out_sems):
-    ats = [slice(k, k + GROUP) for k in range(0, species.shape[1], GROUP)]
-    copies = [pltpu.make_async_copy(species_hbm.at[:, at], species.at[:, at], in_sems.at[i]) for i, at in enumerate(ats)]
-    parts = [slice(first, last) for first, last in groups(species.shape[0])]
-    sends = [pltpu.make_async_copy(species.at[part], out_hbm.at[part], out_sems.at[i]) for i, part in enumerate(parts)]
-    return ats, copies, sends
+def group_copies(src, dst, sems):
+    parts = [slice(first, last) for first, last in groups(src.shape[0])]
+    return [pltpu.make_async_copy(src.at[part], dst.at[part], sems.at[i]) for i, part in enumerate(parts)]
+
+
+def level_copies(src, dst, sems):
+    ats = [slice(k, k + GROUP) for k in range(0, src.shape[1], GROUP)]
+    return ats, [pltpu.make_async_copy(src.at[:, at], dst.at[:, at], sems.at[i]) for i, at in enumerate(ats)]
 
 
 def tracer_kernel(species_hbm, light_hbm, depth_ref, coupling_ref, rates_ref, fields_ref, wet_ref, fcor_ref,
-                  out_hbm, growth_ref, kron_ref, next_fields_ref, species, mixed, light_ref, below, wet, in_sems, out_sems):
+                  out_hbm, mixed_hbm, growth_ref, next_fields_ref, species, mixed, kron_ref, light_ref, below, wet, in_sems, out_sems, mixed_sems):
     tracers, levels, columns = species.shape
-    ats, copies, sends = tracer_copies(species_hbm, species, out_hbm, in_sems, out_sems)
+    ats, copies = level_copies(species_hbm, species, in_sems)
+    sends = group_copies(species, out_hbm, out_sems)
+    _, mixed_sends = level_copies(mixed, mixed_hbm, mixed_sems)
     fetch_light = pltpu.make_async_copy(light_hbm, light_ref, in_sems.at[len(ats)])
     fetch_light.start()
     for copy in copies:
@@ -383,19 +389,24 @@
     trans, heat = light(species[0])
     light_ref[0] = 0.2 * trans * light_ref[0]
     growth_ref[...] = wet[...] * (light_ref[1] * jnp.exp(0.03 * (wet[...] * heat)))
-    react_and_sink(species, mixed, light_ref.at[0], below, wet, rates_ref, lambda i: sends[i].start())
-    for send in sends:
+    react_and_sink(species, mixed, light_ref.at[0], below, wet, rates_ref, lambda i: None, lambda i: sends[i].start())
+    for send, at in zip(mixed_sends, ats):
+        mix(kron_ref, species, mixed, at)
+        send.start()
+    for send in sends + mixed_sends:
         send.wait()
 
 
-def final_kernel(cpair, species_hbm, growth_ref, depth_ref, kron_ref, rates_ref, recv_ref, order_ref, wet_ref, left_ref, right_ref,
+def final_kernel(cpair, species_hbm, mixed_hbm, growth_ref, depth_ref, rates_ref, recv_ref, order_ref, wet_ref, left_ref, right_ref,
                  first_lon_ref, last_lon_ref, fields, out_hbm, *rest):
-    field_hbms, (species, mixed, back, tile, growth, below, in_sems, out_sems, sems) = rest[:4], rest[4:]
+    field_hbms, (species, mixed, back, tile, growth, below, in_sems, mixed_sems, out_sems, sems) = rest[:4], rest[4:]
     tracers, levels, columns = species.shape
     rows = levels * cpair // 128
-    ats, copies, sends = tracer_copies(species_hbm, species, out_hbm, in_sems, out_sems)
-    for copy in copies:
-        copy.start()
+    copies = list(zip(group_copies(species_hbm, species, in_sems), group_copies(mixed_hbm, mixed, mixed_sems)))
+    sends = group_copies(species, out_hbm, out_sems)
+    for pair in copies:
+        for copy in pair:
+            copy.start()
     tile[...] = fields[...]
     add_edges(wet_ref, left_ref, right_ref, first_lon_ref, last_lon_ref, tile)
     field_sends = [pltpu.make_async_copy(tile.at[n], field_hbms[n], sems.at[n]) for n in range(4)]
@@ -404,12 +415,18 @@
     back_columns(order_ref[...], back, cpair)
     for r, part in enumerate(place_heat(cpair, recv_ref, rows, back, wet_ref, levels)):
         tile[2, :, r, :] = tile[2, :, r, :] + part
-    for copy, at in zip(copies, ats):
-        copy.wait()
-        mix(kron_ref, species, mixed, at)
-    for copy in field_sends:
-        copy.start()
-    react_and_sink(species, mixed, growth, below, None, rates_ref, lambda i: sends[i].start())
+
+    def before(i):
+        for copy in copies[i]:
+            copy.wait()
+
+    def after(i):
+        sends[i].start()
+        if i == FIELDS_AFTER:
+            for copy in field_sends:
+                copy.start()
+
+    react_and_sink(species, mixed, growth, below, None, rates_ref, before, after)
     for copy in sends + field_sends:
         copy.wait()
 
@@ -531,24 +548,26 @@
     )(in_hbm(fields1), recv_a, order, wet_layers, left, right, *edges)
     left, right = halo(*edges)
     steps = levels // GROUP
-    species1, growth, kron, fields2 = pl.pallas_call(
+    species1, mixed, growth, fields2 = pl.pallas_call(
         tracer_kernel,
         out_shape=[
             patch,
+            patch,
             column,
-            jax.ShapeDtypeStruct((16 * tracers, 16 * tracers), BF16),
             jax.ShapeDtypeStruct((4, levels, lons, lats), F32),
         ],
         in_specs=[ANY] * 2 + whole(6),
-        out_specs=[ANY] + whole(3),
+        out_specs=[ANY] * 2 + whole(2),
         scratch_shapes=[
             patch_scratch,
             patch_scratch,
+            pltpu.VMEM((16 * tracers, 16 * tracers), BF16),
             pltpu.VMEM((2, levels, ctile), F32),
             column_scratch,
             column_scratch,
             sem((steps + 1,)),
             sem((len(groups(tracers)),)),
+            sem((steps,)),
         ],
         compiler_params=params(16),
         cost_estimate=cost(mix_flops, 8 * MIB),
@@ -558,7 +577,7 @@
     species2, u2, v2, t2, s2 = pl.pallas_call(
         lambda *refs: final_kernel(cpair, *refs),
         out_shape=[patch] + [pltpu.HBM((levels, lons, lats), F32)] * 4,
-        in_specs=[ANY] + whole(12),
+        in_specs=[ANY] * 2 + whole(11),
         out_specs=[ANY] * 5,
         scratch_shapes=[
             patch_scratch,
@@ -567,13 +586,14 @@
             fields_scratch,
             column_scratch,
             column_scratch,
-            sem((steps,)),
+            sem((len(groups(tracers)),)),
+            sem((len(groups(tracers)),)),
             sem((len(groups(tracers)),)),
             sem((4,)),
         ],
         compiler_params=params(20),
         name="final",
-    )(in_hbm(species1), growth, depth, kron, rates, recv_b, order, wet_layers, left, right, *edges, fields2)
+    )(in_hbm(species1), in_hbm(mixed), growth, depth, rates, recv_b, order, wet_layers, left, right, *edges, fields2)
     return u2, v2, t2, s2, species2
 
 

time: 58.2 us -> 56.7 us (0.974)
  waiting for transfers between devices: 8.74 us -> 6.85 us
    ppermute x2, waiting for transfers between devices: 7.54 us -> 5.65 us  [halo(): lax.ppermute(right_edge, AXES, ahead)]
    pallas_call x1, Pallas kernels: 6.41 us -> 8.3 us  [body(): pl.pallas_call(tracer_kernel, out_shape=[patch, patch, column, jax.ShapeD...]
    pallas_call x1, Pallas kernels: 6.8 us -> 5.18 us  [body(): pl.pallas_call(lambda *refs: final_kernel(cpair, *refs), out_shape=[patch...]
  transfers between devices with their start and end apart: 6 -> 6, of which waited for: 3 -> 3; matrix products, arithmetic and copies ran while one was open for 0% -> 0% of each run, Pallas kernels for 25% -> 29%
where the time goes in v4:
time: 56.7 us; the launch traced here: 56.3 us
  Pallas kernels  27.1 us (48%)
  starting transfers between devices  20.9 us (37%)
  waiting for transfers between devices  6.85 us (12%)
  between operations  1 us (2%)
    all_to_all x2, starting transfers between devices, exchange(): return lax.all_to_all(pay, AXES, split_axis=0, concat_axis=0, tiled=True)  11.8 us
    ppermute x2, starting transfers between devices, halo(): lax.ppermute(left_edge, AXES, [(b, a) for a, b in ahead])  8.65 us
    pallas_call x1, Pallas kernels, body(): pl.pallas_call(tracer_kernel, out_shape=[patch, patch, column, jax.ShapeD...  8.3 us
    ppermute x2, waiting for transfers between devices, halo(): lax.ppermute(right_edge, AXES, ahead)  5.65 us
    pallas_call x1, Pallas kernels, body(): pl.pallas_call(lambda *refs: final_kernel(cpair, *refs), out_shape=[patch...  5.18 us
    pallas_call x1, Pallas kernels, body(): pl.pallas_call(lambda *refs: start_kernel(cpair, *refs), out_shape=[pltpu...  3.73 us
    pallas_call x1, Pallas kernels, body(): pl.pallas_call(react_kernel, out_shape=jax.ShapeDtypeStruct((2, levels, c...  3.02 us
    pallas_call x1, Pallas kernels, body(): pl.pallas_call(lambda *refs: first_tile_kernel(cpair, *refs), out_shape=[...  2.91 us
  transfers between devices with their start and end apart: 6, of which 3 were waited for; matrix products, arithmetic and copies ran while one was open for 0% of the time, Pallas kernels for 29%

profile of v4, /device:TPU:0, one launch (start us, length us, event | category | flops | bytes accessed | tf_op | source)
XLA Modules:
  0.0 56.3 jit_solution(17265061106759582176)
XLA Ops:
  0.6 0.0 copy-start
  0.6 0.0 copy-start.1
  0.7 0.0 copy-start.3
  0.7 0.0 copy-start.2
  0.7 0.0 copy-start.6
  0.7 3.7 %start.1 = (f32[16,72,128]{2,1,0:T(8,128)}, f32[64,1024]{1,0:T(8,128)S(1)}) custom-call(s32[8,128]{1,0:T(8,128)} %refs_6_.3, s32[8,128]{1,0:T(8,128)} %refs_7_.1, f32[64,8,128]{2,1,0:T(8,128)} %refs_2_.4, f32[16,64,1024]{2,1,0:T(8,128)} %species_hbm.3), custom_call_target="tpu_custom_call" | custom-call | tf_op jit(solution)/shard_map/start/pallas_call | solution.py:483
  4.4 7.4 %all-to-all-start = ((f32[16,72,128]{2,1,0:T(8,128)}), f32[16,72,128]{2,1,0:T(8,128)S(1)}, u32[]{:S(2)}, u32[]{:S(2)}) async-start(f32[16,72,128]{2,1,0:T(8,128)} %get-tuple-element.26), calls=%async_computation | async-start | bytes 1179648 | tf_op jit(solution)/shard_map/all_to_all | solution.py:461
  11.8 0.0 copy-done
  11.8 0.0 copy-start.4
  11.9 0.0 copy-start.5
  11.9 0.1 copy.22
  11.9 0.0 copy-done.1
  11.9 0.1 copy.23
  12.0 0.0 copy-done.3
  12.0 0.0 copy-done.2
  12.0 0.0 copy-start.7
  12.0 0.1 copy_bitcast_fusion
  12.2 4.4 %collective-permute-start.1 = (f32[4,64,128]{2,1,0:T(8,128)S(1)}, f32[4,64,128]{2,1,0:T(8,128)S(1)}, u32[]{:S(2)}, u32[]{:S(2)}) collective-permute-start(f32[4,64,128]{2,1,0:T(8,128)S(1)} %get-tuple-element.47.refs_7_.refs_6_), channel_id=1, source_target_pairs={{1,0},{2,1},{3,2},{4,3},{5,4},{6,5},{7,6},{8,7},{9,8},{10,9},{11,1... | collective-permute-start | bytes 393224 | tf_op jit(solution)/shard_map/ppermute | solution.py:457
  16.6 0.0 collective-permute-start
  16.6 0.0 copy-done.6
  16.6 3.0 %react.1.refs_2_ = f32[2,64,1024]{2,1,0:T(8,128)S(1)} custom-call(f32[16,64,1024]{2,1,0:T(8,128)} %species_hbm.3, f32[64,1024]{1,0:T(8,128)S(1)} %get-tuple-element.27.scale_ref, f32[16,16]{1,0:T(8,128)S(1)} %copy-done.6), custom_call_target="tpu_custom_call" | custom-call | flops 2097152 | bytes 4194304 | tf_op jit(solution)/shard_map/react/pallas_call | solution.py:506
  19.6 0.1 sine_multiply_fusion.refs_5_.fcor_ref
  19.7 0.0 copy-done.4
  19.7 0.0 copy-done.5
  19.7 2.9 %tile_one.1 = (f32[4,64,8,128]{3,2,1,0:T(8,128)}, f32[64,1024]{1,0:T(8,128)S(1)}, bf16[256,1024]{1,0:T(8,128)(2,1)S(1)}) custom-call(f32[64,8,128]{2,1,0:T(8,128)S(1)} %copy-done.1, f32[64,8,128]{2,1,0:T(8,128)S(1)} %copy-done.2, f32[64,8,128]{2,1,0:T(8,128)S(1)} %copy-done, f32[64,8,128]{2,1,0:T(8,128)S(1)} %copy-done.3, s32[8,128]{1,0:T(8,128)S(1)} %copy-done.4, ...), custom_call_target="tpu_custom_call" | custom-call | flops 268435456 | bytes 2097152 | tf_op jit(solution)/shard_map/tile_one/pallas_call | solution.py:516
  22.6 1.2 %collective-permute-done.1.refs_6_.refs_5_ = f32[4,64,128]{2,1,0:T(8,128)S(1)} collective-permute-done((f32[4,64,128]{2,1,0:T(8,128)S(1)}, f32[4,64,128]{2,1,0:T(8,128)S(1)}, u32[]{:S(2)}, u32[]{:S(2)}) %collective-permute-start.1) | collective-permute-done | bytes 131104 | tf_op jit(solution)/shard_map/ppermute | solution.py:457
  23.8 5.0 %collective-permute-done.refs_5_.refs_4_ = f32[4,64,128]{2,1,0:T(8,128)S(1)} collective-permute-done((f32[4,64,128]{2,1,0:T(8,128)S(1)}, f32[4,64,128]{2,1,0:T(8,128)S(1)}, u32[]{:S(2)}, u32[]{:S(2)}) %collective-permute-start) | collective-permute-done | bytes 131104 | tf_op jit(solution)/shard_map/ppermute | solution.py:457
  28.8 0.0 all-to-all-done.refs_0_.refs_1_
  28.8 0.0 copy-done.7
  28.8 0.1 broadcast_in_dim.2.refs_1_.rates_ref.refs_4_
  28.9 1.7 %chloro.1 = (f32[16,64,128]{2,1,0:T(8,128)}, f32[2,64,1024]{2,1,0:T(8,128)}, f32[8,1024]{1,0:T(8,128)S(1)}) custom-call(f32[16,72,128]{2,1,0:T(8,128)S(1)} %all-to-all-done.refs_0_.refs_1_, f32[16,8,128]{2,1,0:T(8,128)S(1)} %broadcast_in_dim.2.refs_1_.rates_ref.refs_4_, f32[2,64,1024]{2,1,0:T(8,128)S(1)} %react.1.refs_2_, ...), custom_call_target="tpu_custom_call" | custom-call | tf_op jit(solution)/shard_map/chloro/pallas_call | solution.py:527
  30.6 4.4 %all-to-all-start.1 = ((f32[16,64,128]{2,1,0:T(8,128)}), f32[16,64,128]{2,1,0:T(8,128)S(1)}, u32[]{:S(2)}, u32[]{:S(2)}) async-start(f32[16,64,128]{2,1,0:T(8,128)} %get-tuple-element.33), calls=%async_computation.1 | async-start | bytes 1048576 | tf_op jit(solution)/shard_map/all_to_all | solution.py:461
  35.0 2.2 %heat.1 = (f32[4,64,8,128]{3,2,1,0:T(8,128)S(1)}, f32[4,64,128]{2,1,0:T(8,128)S(1)}, f32[4,64,128]{2,1,0:T(8,128)S(1)}) custom-call(f32[4,64,8,128]{3,2,1,0:T(8,128)} %get-tuple-element.32.refs_0_, f32[16,72,128]{2,1,0:T(8,128)S(1)} %all-to-all-done.refs_0_.refs_1_, s32[8,128]{1,0:T(8,128)S(1)} %copy-done.5, s32[8,128]{1,0:T(8,128)S(1)} %copy-done.4, ...), custom_call_target="tpu_custom_call" | custom-call | flops 268435456 | bytes 4194304 | tf_op jit(solution)/shard_map/heat/pallas_call | solution.py:539
  37.3 0.5 collective-permute-start.2
  37.7 4.2 %collective-permute-start.3 = (f32[4,64,128]{2,1,0:T(8,128)S(1)}, f32[4,64,128]{2,1,0:T(8,128)S(1)}, u32[]{:S(2)}, u32[]{:S(2)}) collective-permute-start(f32[4,64,128]{2,1,0:T(8,128)S(1)} %get-tuple-element.40.refs_10_), channel_id=1, source_target_pairs={{1,0},{2,1},{3,2},{4,3},{5,4},{6,5},{7,6},{8,7},{9,8},{10,9},{11,1... | collective-permute-start | bytes 393224 | tf_op jit(solution)/shard_map/ppermute | solution.py:457
  41.9 8.3 %tracer.1 = (f32[16,64,1024]{2,1,0:T(8,128)}, f32[16,64,1024]{2,1,0:T(8,128)}, f32[64,1024]{1,0:T(8,128)S(1)}, f32[4,64,8,128]{3,2,1,0:T(8,128)S(1)}) custom-call(f32[16,64,1024]{2,1,0:T(8,128)} %species_hbm.3, f32[2,64,1024]{2,1,0:T(8,128)} %get-tuple-element.30.light_hbm, f32[8,1024]{1,0:T(8,128)S(1)} %get-tuple-element.31.depth_ref.refs_3_, ...), custom_call_target="tpu_custom_call" | custom-call | flops 1610612736 | bytes 8388608 | tf_op jit(solution)/shard_map/tracer/pallas_call | solution.py:551
  50.2 0.7 %collective-permute-done.2.refs_8_ = f32[4,64,128]{2,1,0:T(8,128)S(1)} collective-permute-done((f32[4,64,128]{2,1,0:T(8,128)S(1)}, f32[4,64,128]{2,1,0:T(8,128)S(1)}, u32[]{:S(2)}, u32[]{:S(2)}) %collective-permute-start.2) | collective-permute-done | bytes 131104 | tf_op jit(solution)/shard_map/ppermute | solution.py:457
  50.9 0.0 collective-permute-done.3.refs_9_
  50.9 0.0 all-to-all-done.1.refs_5_
  50.9 5.2 %final.1 = (f32[16,64,1024]{2,1,0:T(8,128)}, f32[64,8,128]{2,1,0:T(8,128)}, f32[64,8,128]{2,1,0:T(8,128)}, f32[64,8,128]{2,1,0:T(8,128)}, f32[64,8,128]{2,1,0:T(8,128)}) custom-call(f32[16,64,1024]{2,1,0:T(8,128)} %get-tuple-element.36.refs_0_, f32[16,64,1024]{2,1,0:T(8,128)} %get-tuple-element.37.refs_1_, f32[64,1024]{1,0:T(8,128)S(1)} %get-tuple-element.38.refs_2_, ...), custom_call_target="tpu_custom_call" | custom-call | tf_op jit(solution)/shard_map/final/pallas_call | solution.py:577
  (1 shorter events, 0.0 us)
Async XLA Ops:
  0.6 11.2 %copy-start = (f32[64,8,128]{2,1,0:T(8,128)S(1)}, f32[64,8,128]{2,1,0:T(8,128)}, u32[]{:S(2)}) copy-start(f32[64,8,128]{2,1,0:T(8,128)} %refs_2_.4) | copy-start | bytes 786436
  0.6 11.3 %copy-start.1 = (f32[64,8,128]{2,1,0:T(8,128)S(1)}, f32[64,8,128]{2,1,0:T(8,128)}, u32[]{:S(2)}) copy-start(f32[64,8,128]{2,1,0:T(8,128)} %refs_0_.3) | copy-start | bytes 786436
  0.7 11.3 %copy-start.3 = (f32[64,8,128]{2,1,0:T(8,128)S(1)}, f32[64,8,128]{2,1,0:T(8,128)}, u32[]{:S(2)}) copy-start(f32[64,8,128]{2,1,0:T(8,128)} %refs_3_.4) | copy-start | bytes 786436
  0.7 11.3 %copy-start.2 = (f32[64,8,128]{2,1,0:T(8,128)S(1)}, f32[64,8,128]{2,1,0:T(8,128)}, u32[]{:S(2)}) copy-start(f32[64,8,128]{2,1,0:T(8,128)} %refs_1_.3) | copy-start | bytes 786436
  0.7 15.9 %copy-start.6 = (f32[16,16]{1,0:T(8,128)S(1)}, f32[16,16]{1,0:T(8,128)}, u32[]{:S(2)}) copy-start(f32[16,16]{1,0:T(8,128)} %coupling_ref.3) | copy-start | bytes 3076
  4.4 24.4 %all-to-all-start = ((f32[16,72,128]{2,1,0:T(8,128)}), f32[16,72,128]{2,1,0:T(8,128)S(1)}, u32[]{:S(2)}, u32[]{:S(2)}) async-start(f32[16,72,128]{2,1,0:T(8,128)} %get-tuple-element.26), calls=%async_computation | async-start | bytes 1179648 | tf_op jit(solution)/shard_map/all_to_all | solution.py:461
  11.8 7.8 %copy-start.4 = (s32[8,128]{1,0:T(8,128)S(1)}, s32[8,128]{1,0:T(8,128)}, u32[]{:S(2)}) copy-start(s32[8,128]{1,0:T(8,128)} %refs_7_.1) | copy-start | bytes 12292
  11.9 7.8 %copy-start.5 = (s32[8,128]{1,0:T(8,128)S(1)}, s32[8,128]{1,0:T(8,128)}, u32[]{:S(2)}) copy-start(s32[8,128]{1,0:T(8,128)} %refs_6_.3) | copy-start | bytes 12292
  12.0 16.8 %copy-start.7 = (f32[16]{0:T(128)S(1)}, f32[16]{0:T(128)}, u32[]{:S(2)}) copy-start(f32[16]{0:T(128)} %param.17) | copy-start | bytes 196
  12.2 11.6 %collective-permute-start.1 = (f32[4,64,128]{2,1,0:T(8,128)S(1)}, f32[4,64,128]{2,1,0:T(8,128)S(1)}, u32[]{:S(2)}, u32[]{:S(2)}) collective-permute-start(f32[4,64,128]{2,1,0:T(8,128)S(1)} %get-tuple-element.47.refs_7_.refs_6_), channel_id=1, source_target_pairs={{1,0},{2,1},{3,2},{4,3},{5,4},{6,5},{7,6},{8,7},{9,8},{10,9},{11,1... | collective-permute-start | bytes 393224 | tf_op jit(solution)/shard_map/ppermute | solution.py:457
  16.6 12.2 %collective-permute-start = (f32[4,64,128]{2,1,0:T(8,128)S(1)}, f32[4,64,128]{2,1,0:T(8,128)S(1)}, u32[]{:S(2)}, u32[]{:S(2)}) collective-permute-start(f32[4,64,128]{2,1,0:T(8,128)S(1)} %get-tuple-element.48.refs_8_.refs_7_), channel_id=1, source_target_pairs={{0,1},{1,2},{2,3},{3,4},{4,5},{5,6},{6,7},{7,8},{8,9},{9,10},{10,1... | collective-permute-start | bytes 393224 | tf_op jit(solution)/shard_map/ppermute | solution.py:457
  30.6 20.3 %all-to-all-start.1 = ((f32[16,64,128]{2,1,0:T(8,128)}), f32[16,64,128]{2,1,0:T(8,128)S(1)}, u32[]{:S(2)}, u32[]{:S(2)}) async-start(f32[16,64,128]{2,1,0:T(8,128)} %get-tuple-element.33), calls=%async_computation.1 | async-start | bytes 1048576 | tf_op jit(solution)/shard_map/all_to_all | solution.py:461
  37.3 13.7 %collective-permute-start.2 = (f32[4,64,128]{2,1,0:T(8,128)S(1)}, f32[4,64,128]{2,1,0:T(8,128)S(1)}, u32[]{:S(2)}, u32[]{:S(2)}) collective-permute-start(f32[4,64,128]{2,1,0:T(8,128)S(1)} %get-tuple-element.39.refs_11_), channel_id=1, source_target_pairs={{0,1},{1,2},{2,3},{3,4},{4,5},{5,6},{6,7},{7,8},{8,9},{9,10},{10,1... | collective-permute-start | bytes 393224 | tf_op jit(solution)/shard_map/ppermute | solution.py:457
  37.7 13.2 %collective-permute-start.3 = (f32[4,64,128]{2,1,0:T(8,128)S(1)}, f32[4,64,128]{2,1,0:T(8,128)S(1)}, u32[]{:S(2)}, u32[]{:S(2)}) collective-permute-start(f32[4,64,128]{2,1,0:T(8,128)S(1)} %get-tuple-element.40.refs_10_), channel_id=1, source_target_pairs={{1,0},{2,1},{3,2},{4,3},{5,4},{6,5},{7,6},{8,7},{9,8},{10,9},{11,1... | collective-permute-start | bytes 393224 | tf_op jit(solution)/shard_map/ppermute | solution.py:457

commit v5 on v4

--- a/solution.py
+++ b/solution.py
@@ -11,6 +11,7 @@
 BF16 = jnp.bfloat16
 MIB = 1024 * 1024
 FIELDS_AFTER = 1
+UNIT = 2
 GROUP = 32
 
 
@@ -32,6 +33,20 @@
 
 def iota(shape, dim):
     return lax.broadcasted_iota(jnp.int32, shape, dim)
+
+
+def put(ref, d, row, x):
+    if len(ref.shape) == 3:
+        ref[d, row : row + x.shape[0], :] = x
+    else:
+        for i in range(0, x.shape[0], UNIT):
+            ref[d, (row + i) // UNIT] = x[i : i + UNIT]
+
+
+def get(ref, d, row, rows):
+    if len(ref.shape) == 3:
+        return ref[d, row : row + rows, :]
+    return jnp.concatenate([ref[d, (row + i) // UNIT] for i in range(0, rows, UNIT)], axis=0)
 
 
 def pack(out_ref, row, x, cpair):
@@ -48,7 +63,7 @@
                 if shift:
                     piece = pltpu.roll(piece, shift, 1)
                 out = piece if out is None else jnp.where(lane_group == g, piece, out)
-            out_ref[e * groups + o, row : row + rows, :] = out
+            put(out_ref, e * groups + o, row, out)
 
 
 def unpack(in_ref, row, rows, cpair, first, blocks):
@@ -56,11 +71,11 @@
     lane_group = iota((rows, 128), 1) // cpair
     columns = []
     for e in range(blocks):
+        pieces = [get(in_ref, first + e * groups + o, row, rows) for o in range(groups)]
         levels = []
         for g in range(groups):
             out = None
-            for o in range(groups):
-                piece = in_ref[first + e * groups + o, row : row + rows, :]
+            for o, piece in enumerate(pieces):
                 shift = (o - g) * cpair % 128
                 if shift:
                     piece = pltpu.roll(piece, shift, 1)
@@ -164,7 +179,7 @@
     trans, heat = light(chloro[...])
     scale_ref[...] = 0.2 * trans
     pack(pay, 0, heat, cpair)
-    send_heat = pltpu.make_async_copy(pay.at[:, 0:rows], pay_hbm.at[:, 0:rows], sems.at[4])
+    send_heat = pltpu.make_async_copy(pay.at[:, 0 : rows // UNIT], pay_hbm.at[:, 0 : rows // UNIT], sems.at[4])
     send_heat.start()
     copies[3].wait()
     for r in range(lons):
@@ -175,12 +190,12 @@
         lhs[2 * levels : 2 * levels + 16, at] = jnp.broadcast_to(depth[r : r + 1], (16, lats)).astype(BF16)
     sent = mxu(lhs[...], place[...])
     pack(pay, rows, sent[0:levels] + sent[levels : 2 * levels], cpair)
-    deep = sent[2 * levels : 2 * levels + 8]
+    deep = sent[2 * levels : 2 * levels + UNIT]
     for d in range(pay.shape[0]):
         e, o = divmod(d * cpair, 128)
         part = deep[:, e * 128 : (e + 1) * 128]
-        pay[d, 2 * rows : 2 * rows + 8, :] = pltpu.roll(part, 128 - o, 1) if o else part
-    send_temp = pltpu.make_async_copy(pay.at[:, rows : 2 * rows + 8], pay_hbm.at[:, rows : 2 * rows + 8], sems.at[5])
+        pay[d, 2 * rows // UNIT] = pltpu.roll(part, 128 - o, 1) if o else part
+    send_temp = pltpu.make_async_copy(pay.at[:, rows // UNIT :], pay_hbm.at[:, rows // UNIT :], sems.at[5])
     send_temp.start()
     send_heat.wait()
     send_temp.wait()
@@ -278,15 +293,15 @@
     lons, lats = wet_ref.shape
     rows = levels * cpair // 128
     groups = 128 // cpair
-    lane_group = iota((8, 128), 1) // cpair
+    lane_group = iota((UNIT, 128), 1) // cpair
     for e in range(columns // 128):
         out = None
         for o in range(groups):
-            piece = recv_ref[e * groups + o, 2 * rows : 2 * rows + 8, :]
+            piece = recv_ref[e * groups + o, 2 * rows // UNIT]
             if o:
                 piece = pltpu.roll(piece, o * cpair, 1)
             out = piece if out is None else jnp.where(lane_group == o, piece, out)
-        depth_ref[:, e * 128 : (e + 1) * 128] = out
+        depth_ref[0:UNIT, e * 128 : (e + 1) * 128] = out
     warm = jnp.exp(0.15 * unpack(recv_ref, rows, rows, cpair, 0, columns // 128))
     light_ref[0] = warm
     level = iota((levels, columns), 0).astype(F32)
@@ -482,7 +497,7 @@
 
     pay, scale1 = pl.pallas_call(
         lambda *refs: start_kernel(cpair, *refs),
-        out_shape=[pltpu.HBM((tiles, 2 * rows + 8, 128), F32), column],
+        out_shape=[pltpu.HBM((tiles, 2 * rows // UNIT + 1, UNIT, 128), F32), column],
         in_specs=[ANY] * 4,
         out_specs=[ANY] + whole(1),
         scratch_shapes=[
@@ -490,7 +505,7 @@
             pltpu.VMEM((lons, lats), jnp.int32),
             pltpu.VMEM((levels, lons, lats), F32),
             column_scratch,
-            pltpu.VMEM((tiles, 2 * rows + 8, 128), F32),
+            pltpu.VMEM((tiles, 2 * rows // UNIT + 1, UNIT, 128), F32),
             onehot_scratch,
             pltpu.VMEM((2 * levels + 16, ctile), BF16),
             sem((6,)),

time: 56.7 us -> 55.6 us (0.981)
  waiting for transfers between devices: 6.85 us -> 6.03 us
    ppermute x2, waiting for transfers between devices: 1.19 us -> 0.41 us  [halo(): lax.ppermute(left_edge, AXES, [(b, a) for a, b in ahead])]
  transfers between devices with their start and end apart: 6 -> 6, of which waited for: 3 -> 3; matrix products, arithmetic and copies ran while one was open for 0% -> 1% of each run, Pallas kernels for 29% -> 30%
where the time goes in v5:
time: 55.6 us; the launch traced here: 55.2 us
  Pallas kernels  27.1 us (49%)
  starting transfers between devices  20.7 us (37%)
  waiting for transfers between devices  6.03 us (11%)
  between operations  1 us (2%)
    all_to_all x2, starting transfers between devices, exchange(): return lax.all_to_all(pay, AXES, split_axis=0, concat_axis=0, tiled=True)  11.5 us
    ppermute x2, starting transfers between devices, halo(): lax.ppermute(left_edge, AXES, [(b, a) for a, b in ahead])  8.65 us
    pallas_call x1, Pallas kernels, body(): pl.pallas_call(tracer_kernel, out_shape=[patch, patch, column, jax.ShapeD...  8.3 us
    ppermute x2, waiting for transfers between devices, halo(): lax.ppermute(right_edge, AXES, ahead)  5.62 us
    pallas_call x1, Pallas kernels, body(): pl.pallas_call(lambda *refs: final_kernel(cpair, *refs), out_shape=[patch...  5.18 us
    pallas_call x1, Pallas kernels, body(): pl.pallas_call(lambda *refs: start_kernel(cpair, *refs), out_shape=[pltpu...  3.7 us
    pallas_call x1, Pallas kernels, body(): pl.pallas_call(react_kernel, out_shape=jax.ShapeDtypeStruct((2, levels, c...  3.02 us
    pallas_call x1, Pallas kernels, body(): pl.pallas_call(lambda *refs: first_tile_kernel(cpair, *refs), out_shape=[...  2.91 us
  transfers between devices with their start and end apart: 6, of which 3 were waited for; matrix products, arithmetic and copies ran while one was open for 1% of the time, Pallas kernels for 30%

profile of v5, /device:TPU:0, one launch (start us, length us, event | category | flops | bytes accessed | tf_op | source)
XLA Modules:
  0.0 55.2 jit_solution(12440170030592011587)
XLA Ops:
  0.6 0.0 copy-start
  0.6 0.0 copy-start.1
  0.7 0.0 copy-start.3
  0.7 0.0 copy-start.2
  0.7 0.0 copy-start.6
  0.7 3.7 %start.1 = (f32[16,33,2,128]{3,2,1,0:T(2,128)}, f32[64,1024]{1,0:T(8,128)S(1)}) custom-call(s32[8,128]{1,0:T(8,128)} %refs_6_.3, s32[8,128]{1,0:T(8,128)} %refs_7_.1, f32[64,8,128]{2,1,0:T(8,128)} %refs_2_.4, f32[16,64,1024]{2,1,0:T(8,128)} %species_hbm.3), custom_call_target="tpu_custom_call" | custom-call | tf_op jit(solution)/shard_map/start/pallas_call | solution.py:498
  4.4 7.4 %all-to-all-start = ((f32[16,33,2,128]{3,2,1,0:T(2,128)}), f32[16,33,2,128]{3,2,1,0:T(2,128)S(1)}, u32[]{:S(2)}, u32[]{:S(2)}) async-start(f32[16,33,2,128]{3,2,1,0:T(2,128)} %get-tuple-element.26), calls=%async_computation | async-start | bytes 1081344 | tf_op jit(solution)/shard_map/all_to_all | solution.py:476
  11.8 0.0 copy-done
  11.8 0.0 copy-start.4
  11.8 0.0 copy-start.5
  11.8 0.1 copy.22
  11.9 0.0 copy-done.1
  11.9 0.1 copy.23
  11.9 0.0 copy-done.3
  11.9 0.0 copy-done.2
  12.0 0.0 copy-start.7
  12.0 0.1 copy_bitcast_fusion
  12.1 4.4 %collective-permute-start.1 = (f32[4,64,128]{2,1,0:T(8,128)S(1)}, f32[4,64,128]{2,1,0:T(8,128)S(1)}, u32[]{:S(2)}, u32[]{:S(2)}) collective-permute-start(f32[4,64,128]{2,1,0:T(8,128)S(1)} %get-tuple-element.47.refs_7_.refs_6_), channel_id=1, source_target_pairs={{1,0},{2,1},{3,2},{4,3},{5,4},{6,5},{7,6},{8,7},{9,8},{10,9},{11,1... | collective-permute-start | bytes 393224 | tf_op jit(solution)/shard_map/ppermute | solution.py:472
  16.5 0.0 collective-permute-start
  16.5 0.0 copy-done.6
  16.5 3.0 %react.1.refs_2_ = f32[2,64,1024]{2,1,0:T(8,128)S(1)} custom-call(f32[16,64,1024]{2,1,0:T(8,128)} %species_hbm.3, f32[64,1024]{1,0:T(8,128)S(1)} %get-tuple-element.27.scale_ref, f32[16,16]{1,0:T(8,128)S(1)} %copy-done.6), custom_call_target="tpu_custom_call" | custom-call | flops 2097152 | bytes 4194304 | tf_op jit(solution)/shard_map/react/pallas_call | solution.py:521
  19.6 0.1 sine_multiply_fusion.refs_5_.fcor_ref
  19.6 0.0 copy-done.4
  19.6 0.0 copy-done.5
  19.6 2.9 %tile_one.1 = (f32[4,64,8,128]{3,2,1,0:T(8,128)}, f32[64,1024]{1,0:T(8,128)S(1)}, bf16[256,1024]{1,0:T(8,128)(2,1)S(1)}) custom-call(f32[64,8,128]{2,1,0:T(8,128)S(1)} %copy-done.1, f32[64,8,128]{2,1,0:T(8,128)S(1)} %copy-done.2, f32[64,8,128]{2,1,0:T(8,128)S(1)} %copy-done, f32[64,8,128]{2,1,0:T(8,128)S(1)} %copy-done.3, s32[8,128]{1,0:T(8,128)S(1)} %copy-done.4, ...), custom_call_target="tpu_custom_call" | custom-call | flops 268435456 | bytes 2097152 | tf_op jit(solution)/shard_map/tile_one/pallas_call | solution.py:531
  22.6 0.4 collective-permute-done.1.refs_6_.refs_5_
  23.0 5.0 %collective-permute-done.refs_5_.refs_4_ = f32[4,64,128]{2,1,0:T(8,128)S(1)} collective-permute-done((f32[4,64,128]{2,1,0:T(8,128)S(1)}, f32[4,64,128]{2,1,0:T(8,128)S(1)}, u32[]{:S(2)}, u32[]{:S(2)}) %collective-permute-start) | collective-permute-done | bytes 131104 | tf_op jit(solution)/shard_map/ppermute | solution.py:472
  27.9 0.0 all-to-all-done.refs_0_.refs_1_
  27.9 0.0 copy-done.7
  27.9 0.1 broadcast_in_dim.2.refs_1_.rates_ref.refs_4_
  28.0 1.7 %chloro.1 = (f32[16,64,128]{2,1,0:T(8,128)}, f32[2,64,1024]{2,1,0:T(8,128)}, f32[8,1024]{1,0:T(8,128)S(1)}) custom-call(f32[16,33,2,128]{3,2,1,0:T(2,128)S(1)} %all-to-all-done.refs_0_.refs_1_, f32[16,8,128]{2,1,0:T(8,128)S(1)} %broadcast_in_dim.2.refs_1_.rates_ref.refs_4_, f32[2,64,1024]{2,1,0:T(8,128)S(1)} %react.1.refs_2_, ...), custom_call_target="tpu_custom_call" | custom-call | tf_op jit(solution)/shard_map/chloro/pallas_call | solution.py:542
  29.8 4.2 %all-to-all-start.1 = ((f32[16,64,128]{2,1,0:T(8,128)}), f32[16,64,128]{2,1,0:T(8,128)S(1)}, u32[]{:S(2)}, u32[]{:S(2)}) async-start(f32[16,64,128]{2,1,0:T(8,128)} %get-tuple-element.33), calls=%async_computation.1 | async-start | bytes 1048576 | tf_op jit(solution)/shard_map/all_to_all | solution.py:476
  33.9 2.2 %heat.1 = (f32[4,64,8,128]{3,2,1,0:T(8,128)S(1)}, f32[4,64,128]{2,1,0:T(8,128)S(1)}, f32[4,64,128]{2,1,0:T(8,128)S(1)}) custom-call(f32[4,64,8,128]{3,2,1,0:T(8,128)} %get-tuple-element.32.refs_0_, f32[16,33,2,128]{3,2,1,0:T(2,128)S(1)} %all-to-all-done.refs_0_.refs_1_, s32[8,128]{1,0:T(8,128)S(1)} %copy-done.5, s32[8,128]{1,0:T(8,128)S(1)} %copy-done.4, ...), custom_call_target="tpu_custom_call" | custom-call | flops 268435456 | bytes 4194304 | tf_op jit(solution)/shard_map/heat/pallas_call | solution.py:554
  36.2 0.5 collective-permute-start.2
  36.6 4.2 %collective-permute-start.3 = (f32[4,64,128]{2,1,0:T(8,128)S(1)}, f32[4,64,128]{2,1,0:T(8,128)S(1)}, u32[]{:S(2)}, u32[]{:S(2)}) collective-permute-start(f32[4,64,128]{2,1,0:T(8,128)S(1)} %get-tuple-element.40.refs_10_), channel_id=1, source_target_pairs={{1,0},{2,1},{3,2},{4,3},{5,4},{6,5},{7,6},{8,7},{9,8},{10,9},{11,1... | collective-permute-start | bytes 393224 | tf_op jit(solution)/shard_map/ppermute | solution.py:472
  40.9 8.3 %tracer.1 = (f32[16,64,1024]{2,1,0:T(8,128)}, f32[16,64,1024]{2,1,0:T(8,128)}, f32[64,1024]{1,0:T(8,128)S(1)}, f32[4,64,8,128]{3,2,1,0:T(8,128)S(1)}) custom-call(f32[16,64,1024]{2,1,0:T(8,128)} %species_hbm.3, f32[2,64,1024]{2,1,0:T(8,128)} %get-tuple-element.30.light_hbm, f32[8,1024]{1,0:T(8,128)S(1)} %get-tuple-element.31.depth_ref.refs_3_, ...), custom_call_target="tpu_custom_call" | custom-call | flops 1610612736 | bytes 8388608 | tf_op jit(solution)/shard_map/tracer/pallas_call | solution.py:566
  49.2 0.6 %collective-permute-done.2.refs_8_ = f32[4,64,128]{2,1,0:T(8,128)S(1)} collective-permute-done((f32[4,64,128]{2,1,0:T(8,128)S(1)}, f32[4,64,128]{2,1,0:T(8,128)S(1)}, u32[]{:S(2)}, u32[]{:S(2)}) %collective-permute-start.2) | collective-permute-done | bytes 131104 | tf_op jit(solution)/shard_map/ppermute | solution.py:472
  49.8 0.0 collective-permute-done.3.refs_9_
  49.8 0.0 all-to-all-done.1.refs_5_
  49.8 5.2 %final.1 = (f32[16,64,1024]{2,1,0:T(8,128)}, f32[64,8,128]{2,1,0:T(8,128)}, f32[64,8,128]{2,1,0:T(8,128)}, f32[64,8,128]{2,1,0:T(8,128)}, f32[64,8,128]{2,1,0:T(8,128)}) custom-call(f32[16,64,1024]{2,1,0:T(8,128)} %get-tuple-element.36.refs_0_, f32[16,64,1024]{2,1,0:T(8,128)} %get-tuple-element.37.refs_1_, f32[64,1024]{1,0:T(8,128)S(1)} %get-tuple-element.38.refs_2_, ...), custom_call_target="tpu_custom_call" | custom-call | tf_op jit(solution)/shard_map/final/pallas_call | solution.py:592
  (1 shorter events, 0.0 us)
Async XLA Ops:
  0.6 11.1 %copy-start = (f32[64,8,128]{2,1,0:T(8,128)S(1)}, f32[64,8,128]{2,1,0:T(8,128)}, u32[]{:S(2)}) copy-start(f32[64,8,128]{2,1,0:T(8,128)} %refs_2_.4) | copy-start | bytes 786436
  0.6 11.2 %copy-start.1 = (f32[64,8,128]{2,1,0:T(8,128)S(1)}, f32[64,8,128]{2,1,0:T(8,128)}, u32[]{:S(2)}) copy-start(f32[64,8,128]{2,1,0:T(8,128)} %refs_0_.3) | copy-start | bytes 786436
  0.7 11.3 %copy-start.3 = (f32[64,8,128]{2,1,0:T(8,128)S(1)}, f32[64,8,128]{2,1,0:T(8,128)}, u32[]{:S(2)}) copy-start(f32[64,8,128]{2,1,0:T(8,128)} %refs_3_.4) | copy-start | bytes 786436
  0.7 11.3 %copy-start.2 = (f32[64,8,128]{2,1,0:T(8,128)S(1)}, f32[64,8,128]{2,1,0:T(8,128)}, u32[]{:S(2)}) copy-start(f32[64,8,128]{2,1,0:T(8,128)} %refs_1_.3) | copy-start | bytes 786436
  0.7 15.9 %copy-start.6 = (f32[16,16]{1,0:T(8,128)S(1)}, f32[16,16]{1,0:T(8,128)}, u32[]{:S(2)}) copy-start(f32[16,16]{1,0:T(8,128)} %coupling_ref.3) | copy-start | bytes 3076
  4.4 23.6 %all-to-all-start = ((f32[16,33,2,128]{3,2,1,0:T(2,128)}), f32[16,33,2,128]{3,2,1,0:T(2,128)S(1)}, u32[]{:S(2)}, u32[]{:S(2)}) async-start(f32[16,33,2,128]{3,2,1,0:T(2,128)} %get-tuple-element.26), calls=%async_computation | async-start | bytes 1081344 | tf_op jit(solution)/shard_map/all_to_all | solution.py:476
  11.8 7.8 %copy-start.4 = (s32[8,128]{1,0:T(8,128)S(1)}, s32[8,128]{1,0:T(8,128)}, u32[]{:S(2)}) copy-start(s32[8,128]{1,0:T(8,128)} %refs_7_.1) | copy-start | bytes 12292
  11.8 7.8 %copy-start.5 = (s32[8,128]{1,0:T(8,128)S(1)}, s32[8,128]{1,0:T(8,128)}, u32[]{:S(2)}) copy-start(s32[8,128]{1,0:T(8,128)} %refs_6_.3) | copy-start | bytes 12292
  12.0 16.0 %copy-start.7 = (f32[16]{0:T(128)S(1)}, f32[16]{0:T(128)}, u32[]{:S(2)}) copy-start(f32[16]{0:T(128)} %param.17) | copy-start | bytes 196
  12.1 10.9 %collective-permute-start.1 = (f32[4,64,128]{2,1,0:T(8,128)S(1)}, f32[4,64,128]{2,1,0:T(8,128)S(1)}, u32[]{:S(2)}, u32[]{:S(2)}) collective-permute-start(f32[4,64,128]{2,1,0:T(8,128)S(1)} %get-tuple-element.47.refs_7_.refs_6_), channel_id=1, source_target_pairs={{1,0},{2,1},{3,2},{4,3},{5,4},{6,5},{7,6},{8,7},{9,8},{10,9},{11,1... | collective-permute-start | bytes 393224 | tf_op jit(solution)/shard_map/ppermute | solution.py:472
  16.5 11.4 %collective-permute-start = (f32[4,64,128]{2,1,0:T(8,128)S(1)}, f32[4,64,128]{2,1,0:T(8,128)S(1)}, u32[]{:S(2)}, u32[]{:S(2)}) collective-permute-start(f32[4,64,128]{2,1,0:T(8,128)S(1)} %get-tuple-element.48.refs_8_.refs_7_), channel_id=1, source_target_pairs={{0,1},{1,2},{2,3},{3,4},{4,5},{5,6},{6,7},{7,8},{8,9},{9,10},{10,1... | collective-permute-start | bytes 393224 | tf_op jit(solution)/shard_map/ppermute | solution.py:472
  29.8 20.1 %all-to-all-start.1 = ((f32[16,64,128]{2,1,0:T(8,128)}), f32[16,64,128]{2,1,0:T(8,128)S(1)}, u32[]{:S(2)}, u32[]{:S(2)}) async-start(f32[16,64,128]{2,1,0:T(8,128)} %get-tuple-element.33), calls=%async_computation.1 | async-start | bytes 1048576 | tf_op jit(solution)/shard_map/all_to_all | solution.py:476
  36.2 13.6 %collective-permute-start.2 = (f32[4,64,128]{2,1,0:T(8,128)S(1)}, f32[4,64,128]{2,1,0:T(8,128)S(1)}, u32[]{:S(2)}, u32[]{:S(2)}) collective-permute-start(f32[4,64,128]{2,1,0:T(8,128)S(1)} %get-tuple-element.39.refs_11_), channel_id=1, source_target_pairs={{0,1},{1,2},{2,3},{3,4},{4,5},{5,6},{6,7},{7,8},{8,9},{9,10},{10,1... | collective-permute-start | bytes 393224 | tf_op jit(solution)/shard_map/ppermute | solution.py:472
  36.6 13.2 %collective-permute-start.3 = (f32[4,64,128]{2,1,0:T(8,128)S(1)}, f32[4,64,128]{2,1,0:T(8,128)S(1)}, u32[]{:S(2)}, u32[]{:S(2)}) collective-permute-start(f32[4,64,128]{2,1,0:T(8,128)S(1)} %get-tuple-element.40.refs_10_), channel_id=1, source_target_pairs={{1,0},{2,1},{3,2},{4,3},{5,4},{6,5},{7,6},{8,7},{9,8},{10,9},{11,1... | collective-permute-start | bytes 393224 | tf_op jit(solution)/shard_map/ppermute | solution.py:472
